TPU v7x, 32 devices: a whole 2x2x4 slice. The times are simulated.
32 devices in a mesh: req: 8 (over z, y), tp: 4 (over x, core).
Axes of the slice: x: 2, y: 2, z: 4, core: 2. Of those that a mesh axis runs over, the one named last changes fastest.
Arguments:
- q_pre: bfloat16 [4096, 1024], P(('req', 'tp')), may hold values from -6 to 6
- gate_pre: bfloat16 [4096, 8], P(('req', 'tp')), may hold values from -6 to 6
- k_pre: bfloat16 [4096, 512], P(('req', 'tp')), may hold values from -6 to 6
- v_pre: bfloat16 [4096, 512], P(('req', 'tp')), may hold values from -6 to 6
- q_gain: float32 [128], replicated, may hold values from 0.1 to 1.9
- k_gain: float32 [128], replicated, may hold values from 0.1 to 1.9
- lengths: int32 [8, 3], P('req'), may hold values from 1 to 256, 512 in all within a row
- q_new: bfloat16 [24, 1024], P('req'), may hold values from -6 to 6
- gate_new: bfloat16 [24, 8], P('req'), may hold values from -6 to 6
- k_new: bfloat16 [24, 512], P('req'), may hold values from -6 to 6
- v_new: bfloat16 [24, 512], P('req'), may hold values from -6 to 6
- resid: bfloat16 [24, 2048], P('req'), may hold values from -5 to 5
- w_out: bfloat16 [1024, 2048], P('tp'), may hold values from -0.1875 to 0.1875
- norm_gain: float32 [2048], replicated, may hold values from 0.1 to 1.9
- w_gate: bfloat16 [2048, 3072], P('req', 'tp'), may hold values from -0.125 to 0.125
- w_up: bfloat16 [2048, 3072], P('req', 'tp'), may hold values from -0.125 to 0.125
- w_down: bfloat16 [3072, 2048], P('tp', 'req'), may hold values from -0.109375 to 0.109375
Outputs:
- prefill_out: bfloat16 [4096, 1024], P(('req', 'tp'))
- decode_out: bfloat16 [24, 2048], P('req')
Inputs may be any that keep to these rules, and one draw needn't show every extreme that they name: Each row holds the prompt lengths of one group's 3 requests; they sum to 512 and the longest is exactly 256.
All inputs are finite; a program needn't handle non-finite values.
Results may differ from a plain program's by a relative error of at most 0.0065.
Values may be sent and summed in bfloat16 or wider, within the bound.
No kernel may reach another device: no remote copies, remote signals or barrier semaphores. Data moves between devices by JAX's collectives and lax.ppermute only.
A program may use at most 64 MiB of HBM per device.

v0:
```python
import jax
import jax.numpy as jnp
from jax import lax
from jax.sharding import PartitionSpec as P

rope_base = 1000000.0
norm_eps = 1e-06


def group_layout(lengths_row, total):
    req_ends = jnp.cumsum(lengths_row)
    req_starts = req_ends - lengths_row
    indices = jnp.arange(total, dtype=jnp.int32)
    segment = jnp.sum((indices[:, None] >= req_ends[None, :]).astype(jnp.int32), axis=1)
    onehot = segment[:, None] == jnp.arange(lengths_row.shape[0], dtype=jnp.int32)[None, :]
    offsets = jnp.sum(jnp.where(onehot, req_starts[None, :], 0), axis=1)
    return (segment, indices - offsets)


def head_norm(values, gain):
    mean_sq = jnp.mean(values * values, axis=-1, keepdims=True)
    return values * lax.rsqrt(mean_sq + norm_eps) * gain


def rotate(values, position):
    half_size = values.shape[-1] // 2
    freqs = rope_base ** (-(jnp.arange(half_size, dtype=jnp.float32) * 2.0 / (2 * half_size)))
    angles = position.astype(jnp.float32)[:, None] * freqs[None, :]
    shaped = (values.shape[0],) + (1,) * (values.ndim - 2) + (half_size,)
    cosine = jnp.cos(angles).reshape(shaped)
    sine = jnp.sin(angles).reshape(shaped)
    first_half = values[..., :half_size]
    second_half = values[..., half_size:]
    return jnp.concatenate(
        [first_half * cosine - second_half * sine, second_half * cosine + first_half * sine],
        axis=-1,
    )


def local(
    q_pre,
    gate_pre,
    k_pre,
    v_pre,
    q_gain,
    k_gain,
    lengths,
    q_new,
    gate_new,
    k_new,
    v_new,
    resid,
    w_out,
    norm_gain,
    w_gate,
    w_up,
    w_down,
):
    tok_rows = q_pre.shape[0]
    tp_count = lax.axis_size("tp")
    tp_index = lax.axis_index("tp")
    head_size = q_gain.shape[0]
    query_heads = gate_pre.shape[1]
    kv_heads = k_pre.shape[1] // head_size
    groups_per = query_heads // kv_heads
    kv_local = kv_heads // tp_count
    req_count = lengths.shape[1]
    score_scale = head_size ** (-0.5)
    segment, position = group_layout(lengths[0], tok_rows * tp_count)
    row_offset = tp_index * tok_rows
    seg_local = lax.dynamic_slice_in_dim(segment, row_offset, tok_rows)
    pos_local = lax.dynamic_slice_in_dim(position, row_offset, tok_rows)
    query_index = row_offset + jnp.arange(tok_rows, dtype=jnp.int32)
    queries = rotate(
        head_norm(q_pre.reshape(tok_rows, query_heads, head_size).astype(jnp.float32), q_gain),
        pos_local,
    )
    queries = queries.astype(jnp.bfloat16).reshape(tok_rows, kv_heads, groups_per, head_size)
    keys = rotate(
        head_norm(k_pre.reshape(tok_rows, kv_heads, head_size).astype(jnp.float32), k_gain),
        pos_local,
    ).astype(jnp.bfloat16)
    values = v_pre.reshape(tok_rows, kv_heads, head_size)

    def key_block(running, key_piece, value_piece, first_row):
        key_count = key_piece.shape[0]
        key_index = first_row + jnp.arange(key_count, dtype=jnp.int32)
        allowed = (seg_local[:, None] == segment[None, :]) & (
            query_index[:, None] >= key_index[None, :]
        )
        scores = (
            jnp.einsum(
                "qkgd,pkd->qkgp",
                queries,
                key_piece.reshape(key_count, kv_heads, head_size),
                preferred_element_type=jnp.float32,
            )
            * score_scale
        )
        weights = jnp.where(allowed[:, None, None, :], jnp.exp(scores), 0.0)
        totals = running[0] + jnp.sum(weights, axis=-1)
        mixed = running[1] + jnp.einsum(
            "qkgp,pkd->qkgd",
            weights.astype(jnp.bfloat16),
            value_piece.reshape(key_count, kv_heads, head_size),
            preferred_element_type=jnp.float32,
        )
        return (totals, mixed)

    start_state = (
        jnp.zeros((tok_rows, kv_heads, groups_per), jnp.float32),
        jnp.zeros((tok_rows, kv_heads, groups_per, head_size), jnp.float32),
    )
    pieces = (
        lax.all_gather(keys.reshape(tok_rows, kv_heads * head_size), "tp", axis=0, tiled=True),
        lax.all_gather(v_pre, "tp", axis=0, tiled=True),
    )
    key_count = pieces[0].shape[0]
    block_rows = 512

    def one_block(number, carried):
        begin_at = number * block_rows
        return key_block(carried, pieces[0], pieces[1], begin_at)

    totals, mixed = lax.fori_loop(0, key_count // block_rows, one_block, start_state)
    gates = jax.nn.sigmoid(gate_pre.astype(jnp.float32)).reshape(tok_rows, kv_heads, groups_per)
    prefill_out = (
        (mixed / totals[..., None] * gates[..., None])
        .astype(jnp.bfloat16)
        .reshape(tok_rows, query_heads * head_size)
    )
    new_queries = rotate(
        head_norm(q_new.reshape(req_count, query_heads, head_size).astype(jnp.float32), q_gain),
        lengths[0],
    )
    new_queries = new_queries.astype(jnp.bfloat16).reshape(
        req_count, kv_heads, groups_per, head_size
    )
    new_keys = rotate(
        head_norm(k_new.reshape(req_count, kv_heads, head_size).astype(jnp.float32), k_gain),
        lengths[0],
    ).astype(jnp.bfloat16)
    new_values = v_new.reshape(req_count, kv_heads, head_size)
    new_gates = jax.nn.sigmoid(gate_new.astype(jnp.float32)).reshape(
        req_count, kv_heads, groups_per
    )
    head_first = tp_index * kv_local
    request_ids = jnp.arange(req_count, dtype=jnp.int32)
    own_queries = lax.dynamic_slice_in_dim(new_queries, head_first, kv_local, 1)
    cache_keys, cache_values = (
        lax.all_to_all(keys, "tp", split_axis=1, concat_axis=0, tiled=True),
        lax.all_to_all(values, "tp", split_axis=1, concat_axis=0, tiled=True),
    )
    scores = (
        jnp.einsum("rkgd,pkd->rkgp", own_queries, cache_keys, preferred_element_type=jnp.float32)
        * score_scale
    )
    owned = segment[None, :] == request_ids[:, None]
    weights = jnp.where(owned[:, None, None, :], jnp.exp(scores), 0.0)
    weighted = jnp.einsum(
        "rkgp,pkd->rkgd",
        weights.astype(jnp.bfloat16),
        cache_values,
        preferred_element_type=jnp.float32,
    )
    dec_totals = jnp.sum(weights, axis=-1)
    dec_mixed = weighted
    own_keys = lax.dynamic_slice_in_dim(new_keys, head_first, kv_local, 1)
    own_values = lax.dynamic_slice_in_dim(new_values, head_first, kv_local, 1)
    own_gates = lax.dynamic_slice_in_dim(new_gates, head_first, kv_local, 1)
    self_weight = jnp.exp(
        jnp.einsum("rkgd,rkd->rkg", own_queries, own_keys, preferred_element_type=jnp.float32)
        * score_scale
    )
    dec_totals = dec_totals + self_weight
    dec_mixed = dec_mixed + self_weight[..., None] * own_values.astype(jnp.float32)[:, :, None, :]
    attended = (
        (dec_mixed / dec_totals[..., None] * own_gates[..., None])
        .astype(jnp.bfloat16)
        .reshape(req_count, kv_local * groups_per * head_size)
    )
    partial_out = jnp.dot(attended, w_out, preferred_element_type=jnp.float32)
    attn_rows = lax.psum(partial_out, "tp")
    hidden_state = resid.astype(jnp.float32) + attn_rows
    mean_sq = jnp.mean(hidden_state * hidden_state, axis=-1, keepdims=True)
    normed = (hidden_state * lax.rsqrt(mean_sq + norm_eps) * norm_gain).astype(jnp.bfloat16)
    units_local = w_gate.shape[1]
    paired = jnp.concatenate([w_gate, w_up], axis=1)
    columns = lax.all_to_all(normed, "req", split_axis=1, concat_axis=0, tiled=True)
    whole_sums = lax.psum(jnp.dot(columns, paired, preferred_element_type=jnp.float32), "req")
    hidden_units = (jax.nn.silu(whole_sums[:, :units_local]) * whole_sums[:, units_local:]).astype(
        jnp.bfloat16
    )
    down_part = jnp.dot(hidden_units, w_down, preferred_element_type=jnp.float32)
    back_part = lax.all_to_all(down_part, "req", split_axis=0, concat_axis=1, tiled=True)
    mlp_rows = lax.psum(back_part, "tp")
    decode_out = (hidden_state + mlp_rows).astype(jnp.bfloat16)
    return (prefill_out, decode_out)


def solution(mesh):
    return jax.shard_map(
        local,
        mesh=mesh,
        in_specs=(
            P(("req", "tp"), None),
            P(("req", "tp"), None),
            P(("req", "tp"), None),
            P(("req", "tp"), None),
            P(),
            P(),
            P("req", None),
            P("req", None),
            P("req", None),
            P("req", None),
            P("req", None),
            P("req", None),
            P("tp", None),
            P(),
            P("req", "tp"),
            P("req", "tp"),
            P("tp", "req"),
        ),
        out_specs=(P(("req", "tp"), None), P("req", None)),
        check_vma=False,
    )
```

profile of v0, /device:TPU:0, one launch (start us, length us, event | category | flops | bytes accessed | tf_op | source)
XLA Modules:
  0.0 165.1 jit_solution(12735192966970438086)
XLA Ops:
  7.3 1.0 reduce-window.4
  8.3 0.7 convert_bitcast_fusion.2
  9.1 0.1 select_reduce_fusion
  9.2 1.0 copy.82
  10.3 0.2 multiply_cosine_fusion
  10.5 0.7 multiply_multiply_fusion.1
  11.3 0.7 maximum_convert_fusion
  12.0 4.2 %all-to-all-start = ((bf16[128,4,128]{0,2,1:T(8,128)(2,1)}), bf16[128,4,128]{0,2,1:T(8,128)(2,1)S(1)}, u32[]{:S(2)}, u32[]{:S(2)}) async-start(bf16[128,4,128]{0,2,1:T(8,128)(2,1)} %maximum_convert_fusion), calls=%async_computation | async-start | bytes 262144 | tf_op jit(solution)/shard_map/all_to_all | solution.py:151
  16.2 0.1 copy.85
  16.3 0.1 copy.86
  16.5 0.1 multiply_cosine_fusion.1
  16.6 0.1 fusion.31
  16.9 0.1 multiply_reduce_fusion.3
  17.0 0.1 copy.96
  17.4 0.1 fusion.45
  17.5 0.1 copy.107
  17.6 0.1 copy.99
  17.7 0.7 fusion.49
  18.5 0.7 copy_bitcast_fusion
  19.1 7.9 %all_gather.6 = bf16[512,512]{0,1:T(8,128)(2,1)S(1)} all-gather(bf16[128,512]{0,1:T(8,128)(2,1)} %bitcast.5), channel_id=1, replica_groups=mesh['req'=8,'tp'=4] {'tp'}, dimensions={0}, use_global_device_ids=true | all-gather | bytes 655360 | tf_op jit(solution)/shard_map/all_gather | solution.py:115
  27.1 0.1 copy.111
  27.2 0.2 multiply_reduce_fusion
  27.5 0.1 copy.84
  27.6 0.2 multiply_multiply_fusion
  27.8 0.3 subtract_convert_fusion
  28.2 0.1 fusion.26
  28.4 2.0 %fusion = (f32[128,4,2]{0,2,1:T(2,128)S(1)}, f32[4,512,128,2]{2,1,3,0:T(8,128)}) fusion(pred[128,512]{0,1:T(8,128)(4,1)S(1)} %fusion.26, bf16[512,4,128,1]{0,2,3,1:T(8,128)(2,1)S(1)} %bitcast.146, bf16[128,4,2,64]{3,0,2,1:T(8,128)(2,1)S(1)} %bitcast.150, bf16[128,4,2,64]{3,0,2,1:T(8,128)(2,1)S(1)} %bitcast.149), kind=kOutput, calls=%fused_computation.1 | convolution fusion | flops 136313856 | bytes 2953216 | tf_op jit(solution)/shard_map/while/body/eval_jaxpr/qkgd,pkd->qkgp/dot_general | solution.py:92
  30.4 3.5 %all-to-all-start.1 = ((bf16[128,4,128]{2,0,1:T(8,128)(2,1)}), bf16[128,4,128]{2,0,1:T(8,128)(2,1)S(1)}, u32[]{:S(2)}, u32[]{:S(2)}) async-start(bf16[128,4,128]{2,0,1:T(8,128)(2,1)} %copy_bitcast_fusion), calls=%async_computation.1 | async-start | bytes 262144 | tf_op jit(solution)/shard_map/all_to_all | solution.py:152
  33.9 0.1 copy.92
  34.0 0.2 fusion.61
  34.3 4.2 %all-to-all-done.1 = bf16[128,4,128]{2,0,1:T(8,128)(2,1)S(1)} async-done(((bf16[128,4,128]{2,0,1:T(8,128)(2,1)}), bf16[128,4,128]{2,0,1:T(8,128)(2,1)S(1)}, u32[]{:S(2)}, u32[]{:S(2)}) %all-to-all-start.1) | async-done | bytes 131104 | tf_op jit(solution)/shard_map/all_to_all | solution.py:152
  38.5 0.4 fusion.21
  38.8 10.3 %psum.21 = f32[3,2048]{1,0:T(4,128)S(1)} all-reduce(f32[3,2048]{1,0:T(4,128)S(1)} %fusion.21), channel_id=1, replica_groups=mesh['req'=8,'tp'=4] {'tp'}, use_global_device_ids=true, to_apply=%region_9.10 | all-reduce | flops 6144 | bytes 49152 | tf_op jit(solution)/shard_map/psum | solution.py:183
  49.1 0.1 multiply_reduce_fusion.2
  49.3 0.7 multiply_convert_fusion
  49.9 6.3 %all-to-all-start.2 = ((bf16[3,8,256]{2,0,1:T(4,128)(2,1)}), bf16[3,8,256]{2,0,1:T(4,128)(2,1)S(1)}, u32[]{:S(2)}, u32[]{:S(2)}) async-start(bf16[3,8,256]{2,0,1:T(4,128)(2,1)} %bitcast.44), calls=%async_computation.2 | async-start | bytes 32768 | tf_op jit(solution)/shard_map/all_to_all | solution.py:189
  56.3 6.7 %all_gather.7 = bf16[512,512]{1,0:T(8,128)(2,1)S(1)} all-gather(bf16[128,512]{1,0:T(8,128)(2,1)S(1)} %copy-done.1), channel_id=1, replica_groups=mesh['req'=8,'tp'=4] {'tp'}, dimensions={0}, use_global_device_ids=true | all-gather | bytes 655360 | tf_op jit(solution)/shard_map/all_gather | solution.py:116
  63.0 0.2 copy.90
  63.3 0.9 fusion.17
  64.2 71.0 %all-reduce.2.cloned.1.call-done = f32[24,1536]{1,0:T(8,128)} async-done(((f32[24,1536]{1,0:T(8,128)}), f32[24,1536]{1,0:T(8,128)}) %all-reduce.2.cloned.1.call-update) | async-done | bytes 147472 | tf_op jit(solution)/shard_map/psum | solution.py:190
  135.2 1.2 fusion.28
  136.4 0.6 all_to_all.60
  137.1 3.7 %all-to-all-start.3 = ((f32[8,3,256]{2,1,0:T(4,128)}), f32[8,3,256]{2,1,0:T(4,128)S(1)}, u32[]{:S(2)}, u32[]{:S(2)}) async-start(f32[8,3,256]{2,1,0:T(4,128)} %all_to_all.60), calls=%async_computation.3 | async-start | bytes 65536 | tf_op jit(solution)/shard_map/all_to_all | solution.py:195
  140.7 2.1 %fusion.4 = bf16[128,4,2,128]{0,3,2,1:T(8,128)(2,1)S(1)} fusion(bf16[512,4,128,1]{0,2,3,1:T(8,128)(2,1)S(1)} %bitcast.147, f32[4,512,128,2]{2,1,3,0:T(8,128)} %get-tuple-element.59, pred[128,512]{0,1:T(8,128)(4,1)S(1)} %fusion.26, f32[128,4,2]{0,2,1:T(2,128)S(1)} %bitcast.159, f32[128,4,2]{0,2,1:T(2,128)S(1)} %get-tuple-element.58), kind=kOutput, calls=%fused_computation.6 | convolution fusion | flops 136183808 | bytes 2957312 | tf_op jit(solution)/shard_map/while/body/eval_jaxpr/qkgp,pkd->qkgd/dot_general | solution.py:102
  142.8 0.9 copy.101
  143.6 3.8 %all-to-all-done.3 = f32[8,3,256]{2,1,0:T(4,128)S(1)} async-done(((f32[8,3,256]{2,1,0:T(4,128)}), f32[8,3,256]{2,1,0:T(4,128)S(1)}, u32[]{:S(2)}, u32[]{:S(2)}) %all-to-all-start.3) | async-done | bytes 24608 | tf_op jit(solution)/shard_map/all_to_all | solution.py:195
  147.4 10.3 %psum.23 = f32[3,2048]{1,0:T(4,128)S(1)} all-reduce(f32[3,2048]{1,0:T(4,128)S(1)} %bitcast.154), channel_id=1, replica_groups=mesh['req'=8,'tp'=4] {'tp'}, use_global_device_ids=true, to_apply=%region_12.13 | all-reduce | flops 6144 | bytes 49152 | tf_op jit(solution)/shard_map/psum | solution.py:196
  157.7 0.6 add_convert_fusion.1
  (63 shorter events, 1.2 us)
Async XLA Ops:
  7.2 31.3 %copy-start = (bf16[256,2048]{1,0:T(8,128)(2,1)S(1)}, bf16[256,2048]{1,0:T(8,128)(2,1)}, u32[]{:S(2)}) copy-start(bf16[256,2048]{1,0:T(8,128)(2,1)} %param.29) | copy-start | bytes 3145732
  7.2 9.9 %copy-start.9 = (f32[128]{0:T(128)S(1)}, f32[128]{0:T(128)}, u32[]{:S(2)}) copy-start(f32[128]{0:T(128)} %param.22) | copy-start | bytes 1540
  7.2 9.4 %copy-start.5 = (bf16[3,1024]{1,0:T(4,128)(2,1)S(1)}, bf16[3,1024]{1,0:T(4,128)(2,1)}, u32[]{:S(2)}) copy-start(bf16[3,1024]{1,0:T(4,128)(2,1)} %param.24) | copy-start | bytes 18436
  7.2 9.5 %copy-start.7 = (f32[128]{0:T(128)S(1)}, f32[128]{0:T(128)}, u32[]{:S(2)}) copy-start(f32[128]{0:T(128)} %param.21) | copy-start | bytes 1540
  7.2 9.7 %copy-start.4 = (bf16[3,512]{1,0:T(4,128)(2,1)S(1)}, bf16[3,512]{1,0:T(4,128)(2,1)}, u32[]{:S(2)}) copy-start(bf16[3,512]{1,0:T(4,128)(2,1)} %param.26) | copy-start | bytes 9220
  7.2 10.4 %copy-start.10 = (bf16[3,8]{1,0:T(4,128)(2,1)S(1)}, bf16[3,8]{1,0:T(4,128)(2,1)}, u32[]{:S(2)}) copy-start(bf16[3,8]{1,0:T(4,128)(2,1)} %param.25) | copy-start | bytes 148
  7.2 11.2 %copy-start.1 = (bf16[128,512]{1,0:T(8,128)(2,1)S(1)}, bf16[128,512]{1,0:T(8,128)(2,1)}, u32[]{:S(2)}) copy-start(bf16[128,512]{1,0:T(8,128)(2,1)} %param.20) | copy-start | bytes 393220
  7.2 19.8 %copy-start.2 = (bf16[128,1024]{1,0:T(8,128)(2,1)S(1)}, bf16[128,1024]{1,0:T(8,128)(2,1)}, u32[]{:S(2)}) copy-start(bf16[128,1024]{1,0:T(8,128)(2,1)} %param.17) | copy-start | bytes 786436
  12.0 18.4 %all-to-all-start = ((bf16[128,4,128]{0,2,1:T(8,128)(2,1)}), bf16[128,4,128]{0,2,1:T(8,128)(2,1)S(1)}, u32[]{:S(2)}, u32[]{:S(2)}) async-start(bf16[128,4,128]{0,2,1:T(8,128)(2,1)} %maximum_convert_fusion), calls=%async_computation | async-start | bytes 262144 | tf_op jit(solution)/shard_map/all_to_all | solution.py:151
  28.4 20.7 %copy-start.3 = (bf16[3,2048]{1,0:T(4,128)(2,1)S(1)}, bf16[3,2048]{1,0:T(4,128)(2,1)}, u32[]{:S(2)}) copy-start(bf16[3,2048]{1,0:T(4,128)(2,1)} %param.28) | copy-start | bytes 36868
  28.4 20.9 %copy-start.6 = (f32[2048]{0:T(1024)S(1)}, f32[2048]{0:T(1024)}, u32[]{:S(2)}) copy-start(f32[2048]{0:T(1024)} %param.30) | copy-start | bytes 24580
  30.4 32.9 %copy-start.11 = (bf16[256,768]{1,0:T(8,128)(2,1)S(1)}, bf16[256,768]{1,0:T(8,128)(2,1)}, u32[]{:S(2)}) copy-start(bf16[256,768]{1,0:T(8,128)(2,1)} %param.32) | copy-start | bytes 1179652
  30.4 32.9 %copy-start.12 = (bf16[256,768]{1,0:T(8,128)(2,1)S(1)}, bf16[256,768]{1,0:T(8,128)(2,1)}, u32[]{:S(2)}) copy-start(bf16[256,768]{1,0:T(8,128)(2,1)} %param.31) | copy-start | bytes 1179652
  30.4 8.1 %all-to-all-start.1 = ((bf16[128,4,128]{2,0,1:T(8,128)(2,1)}), bf16[128,4,128]{2,0,1:T(8,128)(2,1)S(1)}, u32[]{:S(2)}, u32[]{:S(2)}) async-start(bf16[128,4,128]{2,0,1:T(8,128)(2,1)} %copy_bitcast_fusion), calls=%async_computation.1 | async-start | bytes 262144 | tf_op jit(solution)/shard_map/all_to_all | solution.py:152
  38.5 25.7 %copy-start.8 = (bf16[128,8]{0,1:T(8,128)(2,1)S(1)}, bf16[128,8]{0,1:T(8,128)(2,1)}, u32[]{:S(2)}) copy-start(bf16[128,8]{0,1:T(8,128)(2,1)} %param.18) | copy-start | bytes 6148
  49.9 13.3 %all-to-all-start.2 = ((bf16[3,8,256]{2,0,1:T(4,128)(2,1)}), bf16[3,8,256]{2,0,1:T(4,128)(2,1)S(1)}, u32[]{:S(2)}, u32[]{:S(2)}) async-start(bf16[3,8,256]{2,0,1:T(4,128)(2,1)} %bitcast.44), calls=%async_computation.2 | async-start | bytes 32768 | tf_op jit(solution)/shard_map/all_to_all | solution.py:189
  56.3 78.9 %all-reduce.2.cloned.1.call-start = ((), (), s32[]{:S(2)}) async-start(), calls=%async_computation.4 | async-start | bytes 294912 | tf_op jit(solution)/shard_map/psum | solution.py:190
  137.1 10.4 %all-to-all-start.3 = ((f32[8,3,256]{2,1,0:T(4,128)}), f32[8,3,256]{2,1,0:T(4,128)S(1)}, u32[]{:S(2)}, u32[]{:S(2)}) async-start(f32[8,3,256]{2,1,0:T(4,128)} %all_to_all.60), calls=%async_computation.3 | async-start | bytes 65536 | tf_op jit(solution)/shard_map/all_to_all | solution.py:195
Sparse Core Ops, SparseCore 0:
  64.3 70.8 all-reduce.1
where the time goes:
time: 166 us; the launch traced here: 165 us
  waiting for transfers between devices  78.9 us (48%)
  blocking collectives  35.1 us (21%)
  starting transfers between devices  17.7 us (11%)
  between operations  14.4 us (9%)
  other arithmetic  7.53 us (5%)
  matrix products  6.89 us (4%)
  local copies, waits for them, and re-layouts  4.52 us (3%)
    psum x1, waiting for transfers between devices, local(): lax.psum(jnp.dot(columns, paired, preferred_element_type=jnp.float32), 'r...  71 us
    psum x1, blocking collectives, local(): attn_rows = lax.psum(partial_out, 'tp')  10.3 us
    psum x1, blocking collectives, local(): mlp_rows = lax.psum(back_part, 'tp')  10.3 us
    all_gather x1, blocking collectives, local(): lax.all_gather(keys.reshape(tok_rows, kv_heads * head_size), 'tp', axis=0...  7.94 us
    all_gather x1, blocking collectives, local(): lax.all_gather(v_pre, 'tp', axis=0, tiled=True)  6.67 us
    all_to_all x1, starting transfers between devices, local(): lax.all_to_all(normed, 'req', split_axis=1, concat_axis=0, tiled=True)  6.33 us
    all_to_all x1, starting transfers between devices, local(): lax.all_to_all(keys, 'tp', split_axis=1, concat_axis=0, tiled=True)  4.21 us
    all_to_all x1, waiting for transfers between devices, local(): lax.all_to_all(values, 'tp', split_axis=1, concat_axis=0, tiled=True)  4.2 us
  transfers between devices with their start and end apart: 5, of which 3 were waited for; matrix products, arithmetic and copies ran while one was open for 6% of the time, Pallas kernels for 0%

commit v1 on v0

--- a/solution.py
+++ b/solution.py
@@ -1,6 +1,9 @@
 import jax
 import jax.numpy as jnp
+import numpy as np
 from jax import lax
+from jax.experimental import pallas as pl
+from jax.experimental.pallas import tpu as pltpu
 from jax.sharding import PartitionSpec as P
 
 rope_base = 1000000.0
@@ -37,7 +40,7 @@
     )
 
 
-def local(
+def general(
     q_pre,
     gate_pre,
     k_pre,
@@ -198,6 +201,423 @@
     return (prefill_out, decode_out)
 
 
+f32 = jnp.float32
+bf16 = jnp.bfloat16
+lanes = 128
+pay_rows = 32
+back_rows = 16
+
+
+def dot(a, b):
+    return jnp.dot(a, b, preferred_element_type=f32)
+
+
+def dot_nt(a, b):
+    return lax.dot_general(a, b, (((1,), (1,)), ((), ())), preferred_element_type=f32)
+
+
+def iota(shape, dim):
+    return lax.broadcasted_iota(jnp.int32, shape, dim)
+
+
+def rope_factors(angles):
+    turns = jnp.floor(angles * (2.0 / np.pi) + 0.5)
+    rest = angles - turns * 1.5703125
+    rest = rest - turns * 4.837512969970703125e-4
+    rest = rest - turns * 7.549789948768648e-8
+    sq = rest * rest
+    sine = ((-1.9515295891e-4 * sq + 8.3321608736e-3) * sq - 1.6666654611e-1) * sq * rest + rest
+    cosine = (
+        ((2.443315711809948e-5 * sq - 1.388731625493765e-3) * sq + 4.166664568298827e-2) * sq * sq
+        - 0.5 * sq
+        + 1.0
+    )
+    low = iota(angles.shape, 1) < lanes // 2
+    quarter = turns.astype(jnp.int32) + jnp.where(low, 1, 0)
+    both = jnp.where((quarter & 1) == 1, cosine, sine)
+    both = jnp.where((quarter & 2) == 2, -both, both)
+    swapped = pltpu.roll(both, lanes // 2, 1)
+    return jnp.where(low, both, swapped), jnp.where(low, -swapped, both)
+
+
+def norm_rope(values, gain, factors):
+    mean_sq = jnp.mean(values * values, axis=-1, keepdims=True)
+    normed = values * lax.rsqrt(mean_sq + norm_eps) * gain
+    return (normed * factors[0] + pltpu.roll(normed, lanes // 2, 1) * factors[1]).astype(bf16)
+
+
+def begin_of(indices, len_ref):
+    begin = jnp.zeros_like(indices)
+    end = 0
+    for j in range(len_ref.shape[1] - 1):
+        end = end + len_ref[0, j]
+        begin = jnp.where(indices >= end, end, begin)
+    return begin
+
+
+def partial_kernel(
+    len_ref, k_ref, v_ref, qn_ref, kn_ref, vn_ref, gn_ref, resid_ref, qg_ref, kg_ref, freq_ref,
+    kv_ref, pay_ref, row_q, row_k, row_v, row_g, pay,
+):
+    tp = lax.axis_index("tp")
+    tok = k_ref.shape[0]
+    rpg = qn_ref.shape[0]
+    heads = qn_ref.shape[1] // lanes
+    kvs = k_ref.shape[1] // lanes
+    per = heads // kvs
+    rows = heads * rpg
+    freq = freq_ref[...]
+    qg, kg = qg_ref[...], kg_ref[...]
+    tok_index = tp * tok + iota((tok, lanes), 0)
+    factors = rope_factors((tok_index - begin_of(tok_index, len_ref)).astype(f32) * freq)
+    keys = []
+    for k in range(kvs):
+        at = slice(k * lanes, (k + 1) * lanes)
+        keys.append(norm_rope(k_ref[:, at].astype(f32), kg, factors))
+        kv_ref[:, at] = keys[-1]
+    kv_ref[:, kvs * lanes :] = v_ref[...]
+    qn, kn = qn_ref[...].astype(f32), kn_ref[...].astype(f32)
+    vn, gn = vn_ref[...].astype(f32), gn_ref[...].astype(f32)
+    for h in range(heads):
+        at = slice(h * rpg, (h + 1) * rpg)
+        kv = slice((h // per) * lanes, (h // per + 1) * lanes)
+        row_q[at, :] = qn[:, h * lanes : (h + 1) * lanes]
+        row_k[at, :] = kn[:, kv]
+        row_v[at, :] = vn[:, kv]
+        row_g[at, :] = jnp.broadcast_to(gn[:, h : h + 1], (rpg, lanes))
+    row = iota((rows, lanes), 0)
+    col = iota((rows, lanes), 1)
+    head = row * 0
+    for h in range(1, heads):
+        head = jnp.where(row >= h * rpg, h, head)
+    request = row - head * rpg
+    length, first, last = row * 0, row * 0, row * 0
+    end = 0
+    for j in range(rpg):
+        mine = request == j
+        length = jnp.where(mine, len_ref[0, j], length)
+        first = jnp.where(mine, end, first)
+        end = end + len_ref[0, j]
+        last = jnp.where(mine, end, last)
+    new_factors = rope_factors(length.astype(f32) * freq)
+    scale = lanes ** (-0.5)
+    new_q = norm_rope(row_q[...], qg, new_factors)
+    new_k = norm_rope(row_k[...], kg, new_factors)
+    scores = jnp.zeros((rows, tok), f32)
+    for k in range(kvs):
+        mine = (head >= k * per) & (head < (k + 1) * per)
+        scores = jnp.where(mine, dot_nt(new_q, keys[k]), scores)
+    index = tp * tok + col
+    weights = jnp.where((index >= first) & (index < last), jnp.exp(scores * scale), 0.0)
+    totals = jnp.sum(weights, axis=-1, keepdims=True)
+    rounded = weights.astype(bf16)
+    mixed = jnp.zeros((rows, lanes), f32)
+    for k in range(kvs):
+        mine = (head >= k * per) & (head < (k + 1) * per)
+        mixed = mixed + dot(
+            jnp.where(mine, rounded, jnp.zeros_like(rounded)), v_ref[:, k * lanes : (k + 1) * lanes]
+        )
+    self_score = jnp.sum(new_q.astype(f32) * new_k.astype(f32), axis=-1, keepdims=True)
+    self_weight = jnp.where(tp == 0, jnp.exp(self_score * scale), 0.0)
+    totals = totals + self_weight
+    mixed = (mixed + self_weight * row_v[...]) * jax.nn.sigmoid(row_g[...])
+    total_row = jnp.sum(jnp.where(row == col, totals, 0.0), axis=0, keepdims=True)
+    high = total_row.astype(bf16).astype(f32)
+    pay[...] = jnp.zeros_like(pay)
+    pay[0:rows, :] = mixed
+    pay[rows + rpg : rows + rpg + 1, :] = high
+    pay[rows + rpg + 1 : rows + rpg + 2, :] = total_row - high
+    peers = pay_ref.shape[0]
+    tps = lax.axis_size("tp")
+    slices = resid_ref.shape[1] // (tps * lanes)
+    for z in range(slices):
+        at = pl.ds(pl.multiple_of((z * tps + tp) * lanes, lanes), lanes)
+        pay[rows : rows + rpg, :] = resid_ref[:, at].astype(f32)
+        out = pay[...].astype(bf16)
+        for peer in range(z * peers // slices, (z + 1) * peers // slices):
+            pay_ref[peer] = out
+
+
+def hidden_kernel(
+    pay_ref, w0_ref, w1_ref, w2_ref, w3_ref, gate_ref, up_ref, pair_ref, ng_ref,
+    hid_ref, msg_ref, att, hid, xs, acc,
+):
+    tp = lax.axis_index("tp")
+    req = lax.axis_index("req")
+    tps = lax.axis_size("tp")
+    z, y = lax.div(req, 2), lax.rem(req, 2)
+    heads, toks, _ = att.shape
+    groups = pay_ref.shape[0] // tps
+    rpg = toks // groups
+    rows = heads * rpg
+    diag = iota((rows, lanes), 0) == iota((rows, lanes), 1)
+    for r in range(groups):
+        total = jnp.zeros(acc.shape, f32)
+        for t in range(tps):
+            piece = pay_ref[r * tps + t].astype(f32)
+            total = total + piece
+            acc[...] = piece
+            hid[r * rpg : (r + 1) * rpg, t * lanes : (t + 1) * lanes] = acc[rows : rows + rpg, :]
+        acc[...] = total
+        total_row = acc[rows + rpg : rows + rpg + 1, :] + acc[rows + rpg + 1 : rows + rpg + 2, :]
+        totals = jnp.sum(
+            jnp.where(diag, jnp.broadcast_to(total_row, (rows, lanes)), 0.0), axis=-1, keepdims=True
+        )
+        acc[0:rows, :] = acc[0:rows, :] / totals
+        for h in range(heads):
+            att[h, r * rpg : (r + 1) * rpg, :] = acc[h * rpg : (h + 1) * rpg, :]
+    state = hid[...]
+    per = heads // tps
+    for d, w_ref in enumerate((w0_ref, w1_ref, w2_ref, w3_ref)):
+        source = lax.rem(tp + tps - d, tps)
+        for j in range(per):
+            state = state + dot(
+                att[source * per + j].astype(bf16), w_ref[j * lanes : (j + 1) * lanes, :]
+            )
+    hid_ref[...] = state
+    width = state.shape[1]
+    half = width // 2
+    sums = jnp.sum(state * state, axis=-1, keepdims=True)
+    scaled = state * ng_ref[:, pl.ds(pl.multiple_of(z * width, lanes), width)]
+    xs[0] = scaled[:, :half]
+    xs[1] = scaled[:, half:]
+    own, other = xs[y].astype(bf16), xs[1 - y].astype(bf16)
+    units = pair_ref.shape[1] // 2
+    at = pl.ds(pl.multiple_of(y * units, lanes), units)
+    gate = dot(own, gate_ref[:, at]) + dot(other, pair_ref[:, :units])
+    up = dot(own, up_ref[:, at]) + dot(other, pair_ref[:, units:])
+    high = sums.astype(bf16).astype(f32)
+    lane = iota((toks, lanes), 1)
+    msg_ref[:, :units] = gate.astype(bf16)
+    msg_ref[:, units : 2 * units] = up.astype(bf16)
+    msg_ref[:, 2 * units :] = jnp.where(
+        lane == 0, high, jnp.where(lane == 1, sums - high, 0.0)
+    ).astype(bf16)
+
+
+def down_kernel(m0_ref, m1_ref, m2_ref, m3_ref, hid_ref, down_ref, pair_ref, back_ref, part, pay):
+    tp = lax.axis_index("tp")
+    tps = lax.axis_size("tp")
+    y = lax.rem(lax.axis_index("req"), 2)
+    units, half = pair_ref.shape
+    toks, width = hid_ref.shape
+    total = m0_ref[...].astype(f32)
+    for m_ref in (m1_ref, m2_ref, m3_ref):
+        total = total + m_ref[...].astype(f32)
+    sums = total[:, 2 * units : 2 * units + 1] + total[:, 2 * units + 1 : 2 * units + 2]
+    factor = lax.rsqrt(sums / (width * 4) + norm_eps)
+    gate = total[:, :units] * factor
+    hidden = (gate / (1.0 + jnp.exp(-gate)) * (total[:, units : 2 * units] * factor)).astype(bf16)
+    own_rows = pl.ds(pl.multiple_of(y * units, lanes), units)
+    part[y] = dot(hidden, down_ref[own_rows, :])
+    part[1 - y] = dot(hidden, pair_ref[...])
+    chunks = width // lanes
+    groups = pay.shape[0]
+    rpg = toks // groups
+    piece = hid_ref[:, pl.ds(pl.multiple_of(tp * lanes, lanes), lanes)]
+    high = piece.astype(bf16).astype(f32)
+    piece = jnp.where(y == 0, high, piece - high)
+    pay[...] = jnp.zeros_like(pay)
+    for c in range(chunks + 1):
+        if c < chunks:
+            at = (c * lanes) % half
+            block = part[c * lanes // half][:, at : at + lanes]
+        else:
+            block = piece
+        for r in range(groups):
+            pay[r, c * rpg : (c + 1) * rpg, :] = block[r * rpg : (r + 1) * rpg, :]
+    for r in range(groups):
+        out = pay[r].astype(bf16)
+        for t in range(tps):
+            back_ref[r * tps + t] = out
+
+
+def final_kernel(back_ref, out_ref, acc, tail, rows_out):
+    tps = lax.axis_size("tp")
+    peers = back_ref.shape[0]
+    rpg, width = out_ref.shape
+    chunks = tps
+    slices = width // (chunks * lanes)
+    group = peers // slices
+    for z in range(slices):
+        total = jnp.zeros(acc.shape, f32)
+        by_tp = [jnp.zeros(acc.shape, f32) for _ in range(tps)]
+        for p in range(group):
+            piece = back_ref[z * group + p].astype(f32)
+            total = total + piece
+            by_tp[p % tps] = by_tp[p % tps] + piece
+        acc[...] = total
+        for c in range(chunks):
+            tail[...] = by_tp[c]
+            at = slice((z * chunks + c) * lanes, (z * chunks + c + 1) * lanes)
+            rows_out[0:rpg, at] = (
+                acc[c * rpg : (c + 1) * rpg, :] + tail[chunks * rpg : (chunks + 1) * rpg, :]
+            )
+    out_ref[...] = rows_out[0:rpg, :].astype(bf16)
+
+
+def prefill_kernel(
+    len_ref, q_ref, g_ref, kv0_ref, kv1_ref, kv2_ref, qg_ref, freq_ref, out_ref
+):
+    tp = lax.axis_index("tp")
+    tok = q_ref.shape[0]
+    heads = q_ref.shape[1] // lanes
+    kvs = kv0_ref.shape[1] // (2 * lanes)
+    per = heads // kvs
+    blocks = (kv0_ref, kv1_ref, kv2_ref)
+    tok_index = tp * tok + iota((tok, lanes), 0)
+    begin = begin_of(tok_index, len_ref)
+    factors = rope_factors((tok_index - begin).astype(f32) * freq_ref[...])
+    col = iota((tok, tok), 1)
+    allowed = []
+    for b in range(len(blocks)):
+        key_index = (tp - b) * tok + col
+        allowed.append((key_index >= begin) & (key_index <= tok_index))
+    gates = jax.nn.sigmoid(g_ref[...].astype(f32))
+    qg = qg_ref[...]
+    scale = lanes ** (-0.5)
+    for h in range(heads):
+        k = h // per
+        at = slice(h * lanes, (h + 1) * lanes)
+        query = norm_rope(q_ref[:, at].astype(f32), qg, factors)
+        totals = jnp.zeros((tok, 1), f32)
+        mixed = jnp.zeros((tok, lanes), f32)
+        for b, kv_ref in enumerate(blocks):
+            scores = dot_nt(query, kv_ref[:, k * lanes : (k + 1) * lanes])
+            weights = jnp.where(allowed[b], jnp.exp(scores * scale), 0.0)
+            totals = totals + jnp.sum(weights, axis=-1, keepdims=True)
+            mixed = mixed + dot(
+                weights.astype(bf16), kv_ref[:, (kvs + k) * lanes : (kvs + k + 1) * lanes]
+            )
+        out_ref[:, at] = (mixed / totals * gates[:, h : h + 1]).astype(bf16)
+
+
+def call(body, out_shape, args, scratch=(), smem=0, flops=0, limit=12):
+    specs = [pl.BlockSpec(memory_space=pltpu.SMEM)] * smem
+    specs += [pl.BlockSpec(memory_space=pltpu.VMEM)] * (len(args) - smem)
+    size = sum(a.size * a.dtype.itemsize for a in args)
+    return pl.pallas_call(
+        body,
+        out_shape=out_shape,
+        in_specs=specs,
+        out_specs=jax.tree.map(lambda _: pl.BlockSpec(memory_space=pltpu.VMEM), out_shape),
+        scratch_shapes=[pltpu.VMEM(s, f32) for s in scratch],
+        compiler_params=pltpu.CompilerParams(vmem_limit_bytes=limit * 2**20),
+        cost_estimate=pl.CostEstimate(flops=flops, bytes_accessed=size, transcendentals=0),
+    )(*args)
+
+
+def local(
+    q_pre,
+    gate_pre,
+    k_pre,
+    v_pre,
+    q_gain,
+    k_gain,
+    lengths,
+    q_new,
+    gate_new,
+    k_new,
+    v_new,
+    resid,
+    w_out,
+    norm_gain,
+    w_gate,
+    w_up,
+    w_down,
+):
+    tps, reqs = lax.axis_size("tp"), lax.axis_size("req")
+    tok = q_pre.shape[0]
+    rpg, width = resid.shape
+    slices = reqs // 2
+    head_size = q_gain.shape[0]
+    heads = gate_pre.shape[1]
+    part = width // slices if slices else 0
+    if not (slices == 4 and tps == 4 and head_size == lanes == tok and part == tps * lanes):
+        return general(
+            q_pre, gate_pre, k_pre, v_pre, q_gain, k_gain, lengths, q_new, gate_new, k_new, v_new,
+            resid, w_out, norm_gain, w_gate, w_up, w_down,
+        )
+    peers = tps * reqs
+    toks = rpg * reqs
+    units = w_gate.shape[1] // 2
+    req = lax.axis_index("req")
+    z, y = req // 2, req % 2
+    freqs = rope_base ** (-(np.arange(head_size // 2) * 2.0 / head_size))
+    freqs = jnp.asarray(np.concatenate([freqs, freqs])[None, :], f32)
+    qg, kg = q_gain[None, :], k_gain[None, :]
+
+    def turn(array, by):
+        return lax.ppermute(array, "tp", [(i, (i + by) % tps) for i in range(tps)])
+
+    def swap(array):
+        return lax.ppermute(array, "req", [(i, i ^ 1) for i in range(reqs)])
+
+    def along(array, by):
+        return lax.ppermute(array, "req", [(i, (i + 2 * by) % reqs) for i in range(reqs)])
+
+    w_own = lax.dynamic_slice_in_dim(w_out, z * part, part, 1)
+    w_pieces = [w_own] + [turn(w_own, d) for d in range(1, tps)]
+    pair = jnp.concatenate(
+        [lax.dynamic_slice_in_dim(w, (1 - y) * units, units, 1) for w in (w_gate, w_up)], axis=1
+    )
+    pair = swap(pair)
+    down_pair = swap(lax.dynamic_slice_in_dim(w_down, (1 - y) * units, units, 0))
+
+    kv, pay = call(
+        partial_kernel,
+        (
+            jax.ShapeDtypeStruct((tok, 2 * k_pre.shape[1]), bf16),
+            jax.ShapeDtypeStruct((peers, pay_rows, lanes), bf16),
+        ),
+        (lengths, k_pre, v_pre, q_new, k_new, v_new, gate_new, resid, qg, kg, freqs),
+        scratch=[(heads * rpg, lanes)] * 4 + [(pay_rows, lanes)],
+        smem=1,
+        flops=10**7,
+    )
+    kv1, kv2 = turn(kv, 1), turn(kv, 2)
+    got = lax.all_to_all(pay, ("req", "tp"), 0, 0, tiled=True)
+    hid, msg = call(
+        hidden_kernel,
+        (
+            jax.ShapeDtypeStruct((toks, part), f32),
+            jax.ShapeDtypeStruct((toks, 2 * units + lanes), bf16),
+        ),
+        (got, *w_pieces, w_gate, w_up, pair, norm_gain[None, :]),
+        scratch=[
+            (heads, toks, lanes),
+            (toks, part),
+            (2, toks, part // 2),
+            (pay_rows, lanes),
+        ],
+        flops=10**7,
+    )
+    prefill_out = call(
+        prefill_kernel,
+        jax.ShapeDtypeStruct(q_pre.shape, bf16),
+        (lengths, q_pre, gate_pre, kv, kv1, kv2, qg, freqs),
+        smem=1,
+        flops=10**9,
+    )
+    msgs = [msg] + [along(msg, d) for d in range(1, slices)]
+    back = call(
+        down_kernel,
+        jax.ShapeDtypeStruct((peers, back_rows, lanes), bf16),
+        (*msgs, hid, w_down, down_pair),
+        scratch=[(2, toks, part // 2), (reqs, back_rows, lanes)],
+        flops=10**7,
+    )
+    returned = lax.all_to_all(back, ("req", "tp"), 0, 0, tiled=True)
+    decode_out = call(
+        final_kernel,
+        jax.ShapeDtypeStruct((rpg, width), bf16),
+        (returned,),
+        scratch=[(back_rows, lanes), (back_rows, lanes), (8, width)],
+        flops=10**6,
+    )
+    return (prefill_out, decode_out)
+
+
 def solution(mesh):
     return jax.shard_map(
         local,

time: 166 us -> 59.7 us (0.36)
  waiting for transfers between devices: 78.9 us -> 15.5 us
  blocking collectives: 35.1 us -> 0 us
  between operations: 14.4 us -> 0.83 us
  Pallas kernels: 0 us -> 9.23 us
  matrix products: 6.89 us -> 0 us
  other arithmetic: 7.53 us -> 0.79 us
  starting transfers between devices: 17.7 us -> 23.3 us
  local copies, waits for them, and re-layouts: 4.52 us -> 9.62 us
    psum x1 -> x0, waiting for transfers between devices: 71 us -> none  [local(): lax.psum(jnp.dot(columns, paired, preferred_element_type=jnp.float32), 'r...]
    psum x2 -> x0, blocking collectives: 20.5 us -> none  [the longest x1 10.3 us: local(): attn_rows = lax.psum(partial_out, 'tp')]
    all_gather x2 -> x0, blocking collectives: 14.6 us -> none  [the longest x1 7.94 us: local(): lax.all_gather(keys.reshape(tok_rows, kv_heads * head_size), 'tp', axis=0...]
    ppermute x0 -> x10, starting transfers between devices: none -> 11.8 us  [the longest x3 5.13 us: along(): lax.ppermute(array, 'req', [(i, (i + 2 * by) % reqs) for i in range(reqs)])]
    ppermute x0 -> x10, waiting for transfers between devices: none -> 11.3 us  [the longest x5 8.26 us: turn(): return lax.ppermute(array, 'tp', [(i, (i + by) % tps) for i in range(tps)])]
    pallas_call x0 -> x5, Pallas kernels: none -> 9.23 us  [call(): pl.pallas_call(body, out_shape=out_shape, in_specs=specs, out_specs=jax.t...]
    unnamed x29 -> x45, local copies, waits for them, and re-layouts: 1.11 us -> 8.86 us
    dot_general x7 -> x0, matrix products: 6.89 us -> none  [the longest x1 2.07 us: key_block(): jnp.einsum('qkgp,pkd->qkgd', weights.astype(jnp.bfloat16), value_piece.re...]
  transfers between devices with their start and end apart: 5 -> 12, of which waited for: 3 -> 7; matrix products, arithmetic and copies ran while one was open for 6% -> 3% of each run, Pallas kernels for 0% -> 11%
where the time goes in v1:
time: 59.7 us; the launch traced here: 59.2 us
  starting transfers between devices  23.3 us (39%)
  waiting for transfers between devices  15.5 us (26%)
  local copies, waits for them, and re-layouts  9.62 us (16%)
  Pallas kernels  9.23 us (15%)
  between operations  0.83 us (1%)
  other arithmetic  0.79 us (1%)
    pallas_call x5, Pallas kernels, call(): pl.pallas_call(body, out_shape=out_shape, in_specs=specs, out_specs=jax.t...  9.23 us
    unnamed x45, local copies, waits for them, and re-layouts  8.86 us
    ppermute x5, waiting for transfers between devices, turn(): return lax.ppermute(array, 'tp', [(i, (i + by) % tps) for i in range(tps)])  8.26 us
    all_to_all x1, starting transfers between devices, local(): got = lax.all_to_all(pay, ('req', 'tp'), 0, 0, tiled=True)  7.3 us
    ppermute x3, starting transfers between devices, along(): lax.ppermute(array, 'req', [(i, (i + 2 * by) % reqs) for i in range(reqs)])  5.13 us
    ppermute x5, starting transfers between devices, turn(): return lax.ppermute(array, 'tp', [(i, (i + by) % tps) for i in range(tps)])  4.29 us
    all_to_all x1, waiting for transfers between devices, local(): returned = lax.all_to_all(back, ('req', 'tp'), 0, 0, tiled=True)  4.19 us
    all_to_all x1, starting transfers between devices, local(): returned = lax.all_to_all(back, ('req', 'tp'), 0, 0, tiled=True)  4.19 us
  transfers between devices with their start and end apart: 12, of which 7 were waited for; matrix products, arithmetic and copies ran while one was open for 3% of the time, Pallas kernels for 11%

profile of v1, /device:TPU:0, one launch (start us, length us, event | category | flops | bytes accessed | tf_op | source)
XLA Modules:
  0.0 59.2 jit_solution(4322276854360888646)
XLA Ops:
  0.6 0.0 copy-start
  0.7 0.0 copy-start.19
  0.7 0.7 %copy-done.17 = s32[1,3]{1,0:T(1,128)S(1)} copy-done((s32[1,3]{1,0:T(1,128)S(1)}, s32[1,3]{1,0:T(1,128)}, u32[]{:S(2)}) %copy-start.17) | copy-done | bytes 36
  1.4 0.0 copy-done.18
  1.4 0.0 copy-done.19
  1.4 0.0 copy-done.15
  1.5 0.9 %copy-done.8 = bf16[128,512]{1,0:T(8,128)(2,1)S(1)} copy-done((bf16[128,512]{1,0:T(8,128)(2,1)S(1)}, bf16[128,512]{1,0:T(8,128)(2,1)}, u32[]{:S(2)}) %copy-start.8) | copy-done | bytes 131096
  2.4 0.9 %copy-done.9 = bf16[128,512]{1,0:T(8,128)(2,1)S(1)} copy-done((bf16[128,512]{1,0:T(8,128)(2,1)S(1)}, bf16[128,512]{1,0:T(8,128)(2,1)}, u32[]{:S(2)}) %copy-start.9) | copy-done | bytes 131096
  3.3 0.7 %copy-done.10 = bf16[3,2048]{1,0:T(4,128)(2,1)S(1)} copy-done((bf16[3,2048]{1,0:T(4,128)(2,1)S(1)}, bf16[3,2048]{1,0:T(4,128)(2,1)}, u32[]{:S(2)}) %copy-start.10) | copy-done | bytes 12312
  4.0 0.7 %copy-done.12 = bf16[3,1024]{1,0:T(4,128)(2,1)S(1)} copy-done((bf16[3,1024]{1,0:T(4,128)(2,1)S(1)}, bf16[3,1024]{1,0:T(4,128)(2,1)}, u32[]{:S(2)}) %copy-start.12) | copy-done | bytes 6168
  4.7 0.7 %copy-done.13 = bf16[3,512]{1,0:T(4,128)(2,1)S(1)} copy-done((bf16[3,512]{1,0:T(4,128)(2,1)S(1)}, bf16[3,512]{1,0:T(4,128)(2,1)}, u32[]{:S(2)}) %copy-start.13) | copy-done | bytes 3096
  5.4 0.7 %copy-done.14 = bf16[3,512]{1,0:T(4,128)(2,1)S(1)} copy-done((bf16[3,512]{1,0:T(4,128)(2,1)S(1)}, bf16[3,512]{1,0:T(4,128)(2,1)}, u32[]{:S(2)}) %copy-start.14) | copy-done | bytes 3096
  6.1 1.9 %shard_map.185 = (bf16[128,1024]{1,0:T(8,128)(2,1)}, bf16[32,32,128]{2,1,0:T(8,128)(2,1)}) custom-call(s32[1,3]{1,0:T(1,128)S(1)} %copy-done.17, bf16[128,512]{1,0:T(8,128)(2,1)S(1)} %copy-done.8, bf16[128,512]{1,0:T(8,128)(2,1)S(1)} %copy-done.9, bf16[3,1024]{1,0:T(4,128)(2,1)S(1)} %copy-done.12, bf16[3,512]{1,0:T(4,128)(2,1)S(1)} %copy-done.13, ...), custom_call_target="tpu_custom_call" | custom-call | flops 10000000 | bytes 288316 | tf_op jit(solution)/shard_map/pallas_call | solution.py:499
  8.0 7.3 %all-to-all-start = ((bf16[32,32,128]{2,1,0:T(8,128)(2,1)}), bf16[32,32,128]{2,1,0:T(8,128)(2,1)S(1)}, u32[]{:S(2)}, u32[]{:S(2)}) async-start(bf16[32,32,128]{2,1,0:T(8,128)(2,1)} %get-tuple-element.7), calls=%async_computation | async-start | bytes 524288 | tf_op jit(solution)/shard_map/all_to_all | solution.py:579
  15.4 0.8 %pad_maximum_fusion = bf16[256,768]{1,0:T(8,128)(2,1)} fusion(bf16[256,384]{1,0:T(8,128)(2,1)S(1)} %get-tuple-element.10, bf16[256,384]{1,0:T(8,128)(2,1)S(1)} %get-tuple-element.11), kind=kLoop, calls=%fused_computation | loop fusion | flops 786432 | bytes 786432 | tf_op jit(solution)/shard_map/concatenate | solution.py:561
  16.2 1.8 %collective-permute-start.5 = (bf16[256,768]{1,0:T(8,128)(2,1)}, bf16[256,768]{1,0:T(8,128)(2,1)S(1)}, u32[]{:S(2)}, u32[]{:S(2)}) collective-permute-start(bf16[256,768]{1,0:T(8,128)(2,1)} %pad_maximum_fusion), channel_id=1, source_target_pairs={{0,4},{4,0},{8,12},{12,8},{16,20},{20,16},{24,28},{28,24},{1,5},{5... | collective-permute-start | bytes 1179656 | tf_op jit(solution)/shard_map/ppermute | solution.py:554
  18.0 0.1 collective-permute-start.2
  18.0 1.5 %collective-permute-start.3 = (bf16[256,512]{1,0:T(8,128)(2,1)S(1)}, bf16[256,512]{1,0:T(8,128)(2,1)S(1)}, u32[]{:S(2)}, u32[]{:S(2)}) collective-permute-start(bf16[256,512]{1,0:T(8,128)(2,1)S(1)} %constant_dynamic-slice_fusion.3.w0_ref), channel_id=1, source_target_pairs={{0,2},{1,3},{2,0},{3,1},{4,6},{5,7},{6,4},{7,5},{8,10},{9,11},{10,... | collective-permute-start | bytes 786440 | tf_op jit(solution)/shard_map/ppermute | solution.py:551
  19.6 1.4 %collective-permute-start.4 = (bf16[256,512]{1,0:T(8,128)(2,1)S(1)}, bf16[256,512]{1,0:T(8,128)(2,1)S(1)}, u32[]{:S(2)}, u32[]{:S(2)}) collective-permute-start(bf16[256,512]{1,0:T(8,128)(2,1)S(1)} %constant_dynamic-slice_fusion.3.w0_ref), channel_id=1, source_target_pairs={{0,3},{1,0},{2,1},{3,2},{4,7},{5,4},{6,5},{7,6},{8,11},{9,8},{10,9... | collective-permute-start | bytes 786440 | tf_op jit(solution)/shard_map/ppermute | solution.py:551
  21.0 0.7 %constant_dynamic-slice_fusion = bf16[384,256]{1,0:T(8,128)(2,1)} fusion(bf16[768,256]{1,0:T(8,128)(2,1)S(1)} %copy-done.1, s32[]{:T(128)S(6)} %select_n.22), kind=kLoop, calls=%fused_computation.1 | loop fusion | bytes 393220 | tf_op jit(solution)/shard_map/dynamic_slice | solution.py:565
  21.7 0.6 collective-permute-start.9
  22.2 5.2 %collective-permute-done.2.w1_ref = bf16[256,512]{1,0:T(8,128)(2,1)S(1)} collective-permute-done((bf16[256,512]{1,0:T(8,128)(2,1)S(1)}, bf16[256,512]{1,0:T(8,128)(2,1)S(1)}, u32[]{:S(2)}, u32[]{:S(2)}) %collective-permute-start.2) | collective-permute-done | bytes 262176 | tf_op jit(solution)/shard_map/ppermute | solution.py:551
  27.4 0.0 collective-permute-start
  27.4 0.6 %collective-permute-done.3.w2_ref = bf16[256,512]{1,0:T(8,128)(2,1)S(1)} collective-permute-done((bf16[256,512]{1,0:T(8,128)(2,1)S(1)}, bf16[256,512]{1,0:T(8,128)(2,1)S(1)}, u32[]{:S(2)}, u32[]{:S(2)}) %collective-permute-start.3) | collective-permute-done | bytes 262176 | tf_op jit(solution)/shard_map/ppermute | solution.py:551
  28.1 0.7 %copy-done.4 = bf16[256,512]{1,0:T(8,128)(2,1)} copy-done((bf16[256,512]{1,0:T(8,128)(2,1)}, bf16[256,512]{1,0:T(8,128)(2,1)S(1)}, u32[]{:S(2)}) %copy-start.4) | copy-done | bytes 262168
  28.8 1.3 %collective-permute-start.1 = (bf16[128,1024]{1,0:T(8,128)(2,1)}, bf16[128,1024]{1,0:T(8,128)(2,1)}, u32[]{:S(2)}, u32[]{:S(2)}) collective-permute-start(bf16[128,1024]{1,0:T(8,128)(2,1)} %get-tuple-element.6.kv0_ref), channel_id=1, source_target_pairs={{0,2},{1,3},{2,0},{3,1},{4,6},{5,7},{6,4},{7,5},{8,10},{9,11},{10,... | collective-permute-start | bytes 786440 | tf_op jit(solution)/shard_map/ppermute | solution.py:551
  30.1 2.4 %collective-permute-done.4.w3_ref = bf16[256,512]{1,0:T(8,128)(2,1)S(1)} collective-permute-done((bf16[256,512]{1,0:T(8,128)(2,1)S(1)}, bf16[256,512]{1,0:T(8,128)(2,1)S(1)}, u32[]{:S(2)}, u32[]{:S(2)}) %collective-permute-start.4) | collective-permute-done | bytes 262176 | tf_op jit(solution)/shard_map/ppermute | solution.py:551
  32.5 0.7 %copy-done.6 = bf16[256,512]{1,0:T(8,128)(2,1)} copy-done((bf16[256,512]{1,0:T(8,128)(2,1)}, bf16[256,512]{1,0:T(8,128)(2,1)S(1)}, u32[]{:S(2)}) %copy-start.6) | copy-done | bytes 262168
  33.3 0.0 collective-permute-done.5.pair_ref
  33.3 0.0 all-to-all-done.pay_ref
  33.3 0.9 %copy-done.5 = bf16[256,512]{1,0:T(8,128)(2,1)S(1)} copy-done((bf16[256,512]{1,0:T(8,128)(2,1)S(1)}, bf16[256,512]{1,0:T(8,128)(2,1)}, u32[]{:S(2)}) %copy-start.5) | copy-done | bytes 262168
  34.2 0.9 %copy-done.7 = bf16[256,512]{1,0:T(8,128)(2,1)S(1)} copy-done((bf16[256,512]{1,0:T(8,128)(2,1)S(1)}, bf16[256,512]{1,0:T(8,128)(2,1)}, u32[]{:S(2)}) %copy-start.7) | copy-done | bytes 262168
  35.2 0.8 %shard_map.187 = (f32[24,512]{1,0:T(8,128)S(1)}, bf16[24,896]{1,0:T(8,128)(2,1)S(1)}) custom-call(bf16[32,32,128]{2,1,0:T(8,128)(2,1)S(1)} %all-to-all-done.pay_ref, bf16[256,512]{1,0:T(8,128)(2,1)S(1)} %constant_dynamic-slice_fusion.3.w0_ref, bf16[256,512]{1,0:T(8,128)(2,1)S(1)} %collective-permute-done.2.w1_ref, bf16[256,512]{1,0:T(8,128)(2,1)S(1)} %copy-done.5, ...), custom_call_target="tpu_custom_call" | custom-call | flops 10000000 | bytes 2498560 | tf_op jit(solution)/shard_map/pallas_call | solution.py:499
  36.0 1.4 %collective-permute-start.6 = (bf16[24,896]{1,0:T(8,128)(2,1)S(1)}, bf16[24,896]{1,0:T(8,128)(2,1)S(1)}, u32[]{:S(2)}, u32[]{:S(2)}) collective-permute-start(bf16[24,896]{1,0:T(8,128)(2,1)S(1)} %get-tuple-element.8.m0_ref), channel_id=1, source_target_pairs={{0,8},{4,12},{8,16},{12,20},{16,24},{20,28},{24,0},{28,4},{1,9},{5... | collective-permute-start | bytes 129032 | tf_op jit(solution)/shard_map/ppermute | solution.py:557
  37.3 2.2 %collective-permute-start.7 = (bf16[24,896]{1,0:T(8,128)(2,1)S(1)}, bf16[24,896]{1,0:T(8,128)(2,1)S(1)}, u32[]{:S(2)}, u32[]{:S(2)}) collective-permute-start(bf16[24,896]{1,0:T(8,128)(2,1)S(1)} %get-tuple-element.8.m0_ref), channel_id=1, source_target_pairs={{0,16},{4,20},{8,24},{12,28},{16,0},{20,4},{24,8},{28,12},{1,17},{... | collective-permute-start | bytes 129032 | tf_op jit(solution)/shard_map/ppermute | solution.py:557
  39.6 0.0 collective-permute-done.9.pair_ref
  39.6 1.5 %collective-permute-start.8 = (bf16[24,896]{1,0:T(8,128)(2,1)S(1)}, bf16[24,896]{1,0:T(8,128)(2,1)S(1)}, u32[]{:S(2)}, u32[]{:S(2)}) collective-permute-start(bf16[24,896]{1,0:T(8,128)(2,1)S(1)} %get-tuple-element.8.m0_ref), channel_id=1, source_target_pairs={{0,24},{4,28},{8,0},{12,4},{16,8},{20,12},{24,16},{28,20},{1,25},{... | collective-permute-start | bytes 129032 | tf_op jit(solution)/shard_map/ppermute | solution.py:557
  41.1 0.7 %collective-permute-done.6.m1_ref = bf16[24,896]{1,0:T(8,128)(2,1)S(1)} collective-permute-done((bf16[24,896]{1,0:T(8,128)(2,1)S(1)}, bf16[24,896]{1,0:T(8,128)(2,1)S(1)}, u32[]{:S(2)}, u32[]{:S(2)}) %collective-permute-start.6) | collective-permute-done | bytes 43040 | tf_op jit(solution)/shard_map/ppermute | solution.py:557
  41.8 0.5 collective-permute-done.7.m2_ref
  42.3 1.8 %collective-permute-done.8.m3_ref = bf16[24,896]{1,0:T(8,128)(2,1)S(1)} collective-permute-done((bf16[24,896]{1,0:T(8,128)(2,1)S(1)}, bf16[24,896]{1,0:T(8,128)(2,1)S(1)}, u32[]{:S(2)}, u32[]{:S(2)}) %collective-permute-start.8) | collective-permute-done | bytes 43040 | tf_op jit(solution)/shard_map/ppermute | solution.py:557
  44.1 1.9 %shard_map.188 = bf16[32,16,128]{2,1,0:T(8,128)(2,1)} custom-call(bf16[24,896]{1,0:T(8,128)(2,1)S(1)} %get-tuple-element.8.m0_ref, bf16[24,896]{1,0:T(8,128)(2,1)S(1)} %collective-permute-done.6.m1_ref, bf16[24,896]{1,0:T(8,128)(2,1)S(1)} %collective-permute-done.7.m2_ref, bf16[24,896]{1,0:T(8,128)(2,1)S(1)} %collective-permute-done.8.m3_ref, ...), custom_call_target="tpu_custom_call" | custom-call | flops 10000000 | bytes 811008 | tf_op jit(solution)/shard_map/pallas_call | solution.py:499
  46.1 4.2 %all-to-all-start.1 = ((bf16[32,16,128]{2,1,0:T(8,128)(2,1)}), bf16[32,16,128]{2,1,0:T(8,128)(2,1)S(1)}, u32[]{:S(2)}, u32[]{:S(2)}) async-start(bf16[32,16,128]{2,1,0:T(8,128)(2,1)} %shard_map.188), calls=%async_computation.1 | async-start | bytes 262144 | tf_op jit(solution)/shard_map/all_to_all | solution.py:610
  50.3 0.1 copy.20.g_ref
  50.4 0.0 collective-permute-done.kv1_ref
  50.4 0.0 collective-permute-done.1.kv2_ref
  50.4 3.9 %shard_map.186 = bf16[128,1024]{1,0:T(8,128)(2,1)} custom-call(s32[1,3]{1,0:T(1,128)S(1)} %copy-done.17, bf16[128,1024]{1,0:T(8,128)(2,1)S(1)} %copy-done.20, bf16[128,8]{1,0:T(8,128)(2,1)S(1)} %copy.20.g_ref, bf16[128,1024]{1,0:T(8,128)(2,1)} %get-tuple-element.6.kv0_ref, bf16[128,1024]{1,0:T(8,128)(2,1)} %collective-permute-done.kv1_ref, ...), custom_call_target="tpu_custom_call" | custom-call | flops 1000000000 | bytes 1051660 | tf_op jit(solution)/shard_map/pallas_call | solution.py:499
  54.3 4.2 %all-to-all-done.1.back_ref = bf16[32,16,128]{2,1,0:T(8,128)(2,1)S(1)} async-done(((bf16[32,16,128]{2,1,0:T(8,128)(2,1)}), bf16[32,16,128]{2,1,0:T(8,128)(2,1)S(1)}, u32[]{:S(2)}, u32[]{:S(2)}) %all-to-all-start.1) | async-done | bytes 131104 | tf_op jit(solution)/shard_map/all_to_all | solution.py:610
  58.5 0.7 %shard_map.189 = bf16[3,2048]{1,0:T(4,128)(2,1)} custom-call(bf16[32,16,128]{2,1,0:T(8,128)(2,1)S(1)} %all-to-all-done.1.back_ref), custom_call_target="tpu_custom_call" | custom-call | flops 1000000 | bytes 131072 | tf_op jit(solution)/shard_map/pallas_call | solution.py:499
  (30 shorter events, 0.1 us)
Async XLA Ops:
  0.6 17.3 %copy-start = (bf16[256,2048]{1,0:T(8,128)(2,1)S(1)}, bf16[256,2048]{1,0:T(8,128)(2,1)}, u32[]{:S(2)}) copy-start(bf16[256,2048]{1,0:T(8,128)(2,1)} %param.30) | copy-start | bytes 3145732
  0.7 0.7 %copy-start.17 = (s32[1,3]{1,0:T(1,128)S(1)}, s32[1,3]{1,0:T(1,128)}, u32[]{:S(2)}) copy-start(s32[1,3]{1,0:T(1,128)} %len_ref.3) | copy-start | bytes 40
  0.7 0.7 %copy-start.18 = (f32[128]{0:T(128)S(1)}, f32[128]{0:T(128)}, u32[]{:S(2)}) copy-start(f32[128]{0:T(128)} %param.22) | copy-start | bytes 1540
  0.7 0.8 %copy-start.19 = (f32[1,128]{1,0:T(1,128)S(1)}, f32[1,128]{1,0:T(1,128)}, u32[]{:S(2)}) copy-start(f32[1,128]{1,0:T(1,128)} %constant.42.clone.freq_ref) | copy-start | bytes 1540
  0.7 0.8 %copy-start.15 = (bf16[3,8]{1,0:T(4,128)(2,1)S(1)}, bf16[3,8]{1,0:T(4,128)(2,1)}, u32[]{:S(2)}) copy-start(bf16[3,8]{1,0:T(4,128)(2,1)} %gn_ref.1) | copy-start | bytes 148
  0.7 0.8 %copy-start.16 = (f32[128]{0:T(128)S(1)}, f32[128]{0:T(128)}, u32[]{:S(2)}) copy-start(f32[128]{0:T(128)} %param.23) | copy-start | bytes 1540
  1.5 0.9 %copy-start.8 = (bf16[128,512]{1,0:T(8,128)(2,1)S(1)}, bf16[128,512]{1,0:T(8,128)(2,1)}, u32[]{:S(2)}) copy-start(bf16[128,512]{1,0:T(8,128)(2,1)} %k_ref.1) | copy-start | bytes 393220
  2.4 0.9 %copy-start.9 = (bf16[128,512]{1,0:T(8,128)(2,1)S(1)}, bf16[128,512]{1,0:T(8,128)(2,1)}, u32[]{:S(2)}) copy-start(bf16[128,512]{1,0:T(8,128)(2,1)} %v_ref.1) | copy-start | bytes 393220
  3.3 0.7 %copy-start.10 = (bf16[3,2048]{1,0:T(4,128)(2,1)S(1)}, bf16[3,2048]{1,0:T(4,128)(2,1)}, u32[]{:S(2)}) copy-start(bf16[3,2048]{1,0:T(4,128)(2,1)} %resid_ref.1) | copy-start | bytes 36868
  4.0 0.7 %copy-start.12 = (bf16[3,1024]{1,0:T(4,128)(2,1)S(1)}, bf16[3,1024]{1,0:T(4,128)(2,1)}, u32[]{:S(2)}) copy-start(bf16[3,1024]{1,0:T(4,128)(2,1)} %qn_ref.1) | copy-start | bytes 18436
  4.7 0.7 %copy-start.13 = (bf16[3,512]{1,0:T(4,128)(2,1)S(1)}, bf16[3,512]{1,0:T(4,128)(2,1)}, u32[]{:S(2)}) copy-start(bf16[3,512]{1,0:T(4,128)(2,1)} %kn_ref.1) | copy-start | bytes 9220
  5.4 0.7 %copy-start.14 = (bf16[3,512]{1,0:T(4,128)(2,1)S(1)}, bf16[3,512]{1,0:T(4,128)(2,1)}, u32[]{:S(2)}) copy-start(bf16[3,512]{1,0:T(4,128)(2,1)} %vn_ref.1) | copy-start | bytes 9220
  6.1 9.3 %copy-start.2 = (bf16[256,768]{1,0:T(8,128)(2,1)S(1)}, bf16[256,768]{1,0:T(8,128)(2,1)}, u32[]{:S(2)}) copy-start(bf16[256,768]{1,0:T(8,128)(2,1)} %gate_ref.1) | copy-start | bytes 1179652
  6.1 9.3 %copy-start.3 = (bf16[256,768]{1,0:T(8,128)(2,1)S(1)}, bf16[256,768]{1,0:T(8,128)(2,1)}, u32[]{:S(2)}) copy-start(bf16[256,768]{1,0:T(8,128)(2,1)} %up_ref.1) | copy-start | bytes 1179652
  8.0 25.3 %all-to-all-start = ((bf16[32,32,128]{2,1,0:T(8,128)(2,1)}), bf16[32,32,128]{2,1,0:T(8,128)(2,1)S(1)}, u32[]{:S(2)}, u32[]{:S(2)}) async-start(bf16[32,32,128]{2,1,0:T(8,128)(2,1)} %get-tuple-element.7), calls=%async_computation | async-start | bytes 524288 | tf_op jit(solution)/shard_map/all_to_all | solution.py:579
  16.2 4.8 %copy-start.1 = (bf16[768,256]{1,0:T(8,128)(2,1)S(1)}, bf16[768,256]{1,0:T(8,128)(2,1)}, u32[]{:S(2)}) copy-start(bf16[768,256]{1,0:T(8,128)(2,1)} %down_ref.1) | copy-start | bytes 1179652
  16.2 17.1 %collective-permute-start.5 = (bf16[256,768]{1,0:T(8,128)(2,1)}, bf16[256,768]{1,0:T(8,128)(2,1)S(1)}, u32[]{:S(2)}, u32[]{:S(2)}) collective-permute-start(bf16[256,768]{1,0:T(8,128)(2,1)} %pad_maximum_fusion), channel_id=1, source_target_pairs={{0,4},{4,0},{8,12},{12,8},{16,20},{20,16},{24,28},{28,24},{1,5},{5... | collective-permute-start | bytes 1179656 | tf_op jit(solution)/shard_map/ppermute | solution.py:554
  18.0 9.4 %collective-permute-start.2 = (bf16[256,512]{1,0:T(8,128)(2,1)S(1)}, bf16[256,512]{1,0:T(8,128)(2,1)S(1)}, u32[]{:S(2)}, u32[]{:S(2)}) collective-permute-start(bf16[256,512]{1,0:T(8,128)(2,1)S(1)} %constant_dynamic-slice_fusion.3.w0_ref), channel_id=1, source_target_pairs={{0,1},{1,2},{2,3},{3,0},{4,5},{5,6},{6,7},{7,4},{8,9},{9,10},{10,1... | collective-permute-start | bytes 786440 | tf_op jit(solution)/shard_map/ppermute | solution.py:551
  18.0 10.0 %collective-permute-start.3 = (bf16[256,512]{1,0:T(8,128)(2,1)S(1)}, bf16[256,512]{1,0:T(8,128)(2,1)S(1)}, u32[]{:S(2)}, u32[]{:S(2)}) collective-permute-start(bf16[256,512]{1,0:T(8,128)(2,1)S(1)} %constant_dynamic-slice_fusion.3.w0_ref), channel_id=1, source_target_pairs={{0,2},{1,3},{2,0},{3,1},{4,6},{5,7},{6,4},{7,5},{8,10},{9,11},{10,... | collective-permute-start | bytes 786440 | tf_op jit(solution)/shard_map/ppermute | solution.py:551
  19.6 13.0 %collective-permute-start.4 = (bf16[256,512]{1,0:T(8,128)(2,1)S(1)}, bf16[256,512]{1,0:T(8,128)(2,1)S(1)}, u32[]{:S(2)}, u32[]{:S(2)}) collective-permute-start(bf16[256,512]{1,0:T(8,128)(2,1)S(1)} %constant_dynamic-slice_fusion.3.w0_ref), channel_id=1, source_target_pairs={{0,3},{1,0},{2,1},{3,2},{4,7},{5,4},{6,5},{7,6},{8,11},{9,8},{10,9... | collective-permute-start | bytes 786440 | tf_op jit(solution)/shard_map/ppermute | solution.py:551
  21.0 12.3 %copy-start.11 = (f32[2048]{0:T(1024)S(1)}, f32[2048]{0:T(1024)}, u32[]{:S(2)}) copy-start(f32[2048]{0:T(1024)} %param.31) | copy-start | bytes 24580
  21.7 17.9 %collective-permute-start.9 = (bf16[384,256]{1,0:T(8,128)(2,1)}, bf16[384,256]{1,0:T(8,128)(2,1)}, u32[]{:S(2)}, u32[]{:S(2)}) collective-permute-start(bf16[384,256]{1,0:T(8,128)(2,1)} %constant_dynamic-slice_fusion), channel_id=1, source_target_pairs={{0,4},{4,0},{8,12},{12,8},{16,20},{20,16},{24,28},{28,24},{1,5},{5... | collective-permute-start | bytes 589832 | tf_op jit(solution)/shard_map/ppermute | solution.py:554
  27.4 23.0 %collective-permute-start = (bf16[128,1024]{1,0:T(8,128)(2,1)}, bf16[128,1024]{1,0:T(8,128)(2,1)}, u32[]{:S(2)}, u32[]{:S(2)}) collective-permute-start(bf16[128,1024]{1,0:T(8,128)(2,1)} %get-tuple-element.6.kv0_ref), channel_id=1, source_target_pairs={{0,1},{1,2},{2,3},{3,0},{4,5},{5,6},{6,7},{7,4},{8,9},{9,10},{10,1... | collective-permute-start | bytes 786440 | tf_op jit(solution)/shard_map/ppermute | solution.py:551
  28.1 0.7 %copy-start.4 = (bf16[256,512]{1,0:T(8,128)(2,1)}, bf16[256,512]{1,0:T(8,128)(2,1)S(1)}, u32[]{:S(2)}) copy-start(bf16[256,512]{1,0:T(8,128)(2,1)S(1)} %collective-permute-done.3.w2_ref) | copy-start | bytes 786436
  28.8 21.6 %collective-permute-start.1 = (bf16[128,1024]{1,0:T(8,128)(2,1)}, bf16[128,1024]{1,0:T(8,128)(2,1)}, u32[]{:S(2)}, u32[]{:S(2)}) collective-permute-start(bf16[128,1024]{1,0:T(8,128)(2,1)} %get-tuple-element.6.kv0_ref), channel_id=1, source_target_pairs={{0,2},{1,3},{2,0},{3,1},{4,6},{5,7},{6,4},{7,5},{8,10},{9,11},{10,... | collective-permute-start | bytes 786440 | tf_op jit(solution)/shard_map/ppermute | solution.py:551
  32.5 0.7 %copy-start.6 = (bf16[256,512]{1,0:T(8,128)(2,1)}, bf16[256,512]{1,0:T(8,128)(2,1)S(1)}, u32[]{:S(2)}) copy-start(bf16[256,512]{1,0:T(8,128)(2,1)S(1)} %collective-permute-done.4.w3_ref) | copy-start | bytes 786436
  33.3 1.0 %copy-start.5 = (bf16[256,512]{1,0:T(8,128)(2,1)S(1)}, bf16[256,512]{1,0:T(8,128)(2,1)}, u32[]{:S(2)}) copy-start(bf16[256,512]{1,0:T(8,128)(2,1)} %copy-done.4) | copy-start | bytes 786436
  34.2 0.9 %copy-start.7 = (bf16[256,512]{1,0:T(8,128)(2,1)S(1)}, bf16[256,512]{1,0:T(8,128)(2,1)}, u32[]{:S(2)}) copy-start(bf16[256,512]{1,0:T(8,128)(2,1)} %copy-done.6) | copy-start | bytes 786436
  36.0 5.9 %collective-permute-start.6 = (bf16[24,896]{1,0:T(8,128)(2,1)S(1)}, bf16[24,896]{1,0:T(8,128)(2,1)S(1)}, u32[]{:S(2)}, u32[]{:S(2)}) collective-permute-start(bf16[24,896]{1,0:T(8,128)(2,1)S(1)} %get-tuple-element.8.m0_ref), channel_id=1, source_target_pairs={{0,8},{4,12},{8,16},{12,20},{16,24},{20,28},{24,0},{28,4},{1,9},{5... | collective-permute-start | bytes 129032 | tf_op jit(solution)/shard_map/ppermute | solution.py:557
  37.3 5.0 %collective-permute-start.7 = (bf16[24,896]{1,0:T(8,128)(2,1)S(1)}, bf16[24,896]{1,0:T(8,128)(2,1)S(1)}, u32[]{:S(2)}, u32[]{:S(2)}) collective-permute-start(bf16[24,896]{1,0:T(8,128)(2,1)S(1)} %get-tuple-element.8.m0_ref), channel_id=1, source_target_pairs={{0,16},{4,20},{8,24},{12,28},{16,0},{20,4},{24,8},{28,12},{1,17},{... | collective-permute-start | bytes 129032 | tf_op jit(solution)/shard_map/ppermute | solution.py:557
  39.6 4.5 %collective-permute-start.8 = (bf16[24,896]{1,0:T(8,128)(2,1)S(1)}, bf16[24,896]{1,0:T(8,128)(2,1)S(1)}, u32[]{:S(2)}, u32[]{:S(2)}) collective-permute-start(bf16[24,896]{1,0:T(8,128)(2,1)S(1)} %get-tuple-element.8.m0_ref), channel_id=1, source_target_pairs={{0,24},{4,28},{8,0},{12,4},{16,8},{20,12},{24,16},{28,20},{1,25},{... | collective-permute-start | bytes 129032 | tf_op jit(solution)/shard_map/ppermute | solution.py:557
  44.1 6.1 %copy-start.21 = (bf16[128,8]{0,1:T(8,128)(2,1)S(1)}, bf16[128,8]{0,1:T(8,128)(2,1)}, u32[]{:S(2)}) copy-start(bf16[128,8]{0,1:T(8,128)(2,1)} %param.19) | copy-start | bytes 6148
  46.1 4.3 %copy-start.20 = (bf16[128,1024]{1,0:T(8,128)(2,1)S(1)}, bf16[128,1024]{1,0:T(8,128)(2,1)}, u32[]{:S(2)}) copy-start(bf16[128,1024]{1,0:T(8,128)(2,1)} %q_ref.1) | copy-start | bytes 786436
  46.1 12.4 %all-to-all-start.1 = ((bf16[32,16,128]{2,1,0:T(8,128)(2,1)}), bf16[32,16,128]{2,1,0:T(8,128)(2,1)S(1)}, u32[]{:S(2)}, u32[]{:S(2)}) async-start(bf16[32,16,128]{2,1,0:T(8,128)(2,1)} %shard_map.188), calls=%async_computation.1 | async-start | bytes 262144 | tf_op jit(solution)/shard_map/all_to_all | solution.py:610

commit v2 on v1

--- a/solution.py
+++ b/solution.py
@@ -256,20 +256,44 @@
 
 
 def partial_kernel(
-    len_ref, k_ref, v_ref, qn_ref, kn_ref, vn_ref, gn_ref, resid_ref, qg_ref, kg_ref, freq_ref,
-    kv_ref, pay_ref, row_q, row_k, row_v, row_g, pay,
+    len_hbm, k_hbm, v_hbm, qn_hbm, kn_hbm, vn_hbm, gn_hbm, resid_hbm, qg_hbm, kg_hbm, freq_hbm,
+    w_hbm, gate_hbm, up_hbm, down_hbm,
+    kv_ref, pay_ref, own_ref, pair_ref, down_pair_ref, row_q, row_k, row_v, row_g, pay, len_ref, k_ref, v_ref, qn_ref, kn_ref, vn_ref, gn_ref,
+    resid_ref, qg_ref, kg_ref, freq_ref, sems,
 ):
     tp = lax.axis_index("tp")
+    req = lax.axis_index("req")
+    z, other = lax.div(req, 2), 1 - lax.rem(req, 2)
+    width = own_ref.shape[1]
+    units = down_pair_ref.shape[0]
+    cols = pl.ds(pl.multiple_of(z * width, lanes), width)
+    theirs = pl.ds(pl.multiple_of(other * units, lanes), units)
+    moves = (
+        (len_hbm, len_ref), (freq_hbm, freq_ref), (k_hbm, k_ref), (kg_hbm, kg_ref),
+        (qn_hbm, qn_ref), (kn_hbm, kn_ref), (vn_hbm, vn_ref), (gn_hbm, gn_ref), (qg_hbm, qg_ref),
+        (v_hbm, v_ref), (resid_hbm, resid_ref),
+        (gate_hbm.at[:, theirs], pair_ref.at[:, pl.ds(0, units)]),
+        (up_hbm.at[:, theirs], pair_ref.at[:, pl.ds(units, units)]),
+        (w_hbm.at[:, cols], own_ref),
+        (down_hbm.at[theirs, :], down_pair_ref),
+    )
+    copies = [pltpu.make_async_copy(a, b, sems.at[i]) for i, (a, b) in enumerate(moves)]
+    for copy in copies:
+        copy.start()
     tok = k_ref.shape[0]
     rpg = qn_ref.shape[0]
     heads = qn_ref.shape[1] // lanes
     kvs = k_ref.shape[1] // lanes
     per = heads // kvs
     rows = heads * rpg
+    for copy in copies[:2]:
+        copy.wait()
     freq = freq_ref[...]
-    qg, kg = qg_ref[...], kg_ref[...]
     tok_index = tp * tok + iota((tok, lanes), 0)
     factors = rope_factors((tok_index - begin_of(tok_index, len_ref)).astype(f32) * freq)
+    for copy in copies[2:11]:
+        copy.wait()
+    qg, kg = qg_ref[...], kg_ref[...]
     keys = []
     for k in range(kvs):
         at = slice(k * lanes, (k + 1) * lanes)
@@ -336,10 +360,16 @@
         out = pay[...].astype(bf16)
         for peer in range(z * peers // slices, (z + 1) * peers // slices):
             pay_ref[peer] = out
+    for copy in copies[11:]:
+        copy.wait()
+
+
+def ready_kernel(*refs):
+    refs[-1][...] = jnp.zeros_like(refs[-1])
 
 
 def hidden_kernel(
-    pay_ref, w0_ref, w1_ref, w2_ref, w3_ref, gate_ref, up_ref, pair_ref, ng_ref,
+    pay_ref, w0_ref, w1_ref, w2_ref, w3_ref, gate_ref, up_ref, pair_ref, ng_ref, _,
     hid_ref, msg_ref, att, hid, xs, acc,
 ):
     tp = lax.axis_index("tp")
@@ -369,7 +399,7 @@
     state = hid[...]
     per = heads // tps
     for d, w_ref in enumerate((w0_ref, w1_ref, w2_ref, w3_ref)):
-        source = lax.rem(tp + tps - d, tps)
+        source = tp ^ d
         for j in range(per):
             state = state + dot(
                 att[source * per + j].astype(bf16), w_ref[j * lanes : (j + 1) * lanes, :]
@@ -457,21 +487,23 @@
 
 
 def prefill_kernel(
-    len_ref, q_ref, g_ref, kv0_ref, kv1_ref, kv2_ref, qg_ref, freq_ref, out_ref
+    len_ref, q_ref, g_ref, kv0_ref, kv1_ref, kv2_ref, kv3_ref, qg_ref, freq_ref, out_ref, mid_ref
 ):
     tp = lax.axis_index("tp")
     tok = q_ref.shape[0]
     heads = q_ref.shape[1] // lanes
     kvs = kv0_ref.shape[1] // (2 * lanes)
     per = heads // kvs
-    blocks = (kv0_ref, kv1_ref, kv2_ref)
+    third = tp == 2
+    mid_ref[...] = jnp.where(third, kv3_ref[...], kv1_ref[...])
+    blocks = ((tp, kv0_ref), (jnp.where(third, tp ^ 3, tp ^ 1), mid_ref), (tp ^ 2, kv2_ref))
     tok_index = tp * tok + iota((tok, lanes), 0)
     begin = begin_of(tok_index, len_ref)
     factors = rope_factors((tok_index - begin).astype(f32) * freq_ref[...])
     col = iota((tok, tok), 1)
     allowed = []
-    for b in range(len(blocks)):
-        key_index = (tp - b) * tok + col
+    for block, _ in blocks:
+        key_index = block * tok + col
         allowed.append((key_index >= begin) & (key_index <= tok_index))
     gates = jax.nn.sigmoid(g_ref[...].astype(f32))
     qg = qg_ref[...]
@@ -482,7 +514,7 @@
         query = norm_rope(q_ref[:, at].astype(f32), qg, factors)
         totals = jnp.zeros((tok, 1), f32)
         mixed = jnp.zeros((tok, lanes), f32)
-        for b, kv_ref in enumerate(blocks):
+        for b, (_, kv_ref) in enumerate(blocks):
             scores = dot_nt(query, kv_ref[:, k * lanes : (k + 1) * lanes])
             weights = jnp.where(allowed[b], jnp.exp(scores * scale), 0.0)
             totals = totals + jnp.sum(weights, axis=-1, keepdims=True)
@@ -492,19 +524,31 @@
         out_ref[:, at] = (mixed / totals * gates[:, h : h + 1]).astype(bf16)
 
 
-def call(body, out_shape, args, scratch=(), smem=0, flops=0, limit=12):
+def call(body, out_shape, args, scratch=(), hbm=False, smem=0, flops=0, limit=12, **more):
     specs = [pl.BlockSpec(memory_space=pltpu.SMEM)] * smem
-    specs += [pl.BlockSpec(memory_space=pltpu.VMEM)] * (len(args) - smem)
+    space = pltpu.HBM if hbm else pltpu.VMEM
+    specs += [pl.BlockSpec(memory_space=space)] * (len(args) - smem)
     size = sum(a.size * a.dtype.itemsize for a in args)
     return pl.pallas_call(
         body,
         out_shape=out_shape,
         in_specs=specs,
         out_specs=jax.tree.map(lambda _: pl.BlockSpec(memory_space=pltpu.VMEM), out_shape),
-        scratch_shapes=[pltpu.VMEM(s, f32) for s in scratch],
+        scratch_shapes=[pltpu.VMEM(s, f32) if isinstance(s, tuple) else s for s in scratch],
         compiler_params=pltpu.CompilerParams(vmem_limit_bytes=limit * 2**20),
         cost_estimate=pl.CostEstimate(flops=flops, bytes_accessed=size, transcendentals=0),
     )(*args)
+
+
+def hold(arrays, flops):
+    return pl.pallas_call(
+        ready_kernel,
+        out_shape=jax.ShapeDtypeStruct((8, lanes), f32),
+        in_specs=[pl.BlockSpec(memory_space=pl.ANY)] * len(arrays),
+        out_specs=pl.BlockSpec(memory_space=pltpu.VMEM),
+        compiler_params=pltpu.CompilerParams(vmem_limit_bytes=2**20),
+        cost_estimate=pl.CostEstimate(flops=flops, bytes_accessed=0, transcendentals=0),
+    )(*arrays)
 
 
 def local(
@@ -547,8 +591,8 @@
     freqs = jnp.asarray(np.concatenate([freqs, freqs])[None, :], f32)
     qg, kg = q_gain[None, :], k_gain[None, :]
 
-    def turn(array, by):
-        return lax.ppermute(array, "tp", [(i, (i + by) % tps) for i in range(tps)])
+    def cross(array, by):
+        return lax.ppermute(array, "tp", [(i, i ^ by) for i in range(tps)])
 
     def swap(array):
         return lax.ppermute(array, "req", [(i, i ^ 1) for i in range(reqs)])
@@ -556,34 +600,44 @@
     def along(array, by):
         return lax.ppermute(array, "req", [(i, (i + 2 * by) % reqs) for i in range(reqs)])
 
-    w_own = lax.dynamic_slice_in_dim(w_out, z * part, part, 1)
-    w_pieces = [w_own] + [turn(w_own, d) for d in range(1, tps)]
-    pair = jnp.concatenate(
-        [lax.dynamic_slice_in_dim(w, (1 - y) * units, units, 1) for w in (w_gate, w_up)], axis=1
-    )
-    pair = swap(pair)
-    down_pair = swap(lax.dynamic_slice_in_dim(w_down, (1 - y) * units, units, 0))
-
-    kv, pay = call(
+    inputs = (
+        lengths, k_pre, v_pre, q_new, k_new, v_new, gate_new, resid, qg, kg, freqs,
+        w_out, w_gate, w_up, w_down,
+    )
+    kv, pay, w_own, pair, down_pair = call(
         partial_kernel,
         (
             jax.ShapeDtypeStruct((tok, 2 * k_pre.shape[1]), bf16),
             jax.ShapeDtypeStruct((peers, pay_rows, lanes), bf16),
+            jax.ShapeDtypeStruct((w_out.shape[0], part), bf16),
+            jax.ShapeDtypeStruct((w_gate.shape[0], 2 * units), bf16),
+            jax.ShapeDtypeStruct((units, w_down.shape[1]), bf16),
         ),
-        (lengths, k_pre, v_pre, q_new, k_new, v_new, gate_new, resid, qg, kg, freqs),
-        scratch=[(heads * rpg, lanes)] * 4 + [(pay_rows, lanes)],
-        smem=1,
+        inputs,
+        scratch=[(heads * rpg, lanes)] * 4
+        + [(pay_rows, lanes), pltpu.SMEM(lengths.shape, jnp.int32)]
+        + [pltpu.VMEM(a.shape, a.dtype) for a in inputs[1:11]]
+        + [pltpu.SemaphoreType.DMA((len(inputs),))],
+        hbm=True,
         flops=10**7,
-    )
-    kv1, kv2 = turn(kv, 1), turn(kv, 2)
+        limit=56,
+    )
+    w_far = cross(w_own, 2)
+    pair = swap(pair)
+    w_near, w_both = cross(w_own, 1), cross(w_far, 1)
+    late_kv, _ = lax.optimization_barrier((kv, w_far))
+    kv_far, kv_near = cross(late_kv, 2), cross(kv, 1)
+    late_down, _ = lax.optimization_barrier((down_pair, pair))
+    down_pair = swap(late_down)
     got = lax.all_to_all(pay, ("req", "tp"), 0, 0, tiled=True)
+    token = hold((pair, w_near, w_both, kv_near), 2 * 10**9)
     hid, msg = call(
         hidden_kernel,
         (
             jax.ShapeDtypeStruct((toks, part), f32),
             jax.ShapeDtypeStruct((toks, 2 * units + lanes), bf16),
         ),
-        (got, *w_pieces, w_gate, w_up, pair, norm_gain[None, :]),
+        (got, w_own, w_near, w_far, w_both, w_gate, w_up, pair, norm_gain[None, :], token),
         scratch=[
             (heads, toks, lanes),
             (toks, part),
@@ -592,14 +646,17 @@
         ],
         flops=10**7,
     )
+    msgs = [msg] + [along(msg, d) for d in range(1, slices)]
+    kv_far, *_ = lax.optimization_barrier((kv_far, *msgs[1:]))
+    kv_both = cross(kv_far, 1)
     prefill_out = call(
         prefill_kernel,
         jax.ShapeDtypeStruct(q_pre.shape, bf16),
-        (lengths, q_pre, gate_pre, kv, kv1, kv2, qg, freqs),
+        (lengths, q_pre, gate_pre, kv, kv_near, kv_far, kv_both, qg, freqs),
+        scratch=[pltpu.VMEM(kv.shape, bf16)],
         smem=1,
         flops=10**9,
     )
-    msgs = [msg] + [along(msg, d) for d in range(1, slices)]
     back = call(
         down_kernel,
         jax.ShapeDtypeStruct((peers, back_rows, lanes), bf16),
@@ -608,6 +665,7 @@
         flops=10**7,
     )
     returned = lax.all_to_all(back, ("req", "tp"), 0, 0, tiled=True)
+    returned, prefill_out = lax.optimization_barrier((returned, prefill_out))
     decode_out = call(
         final_kernel,
         jax.ShapeDtypeStruct((rpg, width), bf16),

time: 59.7 us -> 45 us (0.75)
  local copies, waits for them, and re-layouts: 9.62 us -> 0.69 us
  starting transfers between devices: 23.3 us -> 21 us
  waiting for transfers between devices: 15.5 us -> 13.5 us
  other arithmetic: 0.79 us -> 0 us
    unnamed x45 -> x23, local copies, waits for them, and re-layouts: 8.86 us -> 0.69 us
    ppermute x5 -> x6, waiting for transfers between devices: 8.26 us -> 0.44 us  [cross(): return lax.ppermute(array, 'tp', [(i, i ^ by) for i in range(tps)])]
    ppermute x2, waiting for transfers between devices: 0.01 us -> 4.28 us  [swap(): return lax.ppermute(array, 'req', [(i, i ^ 1) for i in range(reqs)])]
    all_to_all x1, starting transfers between devices: 7.3 us -> 3.97 us  [local(): got = lax.all_to_all(pay, ('req', 'tp'), 0, 0, tiled=True)]
    all_to_all x1, waiting for transfers between devices: 0.01 us -> 1.62 us  [local(): got = lax.all_to_all(pay, ('req', 'tp'), 0, 0, tiled=True)]
    ppermute x2, starting transfers between devices: 2.34 us -> 3.42 us  [swap(): return lax.ppermute(array, 'req', [(i, i ^ 1) for i in range(reqs)])]
    ppermute x5 -> x6, starting transfers between devices: 4.29 us -> 5.33 us  [cross(): return lax.ppermute(array, 'tp', [(i, i ^ by) for i in range(tps)])]
    concatenate x1 -> x0, other arithmetic: 0.79 us -> none  [local(): jnp.concatenate([lax.dynamic_slice_in_dim(w, (1 - y) * units, units, 1) f...]
  transfers between devices with their start and end apart: 12 -> 13, of which waited for: 7 -> 7; matrix products, arithmetic and copies ran while one was open for 3% -> 0% of each run, Pallas kernels for 11% -> 11%
where the time goes in v2:
time: 45 us; the launch traced here: 44.7 us
  starting transfers between devices  21 us (47%)
  waiting for transfers between devices  13.5 us (30%)
  Pallas kernels  8.78 us (20%)
  between operations  0.76 us (2%)
  local copies, waits for them, and re-layouts  0.69 us (2%)
    pallas_call x5, Pallas kernels, call(): pl.pallas_call(body, out_shape=out_shape, in_specs=specs, out_specs=jax.t...  8.77 us
    ppermute x6, starting transfers between devices, cross(): return lax.ppermute(array, 'tp', [(i, i ^ by) for i in range(tps)])  5.33 us
    ppermute x3, starting transfers between devices, along(): lax.ppermute(array, 'req', [(i, (i + 2 * by) % reqs) for i in range(reqs)])  4.47 us
    ppermute x2, waiting for transfers between devices, swap(): return lax.ppermute(array, 'req', [(i, i ^ 1) for i in range(reqs)])  4.28 us
    all_to_all x1, waiting for transfers between devices, local(): returned = lax.all_to_all(back, ('req', 'tp'), 0, 0, tiled=True)  4.21 us
    all_to_all x1, starting transfers between devices, local(): got = lax.all_to_all(pay, ('req', 'tp'), 0, 0, tiled=True)  3.97 us
    all_to_all x1, starting transfers between devices, local(): returned = lax.all_to_all(back, ('req', 'tp'), 0, 0, tiled=True)  3.83 us
    ppermute x2, starting transfers between devices, swap(): return lax.ppermute(array, 'req', [(i, i ^ 1) for i in range(reqs)])  3.42 us
  transfers between devices with their start and end apart: 13, of which 7 were waited for; matrix products, arithmetic and copies ran while one was open for 0% of the time, Pallas kernels for 11%

profile of v2, /device:TPU:0, one launch (start us, length us, event | category | flops | bytes accessed | tf_op | source)
XLA Modules:
  0.0 44.7 jit_solution(2218726407254293598)
XLA Ops:
  0.6 3.0 %shard_map.185 = (bf16[128,1024]{1,0:T(8,128)(2,1)}, bf16[32,32,128]{2,1,0:T(8,128)(2,1)}, bf16[256,512]{1,0:T(8,128)(2,1)}, bf16[256,768]{1,0:T(8,128)(2,1)}, bf16[384,256]{1,0:T(8,128)(2,1)}) custom-call(s32[1,3]{1,0:T(1,128)} %len_ref.1, bf16[128,512]{1,0:T(8,128)(2,1)} %k_hbm.1, bf16[128,512]{1,0:T(8,128)(2,1)} %v_hbm.1, bf16[3,1024]{1,0:T(4,128)(2,1)} %qn_hbm.1, ...), custom_call_target="tpu_custom_call" | custom-call | flops 10000000 | bytes 2516540 | tf_op jit(solution)/shard_map/pallas_call | solution.py:532
  3.6 3.0 %collective-permute-start.1 = (bf16[256,512]{1,0:T(8,128)(2,1)}, bf16[256,512]{1,0:T(8,128)(2,1)S(1)}, u32[]{:S(2)}, u32[]{:S(2)}) collective-permute-start(bf16[256,512]{1,0:T(8,128)(2,1)} %get-tuple-element.15.w0_ref), channel_id=1, source_target_pairs={{0,2},{1,3},{2,0},{3,1},{4,6},{5,7},{6,4},{7,5},{8,10},{9,11},{10,... | collective-permute-start | bytes 786440 | tf_op jit(solution)/shard_map/ppermute | solution.py:595
  6.6 1.5 %collective-permute-start.3 = (bf16[256,768]{1,0:T(8,128)(2,1)}, bf16[256,768]{1,0:T(8,128)(2,1)S(1)}, u32[]{:S(2)}, u32[]{:S(2)}) collective-permute-start(bf16[256,768]{1,0:T(8,128)(2,1)} %get-tuple-element.16), channel_id=1, source_target_pairs={{0,4},{4,0},{8,12},{12,8},{16,20},{20,16},{24,28},{28,24},{1,5},{5... | collective-permute-start | bytes 1179656 | tf_op jit(solution)/shard_map/ppermute | solution.py:598
  8.1 4.0 %all-to-all-start = ((bf16[32,32,128]{2,1,0:T(8,128)(2,1)}), bf16[32,32,128]{2,1,0:T(8,128)(2,1)S(1)}, u32[]{:S(2)}, u32[]{:S(2)}) async-start(bf16[32,32,128]{2,1,0:T(8,128)(2,1)} %get-tuple-element.14), calls=%async_computation | async-start | bytes 524288 | tf_op jit(solution)/shard_map/all_to_all | solution.py:632
  12.1 0.0 copy-done.3
  12.1 0.3 collective-permute-start
  12.4 0.0 copy-done.9
  12.4 0.3 collective-permute-start.4
  12.7 0.4 collective-permute-done.1.w2_ref
  13.1 0.0 collective-permute-start.2
  13.1 1.7 %collective-permute-start.9 = (bf16[128,1024]{1,0:T(8,128)(2,1)S(1)}, bf16[128,1024]{1,0:T(8,128)(2,1)S(1)}, u32[]{:S(2)}, u32[]{:S(2)}) collective-permute-start(bf16[128,1024]{1,0:T(8,128)(2,1)S(1)} %copy-done.9), channel_id=1, source_target_pairs={{0,2},{1,3},{2,0},{3,1},{4,6},{5,7},{6,4},{7,5},{8,10},{9,11},{10,... | collective-permute-start | bytes 786440 | tf_op jit(solution)/shard_map/ppermute | solution.py:595
  14.9 4.3 %collective-permute-done.3.refs_0_.pair_ref = bf16[256,768]{1,0:T(8,128)(2,1)S(1)} collective-permute-done((bf16[256,768]{1,0:T(8,128)(2,1)}, bf16[256,768]{1,0:T(8,128)(2,1)S(1)}, u32[]{:S(2)}, u32[]{:S(2)}) %collective-permute-start.3) | collective-permute-done | bytes 393248 | tf_op jit(solution)/shard_map/ppermute | solution.py:598
  19.1 1.9 %collective-permute-start.8 = (bf16[384,256]{1,0:T(8,128)(2,1)}, bf16[384,256]{1,0:T(8,128)(2,1)S(1)}, u32[]{:S(2)}, u32[]{:S(2)}) collective-permute-start(bf16[384,256]{1,0:T(8,128)(2,1)} %get-tuple-element.21), channel_id=1, source_target_pairs={{0,4},{4,0},{8,12},{12,8},{16,20},{20,16},{24,28},{28,24},{1,5},{5... | collective-permute-start | bytes 589832 | tf_op jit(solution)/shard_map/ppermute | solution.py:598
  21.0 0.0 collective-permute-done.refs_1_.w1_ref
  21.1 0.0 collective-permute-done.4.refs_3_.kv1_ref
  21.1 0.0 collective-permute-done.2.refs_2_.w3_ref
  21.1 1.6 %all-to-all-done.pay_ref = bf16[32,32,128]{2,1,0:T(8,128)(2,1)S(1)} async-done(((bf16[32,32,128]{2,1,0:T(8,128)(2,1)}), bf16[32,32,128]{2,1,0:T(8,128)(2,1)S(1)}, u32[]{:S(2)}, u32[]{:S(2)}) %all-to-all-start) | async-done | bytes 262176 | tf_op jit(solution)/shard_map/all_to_all | solution.py:632
  22.7 0.0 copy-done
  22.7 0.0 copy-done.1
  22.7 0.0 copy-done.4
  22.7 0.0 copy-start.2
  22.7 0.8 %shard_map.187 = (f32[24,512]{1,0:T(8,128)S(1)}, bf16[24,896]{1,0:T(8,128)(2,1)S(1)}) custom-call(bf16[32,32,128]{2,1,0:T(8,128)(2,1)S(1)} %all-to-all-done.pay_ref, bf16[256,512]{1,0:T(8,128)(2,1)S(1)} %copy-done.3, bf16[256,512]{1,0:T(8,128)(2,1)S(1)} %collective-permute-done.refs_1_.w1_ref, bf16[256,512]{1,0:T(8,128)(2,1)S(1)} %collective-permute-done.1.w2_ref, ...), custom_call_target="tpu_custom_call" | custom-call | flops 10000000 | bytes 2502656 | tf_op jit(solution)/shard_map/pallas_call | solution.py:532
  23.5 1.2 %collective-permute-start.5 = (bf16[24,896]{1,0:T(8,128)(2,1)S(1)}, bf16[24,896]{1,0:T(8,128)(2,1)S(1)}, u32[]{:S(2)}, u32[]{:S(2)}) collective-permute-start(bf16[24,896]{1,0:T(8,128)(2,1)S(1)} %get-tuple-element.18.m0_ref), channel_id=1, source_target_pairs={{0,8},{4,12},{8,16},{12,20},{16,24},{20,28},{24,0},{28,4},{1,9},{5... | collective-permute-start | bytes 129032 | tf_op jit(solution)/shard_map/ppermute | solution.py:601
  24.7 1.9 %collective-permute-start.6 = (bf16[24,896]{1,0:T(8,128)(2,1)S(1)}, bf16[24,896]{1,0:T(8,128)(2,1)S(1)}, u32[]{:S(2)}, u32[]{:S(2)}) collective-permute-start(bf16[24,896]{1,0:T(8,128)(2,1)S(1)} %get-tuple-element.18.m0_ref), channel_id=1, source_target_pairs={{0,16},{4,20},{8,24},{12,28},{16,0},{20,4},{24,8},{28,12},{1,17},{... | collective-permute-start | bytes 129032 | tf_op jit(solution)/shard_map/ppermute | solution.py:601
  26.6 1.4 %collective-permute-start.7 = (bf16[24,896]{1,0:T(8,128)(2,1)S(1)}, bf16[24,896]{1,0:T(8,128)(2,1)S(1)}, u32[]{:S(2)}, u32[]{:S(2)}) collective-permute-start(bf16[24,896]{1,0:T(8,128)(2,1)S(1)} %get-tuple-element.18.m0_ref), channel_id=1, source_target_pairs={{0,24},{4,28},{8,0},{12,4},{16,8},{20,12},{24,16},{28,20},{1,25},{... | collective-permute-start | bytes 129032 | tf_op jit(solution)/shard_map/ppermute | solution.py:601
  28.0 0.0 collective-permute-done.9.kv2_ref
  28.0 1.8 %collective-permute-done.5.m1_ref = bf16[24,896]{1,0:T(8,128)(2,1)S(1)} collective-permute-done((bf16[24,896]{1,0:T(8,128)(2,1)S(1)}, bf16[24,896]{1,0:T(8,128)(2,1)S(1)}, u32[]{:S(2)}, u32[]{:S(2)}) %collective-permute-start.5) | collective-permute-done | bytes 43040 | tf_op jit(solution)/shard_map/ppermute | solution.py:601
  29.8 1.0 %collective-permute-done.6.m2_ref = bf16[24,896]{1,0:T(8,128)(2,1)S(1)} collective-permute-done((bf16[24,896]{1,0:T(8,128)(2,1)S(1)}, bf16[24,896]{1,0:T(8,128)(2,1)S(1)}, u32[]{:S(2)}, u32[]{:S(2)}) %collective-permute-start.6) | collective-permute-done | bytes 43040 | tf_op jit(solution)/shard_map/ppermute | solution.py:601
  30.8 0.1 collective-permute-done.7.m3_ref
  30.9 0.0 collective-permute-start.10
  30.9 0.0 collective-permute-done.8.pair_ref
  30.9 0.0 copy-done.2
  30.9 0.0 copy-start.10
  30.9 1.0 %shard_map.188 = bf16[32,16,128]{2,1,0:T(8,128)(2,1)} custom-call(bf16[24,896]{1,0:T(8,128)(2,1)S(1)} %get-tuple-element.18.m0_ref, bf16[24,896]{1,0:T(8,128)(2,1)S(1)} %collective-permute-done.5.m1_ref, bf16[24,896]{1,0:T(8,128)(2,1)S(1)} %collective-permute-done.6.m2_ref, bf16[24,896]{1,0:T(8,128)(2,1)S(1)} %collective-permute-done.7.m3_ref, ...), custom_call_target="tpu_custom_call" | custom-call | flops 10000000 | bytes 811008 | tf_op jit(solution)/shard_map/pallas_call | solution.py:532
  31.9 3.8 %all-to-all-start.1 = ((bf16[32,16,128]{2,1,0:T(8,128)(2,1)}), bf16[32,16,128]{2,1,0:T(8,128)(2,1)S(1)}, u32[]{:S(2)}, u32[]{:S(2)}) async-start(bf16[32,16,128]{2,1,0:T(8,128)(2,1)} %shard_map.188), calls=%async_computation.1 | async-start | bytes 262144 | tf_op jit(solution)/shard_map/all_to_all | solution.py:667
  35.8 0.0 copy-done.10
  35.8 0.0 copy-start.5
  35.8 0.0 copy-start.6
  35.8 0.0 copy-start.7
  35.8 0.1 copy.20.g_ref
  35.9 0.0 collective-permute-done.10.kv3_ref
  36.0 0.0 copy-done.8
  36.0 0.5 %copy-done.5 = s32[1,3]{1,0:T(1,128)S(1)} copy-done((s32[1,3]{1,0:T(1,128)S(1)}, s32[1,3]{1,0:T(1,128)}, u32[]{:S(2)}) %copy-start.5) | copy-done | bytes 36
  36.4 0.0 copy-done.6
  36.5 0.0 copy-done.7
  36.5 3.3 %shard_map.189 = bf16[128,1024]{1,0:T(8,128)(2,1)} custom-call(s32[1,3]{1,0:T(1,128)S(1)} %copy-done.5, bf16[128,1024]{1,0:T(8,128)(2,1)S(1)} %copy-done.8, bf16[128,8]{1,0:T(8,128)(2,1)S(1)} %copy.20.g_ref, bf16[128,1024]{1,0:T(8,128)(2,1)S(1)} %copy-done.9, bf16[128,1024]{1,0:T(8,128)(2,1)S(1)} %collective-permute-done.4.refs_3_.kv1_ref, ...), custom_call_target="tpu_custom_call" | custom-call | flops 1000000000 | bytes 1313804 | tf_op jit(solution)/shard_map/pallas_call | solution.py:532
  39.8 4.2 %all-to-all-done.1.back_ref = bf16[32,16,128]{2,1,0:T(8,128)(2,1)S(1)} async-done(((bf16[32,16,128]{2,1,0:T(8,128)(2,1)}), bf16[32,16,128]{2,1,0:T(8,128)(2,1)S(1)}, u32[]{:S(2)}, u32[]{:S(2)}) %all-to-all-start.1) | async-done | bytes 131104 | tf_op jit(solution)/shard_map/all_to_all | solution.py:667
  44.0 0.7 %shard_map.190 = bf16[3,2048]{1,0:T(4,128)(2,1)} custom-call(bf16[32,16,128]{2,1,0:T(8,128)(2,1)S(1)} %all-to-all-done.1.back_ref), custom_call_target="tpu_custom_call" | custom-call | flops 1000000 | bytes 131072 | tf_op jit(solution)/shard_map/pallas_call | solution.py:532
  (7 shorter events, 0.0 us)
Async XLA Ops:
  3.6 9.5 %collective-permute-start.1 = (bf16[256,512]{1,0:T(8,128)(2,1)}, bf16[256,512]{1,0:T(8,128)(2,1)S(1)}, u32[]{:S(2)}, u32[]{:S(2)}) collective-permute-start(bf16[256,512]{1,0:T(8,128)(2,1)} %get-tuple-element.15.w0_ref), channel_id=1, source_target_pairs={{0,2},{1,3},{2,0},{3,1},{4,6},{5,7},{6,4},{7,5},{8,10},{9,11},{10,... | collective-permute-start | bytes 786440 | tf_op jit(solution)/shard_map/ppermute | solution.py:595
  6.6 12.5 %collective-permute-start.3 = (bf16[256,768]{1,0:T(8,128)(2,1)}, bf16[256,768]{1,0:T(8,128)(2,1)S(1)}, u32[]{:S(2)}, u32[]{:S(2)}) collective-permute-start(bf16[256,768]{1,0:T(8,128)(2,1)} %get-tuple-element.16), channel_id=1, source_target_pairs={{0,4},{4,0},{8,12},{12,8},{16,20},{20,16},{24,28},{28,24},{1,5},{5... | collective-permute-start | bytes 1179656 | tf_op jit(solution)/shard_map/ppermute | solution.py:598
  8.1 4.0 %copy-start.3 = (bf16[256,512]{1,0:T(8,128)(2,1)S(1)}, bf16[256,512]{1,0:T(8,128)(2,1)}, u32[]{:S(2)}) copy-start(bf16[256,512]{1,0:T(8,128)(2,1)} %get-tuple-element.15.w0_ref) | copy-start | bytes 786436
  8.1 4.3 %copy-start.9 = (bf16[128,1024]{1,0:T(8,128)(2,1)S(1)}, bf16[128,1024]{1,0:T(8,128)(2,1)}, u32[]{:S(2)}) copy-start(bf16[128,1024]{1,0:T(8,128)(2,1)} %get-tuple-element.22.kv0_ref) | copy-start | bytes 786436
  8.1 14.6 %all-to-all-start = ((bf16[32,32,128]{2,1,0:T(8,128)(2,1)}), bf16[32,32,128]{2,1,0:T(8,128)(2,1)S(1)}, u32[]{:S(2)}, u32[]{:S(2)}) async-start(bf16[32,32,128]{2,1,0:T(8,128)(2,1)} %get-tuple-element.14), calls=%async_computation | async-start | bytes 524288 | tf_op jit(solution)/shard_map/all_to_all | solution.py:632
  12.1 8.9 %collective-permute-start = (bf16[256,512]{1,0:T(8,128)(2,1)S(1)}, bf16[256,512]{1,0:T(8,128)(2,1)S(1)}, u32[]{:S(2)}, u32[]{:S(2)}) collective-permute-start(bf16[256,512]{1,0:T(8,128)(2,1)S(1)} %copy-done.3), channel_id=1, source_target_pairs={{0,1},{1,0},{2,3},{3,2},{4,5},{5,4},{6,7},{7,6},{8,9},{9,8},{10,11... | collective-permute-start | bytes 786440 | tf_op jit(solution)/shard_map/ppermute | solution.py:595
  12.4 8.6 %collective-permute-start.4 = (bf16[128,1024]{1,0:T(8,128)(2,1)S(1)}, bf16[128,1024]{1,0:T(8,128)(2,1)S(1)}, u32[]{:S(2)}, u32[]{:S(2)}) collective-permute-start(bf16[128,1024]{1,0:T(8,128)(2,1)S(1)} %copy-done.9), channel_id=1, source_target_pairs={{0,1},{1,0},{2,3},{3,2},{4,5},{5,4},{6,7},{7,6},{8,9},{9,8},{10,11... | collective-permute-start | bytes 786440 | tf_op jit(solution)/shard_map/ppermute | solution.py:595
  13.1 7.9 %collective-permute-start.2 = (bf16[256,512]{1,0:T(8,128)(2,1)S(1)}, bf16[256,512]{1,0:T(8,128)(2,1)S(1)}, u32[]{:S(2)}, u32[]{:S(2)}) collective-permute-start(bf16[256,512]{1,0:T(8,128)(2,1)S(1)} %collective-permute-done.1.w2_ref), channel_id=1, source_target_pairs={{0,1},{1,0},{2,3},{3,2},{4,5},{5,4},{6,7},{7,6},{8,9},{9,8},{10,11... | collective-permute-start | bytes 786440 | tf_op jit(solution)/shard_map/ppermute | solution.py:595
  13.1 14.9 %collective-permute-start.9 = (bf16[128,1024]{1,0:T(8,128)(2,1)S(1)}, bf16[128,1024]{1,0:T(8,128)(2,1)S(1)}, u32[]{:S(2)}, u32[]{:S(2)}) collective-permute-start(bf16[128,1024]{1,0:T(8,128)(2,1)S(1)} %copy-done.9), channel_id=1, source_target_pairs={{0,2},{1,3},{2,0},{3,1},{4,6},{5,7},{6,4},{7,5},{8,10},{9,11},{10,... | collective-permute-start | bytes 786440 | tf_op jit(solution)/shard_map/ppermute | solution.py:595
  19.1 3.6 %copy-start = (bf16[256,768]{1,0:T(8,128)(2,1)S(1)}, bf16[256,768]{1,0:T(8,128)(2,1)}, u32[]{:S(2)}) copy-start(bf16[256,768]{1,0:T(8,128)(2,1)} %gate_ref.1) | copy-start | bytes 1179652
  19.1 3.6 %copy-start.1 = (bf16[256,768]{1,0:T(8,128)(2,1)S(1)}, bf16[256,768]{1,0:T(8,128)(2,1)}, u32[]{:S(2)}) copy-start(bf16[256,768]{1,0:T(8,128)(2,1)} %up_ref.1) | copy-start | bytes 1179652
  19.1 3.6 %copy-start.4 = (f32[2048]{0:T(1024)S(1)}, f32[2048]{0:T(1024)}, u32[]{:S(2)}) copy-start(f32[2048]{0:T(1024)} %param.31) | copy-start | bytes 24580
  19.1 11.8 %collective-permute-start.8 = (bf16[384,256]{1,0:T(8,128)(2,1)}, bf16[384,256]{1,0:T(8,128)(2,1)S(1)}, u32[]{:S(2)}, u32[]{:S(2)}) collective-permute-start(bf16[384,256]{1,0:T(8,128)(2,1)} %get-tuple-element.21), channel_id=1, source_target_pairs={{0,4},{4,0},{8,12},{12,8},{16,20},{20,16},{24,28},{28,24},{1,5},{5... | collective-permute-start | bytes 589832 | tf_op jit(solution)/shard_map/ppermute | solution.py:598
  22.7 8.2 %copy-start.2 = (bf16[768,256]{1,0:T(8,128)(2,1)S(1)}, bf16[768,256]{1,0:T(8,128)(2,1)}, u32[]{:S(2)}) copy-start(bf16[768,256]{1,0:T(8,128)(2,1)} %down_ref.1) | copy-start | bytes 1179652
  23.5 6.3 %collective-permute-start.5 = (bf16[24,896]{1,0:T(8,128)(2,1)S(1)}, bf16[24,896]{1,0:T(8,128)(2,1)S(1)}, u32[]{:S(2)}, u32[]{:S(2)}) collective-permute-start(bf16[24,896]{1,0:T(8,128)(2,1)S(1)} %get-tuple-element.18.m0_ref), channel_id=1, source_target_pairs={{0,8},{4,12},{8,16},{12,20},{16,24},{20,28},{24,0},{28,4},{1,9},{5... | collective-permute-start | bytes 129032 | tf_op jit(solution)/shard_map/ppermute | solution.py:601
  24.7 6.1 %collective-permute-start.6 = (bf16[24,896]{1,0:T(8,128)(2,1)S(1)}, bf16[24,896]{1,0:T(8,128)(2,1)S(1)}, u32[]{:S(2)}, u32[]{:S(2)}) collective-permute-start(bf16[24,896]{1,0:T(8,128)(2,1)S(1)} %get-tuple-element.18.m0_ref), channel_id=1, source_target_pairs={{0,16},{4,20},{8,24},{12,28},{16,0},{20,4},{24,8},{28,12},{1,17},{... | collective-permute-start | bytes 129032 | tf_op jit(solution)/shard_map/ppermute | solution.py:601
  26.6 4.3 %collective-permute-start.7 = (bf16[24,896]{1,0:T(8,128)(2,1)S(1)}, bf16[24,896]{1,0:T(8,128)(2,1)S(1)}, u32[]{:S(2)}, u32[]{:S(2)}) collective-permute-start(bf16[24,896]{1,0:T(8,128)(2,1)S(1)} %get-tuple-element.18.m0_ref), channel_id=1, source_target_pairs={{0,24},{4,28},{8,0},{12,4},{16,8},{20,12},{24,16},{28,20},{1,25},{... | collective-permute-start | bytes 129032 | tf_op jit(solution)/shard_map/ppermute | solution.py:601
  30.9 5.0 %collective-permute-start.10 = (bf16[128,1024]{1,0:T(8,128)(2,1)S(1)}, bf16[128,1024]{1,0:T(8,128)(2,1)S(1)}, u32[]{:S(2)}, u32[]{:S(2)}) collective-permute-start(bf16[128,1024]{1,0:T(8,128)(2,1)S(1)} %collective-permute-done.9.kv2_ref), channel_id=1, source_target_pairs={{0,1},{1,0},{2,3},{3,2},{4,5},{5,4},{6,7},{7,6},{8,9},{9,8},{10,11... | collective-permute-start | bytes 786440 | tf_op jit(solution)/shard_map/ppermute | solution.py:595
  30.9 4.9 %copy-start.10 = (bf16[128,8]{0,1:T(8,128)(2,1)S(1)}, bf16[128,8]{0,1:T(8,128)(2,1)}, u32[]{:S(2)}) copy-start(bf16[128,8]{0,1:T(8,128)(2,1)} %param.19) | copy-start | bytes 6148
  31.9 4.0 %copy-start.8 = (bf16[128,1024]{1,0:T(8,128)(2,1)S(1)}, bf16[128,1024]{1,0:T(8,128)(2,1)}, u32[]{:S(2)}) copy-start(bf16[128,1024]{1,0:T(8,128)(2,1)} %q_ref.1) | copy-start | bytes 786436
  31.9 12.1 %all-to-all-start.1 = ((bf16[32,16,128]{2,1,0:T(8,128)(2,1)}), bf16[32,16,128]{2,1,0:T(8,128)(2,1)S(1)}, u32[]{:S(2)}, u32[]{:S(2)}) async-start(bf16[32,16,128]{2,1,0:T(8,128)(2,1)} %shard_map.188), calls=%async_computation.1 | async-start | bytes 262144 | tf_op jit(solution)/shard_map/all_to_all | solution.py:667
  35.8 0.7 %copy-start.5 = (s32[1,3]{1,0:T(1,128)S(1)}, s32[1,3]{1,0:T(1,128)}, u32[]{:S(2)}) copy-start(s32[1,3]{1,0:T(1,128)} %len_ref.1) | copy-start | bytes 40
  35.8 0.7 %copy-start.6 = (f32[128]{0:T(128)S(1)}, f32[128]{0:T(128)}, u32[]{:S(2)}) copy-start(f32[128]{0:T(128)} %param.22) | copy-start | bytes 1540
  35.8 0.7 %copy-start.7 = (f32[1,128]{1,0:T(1,128)S(1)}, f32[1,128]{1,0:T(1,128)}, u32[]{:S(2)}) copy-start(f32[1,128]{1,0:T(1,128)} %constant.2.clone.freq_hbm.freq_ref) | copy-start | bytes 1540

commit v3 on v2

--- a/solution.py
+++ b/solution.py
@@ -364,12 +364,39 @@
         copy.wait()
 
 
+def fetch_kernel(gate_hbm, up_hbm, ng_hbm, mine_ref, ng_ref, sems):
+    units = mine_ref.shape[1] // 2
+    width = ng_ref.shape[1]
+    req = lax.axis_index("req")
+    at = pl.ds(pl.multiple_of(lax.rem(req, 2) * units, lanes), units)
+    cols = pl.ds(pl.multiple_of(lax.div(req, 2) * width, lanes), width)
+    copies = (
+        pltpu.make_async_copy(gate_hbm.at[:, at], mine_ref.at[:, pl.ds(0, units)], sems.at[0]),
+        pltpu.make_async_copy(up_hbm.at[:, at], mine_ref.at[:, pl.ds(units, units)], sems.at[1]),
+        pltpu.make_async_copy(ng_hbm.at[:, cols], ng_ref, sems.at[2]),
+    )
+    for copy in copies:
+        copy.start()
+    for copy in copies:
+        copy.wait()
+
+
+def columns_kernel(w_hbm, w_ref, sems):
+    width = w_ref.shape[1]
+    z = lax.div(lax.axis_index("req"), 2)
+    copy = pltpu.make_async_copy(
+        w_hbm.at[:, pl.ds(pl.multiple_of(z * width, lanes), width)], w_ref, sems.at[0]
+    )
+    copy.start()
+    copy.wait()
+
+
 def ready_kernel(*refs):
     refs[-1][...] = jnp.zeros_like(refs[-1])
 
 
 def hidden_kernel(
-    pay_ref, w0_ref, w1_ref, w2_ref, w3_ref, gate_ref, up_ref, pair_ref, ng_ref, _,
+    pay_ref, w0_ref, w1_ref, w2_ref, w3_ref, mine_ref, pair_ref, ng_ref, _,
     hid_ref, msg_ref, att, hid, xs, acc,
 ):
     tp = lax.axis_index("tp")
@@ -408,14 +435,13 @@
     width = state.shape[1]
     half = width // 2
     sums = jnp.sum(state * state, axis=-1, keepdims=True)
-    scaled = state * ng_ref[:, pl.ds(pl.multiple_of(z * width, lanes), width)]
+    scaled = state * ng_ref[...]
     xs[0] = scaled[:, :half]
     xs[1] = scaled[:, half:]
     own, other = xs[y].astype(bf16), xs[1 - y].astype(bf16)
     units = pair_ref.shape[1] // 2
-    at = pl.ds(pl.multiple_of(y * units, lanes), units)
-    gate = dot(own, gate_ref[:, at]) + dot(other, pair_ref[:, :units])
-    up = dot(own, up_ref[:, at]) + dot(other, pair_ref[:, units:])
+    gate = dot(own, mine_ref[:, :units]) + dot(other, pair_ref[:, :units])
+    up = dot(own, mine_ref[:, units:]) + dot(other, pair_ref[:, units:])
     high = sums.astype(bf16).astype(f32)
     lane = iota((toks, lanes), 1)
     msg_ref[:, :units] = gate.astype(bf16)
@@ -598,7 +624,7 @@
         return lax.ppermute(array, "req", [(i, i ^ 1) for i in range(reqs)])
 
     def along(array, by):
-        return lax.ppermute(array, "req", [(i, (i + 2 * by) % reqs) for i in range(reqs)])
+        return lax.ppermute(array, "req", [(i, i ^ (2 * by)) for i in range(reqs)])
 
     inputs = (
         lengths, k_pre, v_pre, q_new, k_new, v_new, gate_new, resid, qg, kg, freqs,
@@ -624,20 +650,38 @@
     )
     w_far = cross(w_own, 2)
     pair = swap(pair)
-    w_near, w_both = cross(w_own, 1), cross(w_far, 1)
+    half = jax.ShapeDtypeStruct((w_gate.shape[0], 2 * units), bf16)
+    mine, ng = call(
+        fetch_kernel,
+        (half, jax.ShapeDtypeStruct((1, part), f32)),
+        (w_gate, w_up, norm_gain[None, :]),
+        hbm=True,
+        scratch=[pltpu.SemaphoreType.DMA((3,))],
+    )
+    w_here = call(
+        columns_kernel,
+        jax.ShapeDtypeStruct(w_own.shape, bf16),
+        (w_out,),
+        hbm=True,
+        scratch=[pltpu.SemaphoreType.DMA((1,))],
+    )
+    late_far, _, _ = lax.optimization_barrier((w_far, mine, w_here))
+    w_near, w_both = cross(w_own, 1), cross(late_far, 1)
+    kv_near = cross(kv, 1)
     late_kv, _ = lax.optimization_barrier((kv, w_far))
-    kv_far, kv_near = cross(late_kv, 2), cross(kv, 1)
-    late_down, _ = lax.optimization_barrier((down_pair, pair))
+    kv_far = cross(late_kv, 2)
+    late_down, _ = lax.optimization_barrier((down_pair, w_far))
     down_pair = swap(late_down)
     got = lax.all_to_all(pay, ("req", "tp"), 0, 0, tiled=True)
-    token = hold((pair, w_near, w_both, kv_near), 2 * 10**9)
+    landed = hold((pair,), 2 * 10**9)
+    token = hold((landed, w_near, w_both), 10**9)
     hid, msg = call(
         hidden_kernel,
         (
             jax.ShapeDtypeStruct((toks, part), f32),
             jax.ShapeDtypeStruct((toks, 2 * units + lanes), bf16),
         ),
-        (got, w_own, w_near, w_far, w_both, w_gate, w_up, pair, norm_gain[None, :], token),
+        (got, w_here, w_near, w_far, w_both, mine, pair, ng, token),
         scratch=[
             (heads, toks, lanes),
             (toks, part),
@@ -646,8 +690,7 @@
         ],
         flops=10**7,
     )
-    msgs = [msg] + [along(msg, d) for d in range(1, slices)]
-    kv_far, *_ = lax.optimization_barrier((kv_far, *msgs[1:]))
+    msgs = [msg] + [along(msg, d) for d in (3, 2, 1)]
     kv_both = cross(kv_far, 1)
     prefill_out = call(
         prefill_kernel,
@@ -662,7 +705,7 @@
         jax.ShapeDtypeStruct((peers, back_rows, lanes), bf16),
         (*msgs, hid, w_down, down_pair),
         scratch=[(2, toks, part // 2), (reqs, back_rows, lanes)],
-        flops=10**7,
+        flops=3 * 10**9,
     )
     returned = lax.all_to_all(back, ("req", "tp"), 0, 0, tiled=True)
     returned, prefill_out = lax.optimization_barrier((returned, prefill_out))

time: 45 us -> 43.9 us (0.976)
  starting transfers between devices: 21 us -> 19.2 us
  local copies, waits for them, and re-layouts: 0.69 us -> 1.41 us
    ppermute x2, waiting for transfers between devices: 4.28 us -> 0.01 us  [swap(): return lax.ppermute(array, 'req', [(i, i ^ 1) for i in range(reqs)])]
    all_to_all x1, waiting for transfers between devices: 1.62 us -> 5.27 us  [local(): got = lax.all_to_all(pay, ('req', 'tp'), 0, 0, tiled=True)]
    ppermute x6, starting transfers between devices: 5.33 us -> 3.78 us  [cross(): return lax.ppermute(array, 'tp', [(i, i ^ by) for i in range(tps)])]
    all_to_all x1, starting transfers between devices: 3.83 us -> 2.69 us  [local(): returned = lax.all_to_all(back, ('req', 'tp'), 0, 0, tiled=True)]
    ppermute x2, starting transfers between devices: 3.42 us -> 4.35 us  [swap(): return lax.ppermute(array, 'req', [(i, i ^ 1) for i in range(reqs)])]
    ppermute x6, waiting for transfers between devices: 0.44 us -> 1.3 us  [cross(): return lax.ppermute(array, 'tp', [(i, i ^ by) for i in range(tps)])]
    unnamed x23 -> x27, local copies, waits for them, and re-layouts: 0.69 us -> 1.41 us
    ppermute x3, waiting for transfers between devices: 2.92 us -> 2.44 us  [along(): return lax.ppermute(array, 'req', [(i, i ^ 2 * by) for i in range(reqs)])]
  transfers between devices with their start and end apart: 13 -> 13, of which waited for: 7 -> 5; matrix products, arithmetic and copies ran while one was open for 0% -> 0% of each run, Pallas kernels for 11% -> 12%
where the time goes in v3:
time: 43.9 us; the launch traced here: 43.6 us
  starting transfers between devices  19.2 us (44%)
  waiting for transfers between devices  13.2 us (30%)
  Pallas kernels  8.94 us (20%)
  local copies, waits for them, and re-layouts  1.41 us (3%)
  between operations  0.81 us (2%)
    pallas_call x7, Pallas kernels, call(): pl.pallas_call(body, out_shape=out_shape, in_specs=specs, out_specs=jax.t...  8.94 us
    all_to_all x1, waiting for transfers between devices, local(): got = lax.all_to_all(pay, ('req', 'tp'), 0, 0, tiled=True)  5.27 us
    ppermute x3, starting transfers between devices, along(): return lax.ppermute(array, 'req', [(i, i ^ 2 * by) for i in range(reqs)])  4.45 us
    ppermute x2, starting transfers between devices, swap(): return lax.ppermute(array, 'req', [(i, i ^ 1) for i in range(reqs)])  4.35 us
    all_to_all x1, waiting for transfers between devices, local(): returned = lax.all_to_all(back, ('req', 'tp'), 0, 0, tiled=True)  4.21 us
    all_to_all x1, starting transfers between devices, local(): got = lax.all_to_all(pay, ('req', 'tp'), 0, 0, tiled=True)  3.97 us
    ppermute x6, starting transfers between devices, cross(): return lax.ppermute(array, 'tp', [(i, i ^ by) for i in range(tps)])  3.78 us
    all_to_all x1, starting transfers between devices, local(): returned = lax.all_to_all(back, ('req', 'tp'), 0, 0, tiled=True)  2.69 us
  transfers between devices with their start and end apart: 13, of which 5 were waited for; matrix products, arithmetic and copies ran while one was open for 0% of the time, Pallas kernels for 12%

profile of v3, /device:TPU:0, one launch (start us, length us, event | category | flops | bytes accessed | tf_op | source)
XLA Modules:
  0.0 43.6 jit_solution(4813865505741422345)
XLA Ops:
  0.6 0.0 copy-start
  0.6 3.0 %shard_map.185 = (bf16[128,1024]{1,0:T(8,128)(2,1)}, bf16[32,32,128]{2,1,0:T(8,128)(2,1)}, bf16[256,512]{1,0:T(8,128)(2,1)}, bf16[256,768]{1,0:T(8,128)(2,1)}, bf16[384,256]{1,0:T(8,128)(2,1)}) custom-call(s32[1,3]{1,0:T(1,128)} %len_ref.1, bf16[128,512]{1,0:T(8,128)(2,1)} %k_hbm.1, bf16[128,512]{1,0:T(8,128)(2,1)} %v_hbm.1, bf16[3,1024]{1,0:T(4,128)(2,1)} %qn_hbm.1, ...), custom_call_target="tpu_custom_call" | custom-call | flops 10000000 | bytes 2516540 | tf_op jit(solution)/shard_map/pallas_call | solution.py:558
  3.7 3.0 %collective-permute-start.3 = (bf16[256,768]{1,0:T(8,128)(2,1)}, bf16[256,768]{1,0:T(8,128)(2,1)S(1)}, u32[]{:S(2)}, u32[]{:S(2)}) collective-permute-start(bf16[256,768]{1,0:T(8,128)(2,1)} %get-tuple-element.20), channel_id=1, source_target_pairs={{0,4},{4,0},{8,12},{12,8},{16,20},{20,16},{24,28},{28,24},{1,5},{5... | collective-permute-start | bytes 1179656 | tf_op jit(solution)/shard_map/ppermute | solution.py:624
  6.7 1.5 %collective-permute-start.1 = (bf16[256,512]{1,0:T(8,128)(2,1)}, bf16[256,512]{1,0:T(8,128)(2,1)S(1)}, u32[]{:S(2)}, u32[]{:S(2)}) collective-permute-start(bf16[256,512]{1,0:T(8,128)(2,1)} %get-tuple-element.17), channel_id=1, source_target_pairs={{0,2},{1,3},{2,0},{3,1},{4,6},{5,7},{6,4},{7,5},{8,10},{9,11},{10,... | collective-permute-start | bytes 786440 | tf_op jit(solution)/shard_map/ppermute | solution.py:621
  8.2 4.0 %all-to-all-start = ((bf16[32,32,128]{2,1,0:T(8,128)(2,1)}), bf16[32,32,128]{2,1,0:T(8,128)(2,1)S(1)}, u32[]{:S(2)}, u32[]{:S(2)}) async-start(bf16[32,32,128]{2,1,0:T(8,128)(2,1)} %get-tuple-element.16), calls=%async_computation | async-start | bytes 524288 | tf_op jit(solution)/shard_map/all_to_all | solution.py:675
  12.2 0.0 copy-done.11
  12.2 0.0 copy-start.1
  12.2 0.0 copy-start.2
  12.2 0.0 copy-start.4
  12.2 0.3 collective-permute-start
  12.5 0.0 copy-done
  12.6 0.6 %copy-done.1 = bf16[256,768]{1,0:T(8,128)(2,1)S(1)} copy-done((bf16[256,768]{1,0:T(8,128)(2,1)S(1)}, bf16[256,768]{1,0:T(8,128)(2,1)}, u32[]{:S(2)}) %copy-start.1) | copy-done | bytes 393240
  13.2 0.1 copy-done.2
  13.3 0.1 shard_map.187
  13.4 1.3 %collective-permute-done.1.w2_ref = bf16[256,512]{1,0:T(8,128)(2,1)S(1)} collective-permute-done((bf16[256,512]{1,0:T(8,128)(2,1)}, bf16[256,512]{1,0:T(8,128)(2,1)S(1)}, u32[]{:S(2)}, u32[]{:S(2)}) %collective-permute-start.1) | collective-permute-done | bytes 262176 | tf_op jit(solution)/shard_map/ppermute | solution.py:621
  14.7 0.0 collective-permute-start.2
  14.7 0.0 copy-done.12
  14.7 1.3 %collective-permute-start.7 = (bf16[384,256]{1,0:T(8,128)(2,1)S(1)}, bf16[384,256]{1,0:T(8,128)(2,1)S(1)}, u32[]{:S(2)}, u32[]{:S(2)}) collective-permute-start(bf16[384,256]{1,0:T(8,128)(2,1)S(1)} %copy-done.12), channel_id=1, source_target_pairs={{0,4},{4,0},{8,12},{12,8},{16,20},{20,16},{24,28},{28,24},{1,5},{5... | collective-permute-start | bytes 589832 | tf_op jit(solution)/shard_map/ppermute | solution.py:624
  16.0 1.5 %collective-permute-start.9 = (bf16[128,1024]{1,0:T(8,128)(2,1)S(1)}, bf16[128,1024]{1,0:T(8,128)(2,1)S(1)}, u32[]{:S(2)}, u32[]{:S(2)}) collective-permute-start(bf16[128,1024]{1,0:T(8,128)(2,1)S(1)} %copy-done.9), channel_id=1, source_target_pairs={{0,2},{1,3},{2,0},{3,1},{4,6},{5,7},{6,4},{7,5},{8,10},{9,11},{10,... | collective-permute-start | bytes 786440 | tf_op jit(solution)/shard_map/ppermute | solution.py:621
  17.5 0.0 collective-permute-done.3.refs_0_.pair_ref
  17.5 0.0 collective-permute-done.refs_1_.w1_ref
  17.5 0.0 collective-permute-done.2.refs_2_.w3_ref
  17.5 5.3 %all-to-all-done.pay_ref = bf16[32,32,128]{2,1,0:T(8,128)(2,1)S(1)} async-done(((bf16[32,32,128]{2,1,0:T(8,128)(2,1)}), bf16[32,32,128]{2,1,0:T(8,128)(2,1)S(1)}, u32[]{:S(2)}, u32[]{:S(2)}) %all-to-all-start) | async-done | bytes 262176 | tf_op jit(solution)/shard_map/all_to_all | solution.py:675
  22.8 0.8 %shard_map.190 = (f32[24,512]{1,0:T(8,128)S(1)}, bf16[24,896]{1,0:T(8,128)(2,1)S(1)}) custom-call(bf16[32,32,128]{2,1,0:T(8,128)(2,1)S(1)} %all-to-all-done.pay_ref, bf16[256,512]{1,0:T(8,128)(2,1)S(1)} %shard_map.186.w0_ref, bf16[256,512]{1,0:T(8,128)(2,1)S(1)} %collective-permute-done.refs_1_.w1_ref, bf16[256,512]{1,0:T(8,128)(2,1)S(1)} %collective-permute-done.1.w2_ref, ...), custom_call_target="tpu_custom_call" | custom-call | flops 10000000 | bytes 2103296 | tf_op jit(solution)/shard_map/pallas_call | solution.py:558
  23.6 1.4 %collective-permute-start.4 = (bf16[24,896]{1,0:T(8,128)(2,1)S(1)}, bf16[24,896]{1,0:T(8,128)(2,1)S(1)}, u32[]{:S(2)}, u32[]{:S(2)}) collective-permute-start(bf16[24,896]{1,0:T(8,128)(2,1)S(1)} %get-tuple-element.22.m0_ref), channel_id=1, source_target_pairs={{0,24},{4,28},{8,16},{12,20},{16,8},{20,12},{24,0},{28,4},{1,25},{... | collective-permute-start | bytes 129032 | tf_op jit(solution)/shard_map/ppermute | solution.py:627
  25.0 1.2 %collective-permute-start.5 = (bf16[24,896]{1,0:T(8,128)(2,1)S(1)}, bf16[24,896]{1,0:T(8,128)(2,1)S(1)}, u32[]{:S(2)}, u32[]{:S(2)}) collective-permute-start(bf16[24,896]{1,0:T(8,128)(2,1)S(1)} %get-tuple-element.22.m0_ref), channel_id=1, source_target_pairs={{0,16},{4,20},{8,24},{12,28},{16,0},{20,4},{24,8},{28,12},{1,17},{... | collective-permute-start | bytes 129032 | tf_op jit(solution)/shard_map/ppermute | solution.py:627
  26.2 1.8 %collective-permute-start.6 = (bf16[24,896]{1,0:T(8,128)(2,1)S(1)}, bf16[24,896]{1,0:T(8,128)(2,1)S(1)}, u32[]{:S(2)}, u32[]{:S(2)}) collective-permute-start(bf16[24,896]{1,0:T(8,128)(2,1)S(1)} %get-tuple-element.22.m0_ref), channel_id=1, source_target_pairs={{0,8},{4,12},{8,0},{12,4},{16,24},{20,28},{24,16},{28,20},{1,9},{5... | collective-permute-start | bytes 129032 | tf_op jit(solution)/shard_map/ppermute | solution.py:627
  28.0 0.0 collective-permute-done.7.pair_ref
  28.0 0.0 collective-permute-start.8
  28.0 0.0 collective-permute-done.9.kv2_ref
  28.0 0.5 %collective-permute-start.10 = (bf16[128,1024]{1,0:T(8,128)(2,1)S(1)}, bf16[128,1024]{1,0:T(8,128)(2,1)S(1)}, u32[]{:S(2)}, u32[]{:S(2)}) collective-permute-start(bf16[128,1024]{1,0:T(8,128)(2,1)S(1)} %collective-permute-done.9.kv2_ref), channel_id=1, source_target_pairs={{0,1},{1,0},{2,3},{3,2},{4,5},{5,4},{6,7},{7,6},{8,9},{9,8},{10,11... | collective-permute-start | bytes 786440 | tf_op jit(solution)/shard_map/ppermute | solution.py:621
  28.5 1.3 %collective-permute-done.4.m1_ref = bf16[24,896]{1,0:T(8,128)(2,1)S(1)} collective-permute-done((bf16[24,896]{1,0:T(8,128)(2,1)S(1)}, bf16[24,896]{1,0:T(8,128)(2,1)S(1)}, u32[]{:S(2)}, u32[]{:S(2)}) %collective-permute-start.4) | collective-permute-done | bytes 43040 | tf_op jit(solution)/shard_map/ppermute | solution.py:627
  29.8 1.2 %collective-permute-done.5.m2_ref = bf16[24,896]{1,0:T(8,128)(2,1)S(1)} collective-permute-done((bf16[24,896]{1,0:T(8,128)(2,1)S(1)}, bf16[24,896]{1,0:T(8,128)(2,1)S(1)}, u32[]{:S(2)}, u32[]{:S(2)}) %collective-permute-start.5) | collective-permute-done | bytes 43040 | tf_op jit(solution)/shard_map/ppermute | solution.py:627
  31.0 0.0 collective-permute-done.6.m3_ref
  31.0 1.0 %shard_map.191 = bf16[32,16,128]{2,1,0:T(8,128)(2,1)} custom-call(bf16[24,896]{1,0:T(8,128)(2,1)S(1)} %get-tuple-element.22.m0_ref, bf16[24,896]{1,0:T(8,128)(2,1)S(1)} %collective-permute-done.4.m1_ref, bf16[24,896]{1,0:T(8,128)(2,1)S(1)} %collective-permute-done.5.m2_ref, bf16[24,896]{1,0:T(8,128)(2,1)S(1)} %collective-permute-done.6.m3_ref, ...), custom_call_target="tpu_custom_call" | custom-call | flops 3000000000 | bytes 811008 | tf_op jit(solution)/shard_map/pallas_call | solution.py:558
  32.0 2.7 %all-to-all-start.1 = ((bf16[32,16,128]{2,1,0:T(8,128)(2,1)}), bf16[32,16,128]{2,1,0:T(8,128)(2,1)S(1)}, u32[]{:S(2)}, u32[]{:S(2)}) async-start(bf16[32,16,128]{2,1,0:T(8,128)(2,1)} %shard_map.191), calls=%async_computation.1 | async-start | bytes 262144 | tf_op jit(solution)/shard_map/all_to_all | solution.py:710
  34.7 0.0 copy-start.5
  34.7 0.0 copy-start.6
  34.7 0.0 copy-start.7
  34.7 0.1 copy.20.g_ref
  34.9 0.0 collective-permute-done.8.kv1_ref
  34.9 0.0 collective-permute-done.10.kv3_ref
  34.9 0.5 %copy-done.5 = s32[1,3]{1,0:T(1,128)S(1)} copy-done((s32[1,3]{1,0:T(1,128)S(1)}, s32[1,3]{1,0:T(1,128)}, u32[]{:S(2)}) %copy-start.5) | copy-done | bytes 36
  35.4 0.0 copy-done.6
  35.4 0.0 copy-done.7
  35.4 3.3 %shard_map.192 = bf16[128,1024]{1,0:T(8,128)(2,1)} custom-call(s32[1,3]{1,0:T(1,128)S(1)} %copy-done.5, bf16[128,1024]{1,0:T(8,128)(2,1)S(1)} %copy-done.8, bf16[128,8]{1,0:T(8,128)(2,1)S(1)} %copy.20.g_ref, bf16[128,1024]{1,0:T(8,128)(2,1)S(1)} %copy-done.9, bf16[128,1024]{1,0:T(8,128)(2,1)S(1)} %collective-permute-done.8.kv1_ref, ...), custom_call_target="tpu_custom_call" | custom-call | flops 1000000000 | bytes 1313804 | tf_op jit(solution)/shard_map/pallas_call | solution.py:558
  38.7 4.2 %all-to-all-done.1.back_ref = bf16[32,16,128]{2,1,0:T(8,128)(2,1)S(1)} async-done(((bf16[32,16,128]{2,1,0:T(8,128)(2,1)}), bf16[32,16,128]{2,1,0:T(8,128)(2,1)S(1)}, u32[]{:S(2)}, u32[]{:S(2)}) %all-to-all-start.1) | async-done | bytes 131104 | tf_op jit(solution)/shard_map/all_to_all | solution.py:710
  42.9 0.7 %shard_map.193 = bf16[3,2048]{1,0:T(4,128)(2,1)} custom-call(bf16[32,16,128]{2,1,0:T(8,128)(2,1)S(1)} %all-to-all-done.1.back_ref), custom_call_target="tpu_custom_call" | custom-call | flops 1000000 | bytes 131072 | tf_op jit(solution)/shard_map/pallas_call | solution.py:558
  (14 shorter events, 0.1 us)
Async XLA Ops:
  0.6 11.9 %copy-start = (bf16[256,2048]{1,0:T(8,128)(2,1)S(1)}, bf16[256,2048]{1,0:T(8,128)(2,1)}, u32[]{:S(2)}) copy-start(bf16[256,2048]{1,0:T(8,128)(2,1)} %w_hbm.3) | copy-start | bytes 3145732
  3.7 13.8 %collective-permute-start.3 = (bf16[256,768]{1,0:T(8,128)(2,1)}, bf16[256,768]{1,0:T(8,128)(2,1)S(1)}, u32[]{:S(2)}, u32[]{:S(2)}) collective-permute-start(bf16[256,768]{1,0:T(8,128)(2,1)} %get-tuple-element.20), channel_id=1, source_target_pairs={{0,4},{4,0},{8,12},{12,8},{16,20},{20,16},{24,28},{28,24},{1,5},{5... | collective-permute-start | bytes 1179656 | tf_op jit(solution)/shard_map/ppermute | solution.py:624
  6.7 8.0 %collective-permute-start.1 = (bf16[256,512]{1,0:T(8,128)(2,1)}, bf16[256,512]{1,0:T(8,128)(2,1)S(1)}, u32[]{:S(2)}, u32[]{:S(2)}) collective-permute-start(bf16[256,512]{1,0:T(8,128)(2,1)} %get-tuple-element.17), channel_id=1, source_target_pairs={{0,2},{1,3},{2,0},{3,1},{4,6},{5,7},{6,4},{7,5},{8,10},{9,11},{10,... | collective-permute-start | bytes 786440 | tf_op jit(solution)/shard_map/ppermute | solution.py:621
  8.2 4.0 %copy-start.11 = (bf16[256,512]{1,0:T(8,128)(2,1)S(1)}, bf16[256,512]{1,0:T(8,128)(2,1)}, u32[]{:S(2)}) copy-start(bf16[256,512]{1,0:T(8,128)(2,1)} %get-tuple-element.17) | copy-start | bytes 786436
  8.2 14.6 %all-to-all-start = ((bf16[32,32,128]{2,1,0:T(8,128)(2,1)}), bf16[32,32,128]{2,1,0:T(8,128)(2,1)S(1)}, u32[]{:S(2)}, u32[]{:S(2)}) async-start(bf16[32,32,128]{2,1,0:T(8,128)(2,1)} %get-tuple-element.16), calls=%async_computation | async-start | bytes 524288 | tf_op jit(solution)/shard_map/all_to_all | solution.py:675
  12.2 1.0 %copy-start.1 = (bf16[256,768]{1,0:T(8,128)(2,1)S(1)}, bf16[256,768]{1,0:T(8,128)(2,1)}, u32[]{:S(2)}) copy-start(bf16[256,768]{1,0:T(8,128)(2,1)} %gate_hbm.3) | copy-start | bytes 1179652
  12.2 1.1 %copy-start.2 = (bf16[256,768]{1,0:T(8,128)(2,1)S(1)}, bf16[256,768]{1,0:T(8,128)(2,1)}, u32[]{:S(2)}) copy-start(bf16[256,768]{1,0:T(8,128)(2,1)} %up_hbm.3) | copy-start | bytes 1179652
  12.2 1.1 %copy-start.4 = (f32[2048]{0:T(1024)S(1)}, f32[2048]{0:T(1024)}, u32[]{:S(2)}) copy-start(f32[2048]{0:T(1024)} %param.31) | copy-start | bytes 24580
  12.2 5.3 %collective-permute-start = (bf16[256,512]{1,0:T(8,128)(2,1)S(1)}, bf16[256,512]{1,0:T(8,128)(2,1)S(1)}, u32[]{:S(2)}, u32[]{:S(2)}) collective-permute-start(bf16[256,512]{1,0:T(8,128)(2,1)S(1)} %copy-done.11), channel_id=1, source_target_pairs={{0,1},{1,0},{2,3},{3,2},{4,5},{5,4},{6,7},{7,6},{8,9},{9,8},{10,11... | collective-permute-start | bytes 786440 | tf_op jit(solution)/shard_map/ppermute | solution.py:621
  13.3 1.4 %copy-start.12 = (bf16[384,256]{1,0:T(8,128)(2,1)S(1)}, bf16[384,256]{1,0:T(8,128)(2,1)}, u32[]{:S(2)}) copy-start(bf16[384,256]{1,0:T(8,128)(2,1)} %get-tuple-element.25) | copy-start | bytes 589828
  13.3 2.7 %copy-start.9 = (bf16[128,1024]{1,0:T(8,128)(2,1)S(1)}, bf16[128,1024]{1,0:T(8,128)(2,1)}, u32[]{:S(2)}) copy-start(bf16[128,1024]{1,0:T(8,128)(2,1)} %get-tuple-element.27.kv0_ref) | copy-start | bytes 786436
  14.7 2.8 %collective-permute-start.2 = (bf16[256,512]{1,0:T(8,128)(2,1)S(1)}, bf16[256,512]{1,0:T(8,128)(2,1)S(1)}, u32[]{:S(2)}, u32[]{:S(2)}) collective-permute-start(bf16[256,512]{1,0:T(8,128)(2,1)S(1)} %collective-permute-done.1.w2_ref), channel_id=1, source_target_pairs={{0,1},{1,0},{2,3},{3,2},{4,5},{5,4},{6,7},{7,6},{8,9},{9,8},{10,11... | collective-permute-start | bytes 786440 | tf_op jit(solution)/shard_map/ppermute | solution.py:621
  14.7 13.3 %collective-permute-start.7 = (bf16[384,256]{1,0:T(8,128)(2,1)S(1)}, bf16[384,256]{1,0:T(8,128)(2,1)S(1)}, u32[]{:S(2)}, u32[]{:S(2)}) collective-permute-start(bf16[384,256]{1,0:T(8,128)(2,1)S(1)} %copy-done.12), channel_id=1, source_target_pairs={{0,4},{4,0},{8,12},{12,8},{16,20},{20,16},{24,28},{28,24},{1,5},{5... | collective-permute-start | bytes 589832 | tf_op jit(solution)/shard_map/ppermute | solution.py:624
  16.0 12.0 %collective-permute-start.9 = (bf16[128,1024]{1,0:T(8,128)(2,1)S(1)}, bf16[128,1024]{1,0:T(8,128)(2,1)S(1)}, u32[]{:S(2)}, u32[]{:S(2)}) collective-permute-start(bf16[128,1024]{1,0:T(8,128)(2,1)S(1)} %copy-done.9), channel_id=1, source_target_pairs={{0,2},{1,3},{2,0},{3,1},{4,6},{5,7},{6,4},{7,5},{8,10},{9,11},{10,... | collective-permute-start | bytes 786440 | tf_op jit(solution)/shard_map/ppermute | solution.py:621
  22.8 8.2 %copy-start.3 = (bf16[768,256]{1,0:T(8,128)(2,1)S(1)}, bf16[768,256]{1,0:T(8,128)(2,1)}, u32[]{:S(2)}) copy-start(bf16[768,256]{1,0:T(8,128)(2,1)} %down_ref.1) | copy-start | bytes 1179652
  23.6 6.2 %collective-permute-start.4 = (bf16[24,896]{1,0:T(8,128)(2,1)S(1)}, bf16[24,896]{1,0:T(8,128)(2,1)S(1)}, u32[]{:S(2)}, u32[]{:S(2)}) collective-permute-start(bf16[24,896]{1,0:T(8,128)(2,1)S(1)} %get-tuple-element.22.m0_ref), channel_id=1, source_target_pairs={{0,24},{4,28},{8,16},{12,20},{16,8},{20,12},{24,0},{28,4},{1,25},{... | collective-permute-start | bytes 129032 | tf_op jit(solution)/shard_map/ppermute | solution.py:627
  25.0 6.0 %collective-permute-start.5 = (bf16[24,896]{1,0:T(8,128)(2,1)S(1)}, bf16[24,896]{1,0:T(8,128)(2,1)S(1)}, u32[]{:S(2)}, u32[]{:S(2)}) collective-permute-start(bf16[24,896]{1,0:T(8,128)(2,1)S(1)} %get-tuple-element.22.m0_ref), channel_id=1, source_target_pairs={{0,16},{4,20},{8,24},{12,28},{16,0},{20,4},{24,8},{28,12},{1,17},{... | collective-permute-start | bytes 129032 | tf_op jit(solution)/shard_map/ppermute | solution.py:627
  26.2 4.8 %collective-permute-start.6 = (bf16[24,896]{1,0:T(8,128)(2,1)S(1)}, bf16[24,896]{1,0:T(8,128)(2,1)S(1)}, u32[]{:S(2)}, u32[]{:S(2)}) collective-permute-start(bf16[24,896]{1,0:T(8,128)(2,1)S(1)} %get-tuple-element.22.m0_ref), channel_id=1, source_target_pairs={{0,8},{4,12},{8,0},{12,4},{16,24},{20,28},{24,16},{28,20},{1,9},{5... | collective-permute-start | bytes 129032 | tf_op jit(solution)/shard_map/ppermute | solution.py:627
  28.0 6.8 %collective-permute-start.8 = (bf16[128,1024]{1,0:T(8,128)(2,1)S(1)}, bf16[128,1024]{1,0:T(8,128)(2,1)S(1)}, u32[]{:S(2)}, u32[]{:S(2)}) collective-permute-start(bf16[128,1024]{1,0:T(8,128)(2,1)S(1)} %copy-done.9), channel_id=1, source_target_pairs={{0,1},{1,0},{2,3},{3,2},{4,5},{5,4},{6,7},{7,6},{8,9},{9,8},{10,11... | collective-permute-start | bytes 786440 | tf_op jit(solution)/shard_map/ppermute | solution.py:621
  28.0 6.8 %collective-permute-start.10 = (bf16[128,1024]{1,0:T(8,128)(2,1)S(1)}, bf16[128,1024]{1,0:T(8,128)(2,1)S(1)}, u32[]{:S(2)}, u32[]{:S(2)}) collective-permute-start(bf16[128,1024]{1,0:T(8,128)(2,1)S(1)} %collective-permute-done.9.kv2_ref), channel_id=1, source_target_pairs={{0,1},{1,0},{2,3},{3,2},{4,5},{5,4},{6,7},{7,6},{8,9},{9,8},{10,11... | collective-permute-start | bytes 786440 | tf_op jit(solution)/shard_map/ppermute | solution.py:621
  31.0 3.7 %copy-start.10 = (bf16[128,8]{0,1:T(8,128)(2,1)S(1)}, bf16[128,8]{0,1:T(8,128)(2,1)}, u32[]{:S(2)}) copy-start(bf16[128,8]{0,1:T(8,128)(2,1)} %param.19) | copy-start | bytes 6148
  32.0 2.9 %copy-start.8 = (bf16[128,1024]{1,0:T(8,128)(2,1)S(1)}, bf16[128,1024]{1,0:T(8,128)(2,1)}, u32[]{:S(2)}) copy-start(bf16[128,1024]{1,0:T(8,128)(2,1)} %q_ref.1) | copy-start | bytes 786436
  32.0 10.9 %all-to-all-start.1 = ((bf16[32,16,128]{2,1,0:T(8,128)(2,1)}), bf16[32,16,128]{2,1,0:T(8,128)(2,1)S(1)}, u32[]{:S(2)}, u32[]{:S(2)}) async-start(bf16[32,16,128]{2,1,0:T(8,128)(2,1)} %shard_map.191), calls=%async_computation.1 | async-start | bytes 262144 | tf_op jit(solution)/shard_map/all_to_all | solution.py:710
  34.7 0.7 %copy-start.5 = (s32[1,3]{1,0:T(1,128)S(1)}, s32[1,3]{1,0:T(1,128)}, u32[]{:S(2)}) copy-start(s32[1,3]{1,0:T(1,128)} %len_ref.1) | copy-start | bytes 40
  34.7 0.7 %copy-start.6 = (f32[128]{0:T(128)S(1)}, f32[128]{0:T(128)}, u32[]{:S(2)}) copy-start(f32[128]{0:T(128)} %param.22) | copy-start | bytes 1540
  34.7 0.7 %copy-start.7 = (f32[1,128]{1,0:T(1,128)S(1)}, f32[1,128]{1,0:T(1,128)}, u32[]{:S(2)}) copy-start(f32[1,128]{1,0:T(1,128)} %constant.2.clone.freq_hbm.freq_ref) | copy-start | bytes 1540

commit v4 on v3

--- a/solution.py
+++ b/solution.py
@@ -204,7 +204,7 @@
 f32 = jnp.float32
 bf16 = jnp.bfloat16
 lanes = 128
-pay_rows = 32
+pay_rows = 28
 back_rows = 16
 
 
@@ -347,19 +347,21 @@
     mixed = (mixed + self_weight * row_v[...]) * jax.nn.sigmoid(row_g[...])
     total_row = jnp.sum(jnp.where(row == col, totals, 0.0), axis=0, keepdims=True)
     high = total_row.astype(bf16).astype(f32)
-    pay[...] = jnp.zeros_like(pay)
+    rest = pltpu.roll(jnp.broadcast_to(total_row - high, (8, lanes)), lanes // 2, 1)
     pay[0:rows, :] = mixed
-    pay[rows + rpg : rows + rpg + 1, :] = high
-    pay[rows + rpg + 1 : rows + rpg + 2, :] = total_row - high
+    pay[rows + rpg : rows + rpg + 1, :] = jnp.where(
+        iota((1, lanes), 1) < lanes // 2, high, rest[0:1, :]
+    )
     peers = pay_ref.shape[0]
     tps = lax.axis_size("tp")
     slices = resid_ref.shape[1] // (tps * lanes)
     for z in range(slices):
         at = pl.ds(pl.multiple_of((z * tps + tp) * lanes, lanes), lanes)
         pay[rows : rows + rpg, :] = resid_ref[:, at].astype(f32)
-        out = pay[...].astype(bf16)
-        for peer in range(z * peers // slices, (z + 1) * peers // slices):
-            pay_ref[peer] = out
+        for g in range(pay_ref.shape[1]):
+            out = pay[4 * g : 4 * g + 4, :].astype(bf16)
+            for peer in range(z * peers // slices, (z + 1) * peers // slices):
+                pay_ref[peer, g] = out
     for copy in copies[11:]:
         copy.wait()
 
@@ -408,21 +410,24 @@
     rpg = toks // groups
     rows = heads * rpg
     diag = iota((rows, lanes), 0) == iota((rows, lanes), 1)
+    quads = pay_ref.shape[1]
     for r in range(groups):
-        total = jnp.zeros(acc.shape, f32)
-        for t in range(tps):
-            piece = pay_ref[r * tps + t].astype(f32)
-            total = total + piece
-            acc[...] = piece
-            hid[r * rpg : (r + 1) * rpg, t * lanes : (t + 1) * lanes] = acc[rows : rows + rpg, :]
-        acc[...] = total
-        total_row = acc[rows + rpg : rows + rpg + 1, :] + acc[rows + rpg + 1 : rows + rpg + 2, :]
-        totals = jnp.sum(
-            jnp.where(diag, jnp.broadcast_to(total_row, (rows, lanes)), 0.0), axis=-1, keepdims=True
-        )
-        acc[0:rows, :] = acc[0:rows, :] / totals
+        for g in range(quads):
+            total = jnp.zeros((4, lanes), f32)
+            for t in range(tps):
+                piece = pay_ref[r * tps + t, g].astype(f32)
+                total = total + piece
+                if g == quads - 1:
+                    hid[r * rpg : (r + 1) * rpg, t * lanes : (t + 1) * lanes] = piece[:rpg, :]
+            acc[r, 4 * g : 4 * g + 4, :] = total
+    for r in range(groups):
+        total_row = jnp.broadcast_to(acc[r, pay_rows - 1 : pay_rows, :], (rows, lanes))
+        total_row = total_row + pltpu.roll(total_row, lanes // 2, 1)
+        totals = jnp.sum(jnp.where(diag, total_row, 0.0), axis=-1, keepdims=True)
+        acc[r, 0:rows, :] = acc[r, 0:rows, :] / totals
+    for r in range(groups):
         for h in range(heads):
-            att[h, r * rpg : (r + 1) * rpg, :] = acc[h * rpg : (h + 1) * rpg, :]
+            att[h, r * rpg : (r + 1) * rpg, :] = acc[r, h * rpg : (h + 1) * rpg, :]
     state = hid[...]
     per = heads // tps
     for d, w_ref in enumerate((w0_ref, w1_ref, w2_ref, w3_ref)):
@@ -634,7 +639,7 @@
         partial_kernel,
         (
             jax.ShapeDtypeStruct((tok, 2 * k_pre.shape[1]), bf16),
-            jax.ShapeDtypeStruct((peers, pay_rows, lanes), bf16),
+            jax.ShapeDtypeStruct((peers, pay_rows // 4, 4, lanes), bf16),
             jax.ShapeDtypeStruct((w_out.shape[0], part), bf16),
             jax.ShapeDtypeStruct((w_gate.shape[0], 2 * units), bf16),
             jax.ShapeDtypeStruct((units, w_down.shape[1]), bf16),
@@ -686,7 +691,7 @@
             (heads, toks, lanes),
             (toks, part),
             (2, toks, part // 2),
-            (pay_rows, lanes),
+            (reqs, pay_rows, lanes),
         ],
         flops=10**7,
     )

time: 43.9 us -> 43.2 us (0.984)
  waiting for transfers between devices: 13.2 us -> 12.4 us
    all_to_all x1, waiting for transfers between devices: 5.27 us -> 4.49 us  [local(): got = lax.all_to_all(pay, ('req', 'tp'), 0, 0, tiled=True)]
where the time goes in v4:
time: 43.2 us; the launch traced here: 42.9 us
  starting transfers between devices  19.4 us (45%)
  waiting for transfers between devices  12.4 us (29%)
  Pallas kernels  8.9 us (21%)
  local copies, waits for them, and re-layouts  1.41 us (3%)
  between operations  0.82 us (2%)
    pallas_call x7, Pallas kernels, call(): pl.pallas_call(body, out_shape=out_shape, in_specs=specs, out_specs=jax.t...  8.89 us
    all_to_all x1, waiting for transfers between devices, local(): got = lax.all_to_all(pay, ('req', 'tp'), 0, 0, tiled=True)  4.49 us
    ppermute x3, starting transfers between devices, along(): return lax.ppermute(array, 'req', [(i, i ^ 2 * by) for i in range(reqs)])  4.45 us
    ppermute x2, starting transfers between devices, swap(): return lax.ppermute(array, 'req', [(i, i ^ 1) for i in range(reqs)])  4.34 us
    all_to_all x1, waiting for transfers between devices, local(): returned = lax.all_to_all(back, ('req', 'tp'), 0, 0, tiled=True)  4.21 us
    all_to_all x1, starting transfers between devices, local(): got = lax.all_to_all(pay, ('req', 'tp'), 0, 0, tiled=True)  3.97 us
    ppermute x6, starting transfers between devices, cross(): return lax.ppermute(array, 'tp', [(i, i ^ by) for i in range(tps)])  3.78 us
    all_to_all x1, starting transfers between devices, local(): returned = lax.all_to_all(back, ('req', 'tp'), 0, 0, tiled=True)  2.89 us
  transfers between devices with their start and end apart: 13, of which 5 were waited for; matrix products, arithmetic and copies ran while one was open for 0% of the time, Pallas kernels for 12%

profile of v4, /device:TPU:0, one launch (start us, length us, event | category | flops | bytes accessed | tf_op | source)
XLA Modules:
  0.0 42.9 jit_solution(10087988383681100073)
XLA Ops:
  0.6 3.1 %shard_map.185 = (bf16[128,1024]{1,0:T(8,128)(2,1)}, bf16[32,7,4,128]{3,2,1,0:T(4,128)(2,1)}, bf16[256,512]{1,0:T(8,128)(2,1)}, bf16[256,768]{1,0:T(8,128)(2,1)}, bf16[384,256]{1,0:T(8,128)(2,1)}) custom-call(s32[1,3]{1,0:T(1,128)} %len_ref.1, bf16[128,512]{1,0:T(8,128)(2,1)} %k_hbm.1, bf16[128,512]{1,0:T(8,128)(2,1)} %v_hbm.1, bf16[3,1024]{1,0:T(4,128)(2,1)} %qn_hbm.1, ...), custom_call_target="tpu_custom_call" | custom-call | flops 10000000 | bytes 2516540 | tf_op jit(solution)/shard_map/pallas_call | solution.py:563
  3.7 0.0 copy-start.11
  3.7 3.0 %collective-permute-start.3 = (bf16[256,768]{1,0:T(8,128)(2,1)}, bf16[256,768]{1,0:T(8,128)(2,1)S(1)}, u32[]{:S(2)}, u32[]{:S(2)}) collective-permute-start(bf16[256,768]{1,0:T(8,128)(2,1)} %get-tuple-element.20), channel_id=1, source_target_pairs={{0,4},{4,0},{8,12},{12,8},{16,20},{20,16},{24,28},{28,24},{1,5},{5... | collective-permute-start | bytes 1179656 | tf_op jit(solution)/shard_map/ppermute | solution.py:629
  6.8 1.5 %collective-permute-start.1 = (bf16[256,512]{1,0:T(8,128)(2,1)}, bf16[256,512]{1,0:T(8,128)(2,1)S(1)}, u32[]{:S(2)}, u32[]{:S(2)}) collective-permute-start(bf16[256,512]{1,0:T(8,128)(2,1)} %get-tuple-element.17), channel_id=1, source_target_pairs={{0,2},{1,3},{2,0},{3,1},{4,6},{5,7},{6,4},{7,5},{8,10},{9,11},{10,... | collective-permute-start | bytes 786440 | tf_op jit(solution)/shard_map/ppermute | solution.py:626
  8.3 4.0 %all-to-all-start = ((bf16[32,7,4,128]{3,2,1,0:T(4,128)(2,1)}), bf16[32,7,4,128]{3,2,1,0:T(4,128)(2,1)S(1)}, u32[]{:S(2)}, u32[]{:S(2)}) async-start(bf16[32,7,4,128]{3,2,1,0:T(4,128)(2,1)} %get-tuple-element.16), calls=%async_computation | async-start | bytes 458752 | tf_op jit(solution)/shard_map/all_to_all | solution.py:680
  12.2 0.0 copy-done.11
  12.3 0.0 copy-start.1
  12.3 0.0 copy-start.2
  12.3 0.0 copy-start.4
  12.3 0.3 collective-permute-start
  12.6 0.0 copy-done
  12.6 0.6 %copy-done.1 = bf16[256,768]{1,0:T(8,128)(2,1)S(1)} copy-done((bf16[256,768]{1,0:T(8,128)(2,1)S(1)}, bf16[256,768]{1,0:T(8,128)(2,1)}, u32[]{:S(2)}) %copy-start.1) | copy-done | bytes 393240
  13.3 0.1 copy-done.2
  13.4 0.0 copy-done.4
  13.4 0.1 shard_map.187
  13.5 1.3 %collective-permute-done.1.w2_ref = bf16[256,512]{1,0:T(8,128)(2,1)S(1)} collective-permute-done((bf16[256,512]{1,0:T(8,128)(2,1)}, bf16[256,512]{1,0:T(8,128)(2,1)S(1)}, u32[]{:S(2)}, u32[]{:S(2)}) %collective-permute-start.1) | collective-permute-done | bytes 262176 | tf_op jit(solution)/shard_map/ppermute | solution.py:626
  14.8 0.0 collective-permute-start.2
  14.8 1.3 %collective-permute-start.7 = (bf16[384,256]{1,0:T(8,128)(2,1)S(1)}, bf16[384,256]{1,0:T(8,128)(2,1)S(1)}, u32[]{:S(2)}, u32[]{:S(2)}) collective-permute-start(bf16[384,256]{1,0:T(8,128)(2,1)S(1)} %copy-done.12), channel_id=1, source_target_pairs={{0,4},{4,0},{8,12},{12,8},{16,20},{20,16},{24,28},{28,24},{1,5},{5... | collective-permute-start | bytes 589832 | tf_op jit(solution)/shard_map/ppermute | solution.py:629
  16.1 1.5 %collective-permute-start.9 = (bf16[128,1024]{1,0:T(8,128)(2,1)S(1)}, bf16[128,1024]{1,0:T(8,128)(2,1)S(1)}, u32[]{:S(2)}, u32[]{:S(2)}) collective-permute-start(bf16[128,1024]{1,0:T(8,128)(2,1)S(1)} %copy-done.9), channel_id=1, source_target_pairs={{0,2},{1,3},{2,0},{3,1},{4,6},{5,7},{6,4},{7,5},{8,10},{9,11},{10,... | collective-permute-start | bytes 786440 | tf_op jit(solution)/shard_map/ppermute | solution.py:626
  17.5 0.0 collective-permute-done.3.refs_0_.pair_ref
  17.5 0.0 collective-permute-done.refs_1_.w1_ref
  17.6 0.0 collective-permute-done.2.refs_2_.w3_ref
  17.6 4.5 %all-to-all-done.pay_ref = bf16[32,7,4,128]{3,2,1,0:T(4,128)(2,1)S(1)} async-done(((bf16[32,7,4,128]{3,2,1,0:T(4,128)(2,1)}), bf16[32,7,4,128]{3,2,1,0:T(4,128)(2,1)S(1)}, u32[]{:S(2)}, u32[]{:S(2)}) %all-to-all-start) | async-done | bytes 229408 | tf_op jit(solution)/shard_map/all_to_all | solution.py:680
  22.1 0.7 %shard_map.190 = (f32[24,512]{1,0:T(8,128)S(1)}, bf16[24,896]{1,0:T(8,128)(2,1)S(1)}) custom-call(bf16[32,7,4,128]{3,2,1,0:T(4,128)(2,1)S(1)} %all-to-all-done.pay_ref, bf16[256,512]{1,0:T(8,128)(2,1)S(1)} %shard_map.186.w0_ref, bf16[256,512]{1,0:T(8,128)(2,1)S(1)} %collective-permute-done.refs_1_.w1_ref, ...), custom_call_target="tpu_custom_call" | custom-call | flops 10000000 | bytes 2070528 | tf_op jit(solution)/shard_map/pallas_call | solution.py:563
  22.7 1.6 %collective-permute-start.4 = (bf16[24,896]{1,0:T(8,128)(2,1)S(1)}, bf16[24,896]{1,0:T(8,128)(2,1)S(1)}, u32[]{:S(2)}, u32[]{:S(2)}) collective-permute-start(bf16[24,896]{1,0:T(8,128)(2,1)S(1)} %get-tuple-element.22.m0_ref), channel_id=1, source_target_pairs={{0,24},{4,28},{8,16},{12,20},{16,8},{20,12},{24,0},{28,4},{1,25},{... | collective-permute-start | bytes 129032 | tf_op jit(solution)/shard_map/ppermute | solution.py:632
  24.3 1.0 %collective-permute-start.5 = (bf16[24,896]{1,0:T(8,128)(2,1)S(1)}, bf16[24,896]{1,0:T(8,128)(2,1)S(1)}, u32[]{:S(2)}, u32[]{:S(2)}) collective-permute-start(bf16[24,896]{1,0:T(8,128)(2,1)S(1)} %get-tuple-element.22.m0_ref), channel_id=1, source_target_pairs={{0,16},{4,20},{8,24},{12,28},{16,0},{20,4},{24,8},{28,12},{1,17},{... | collective-permute-start | bytes 129032 | tf_op jit(solution)/shard_map/ppermute | solution.py:632
  25.3 1.9 %collective-permute-start.6 = (bf16[24,896]{1,0:T(8,128)(2,1)S(1)}, bf16[24,896]{1,0:T(8,128)(2,1)S(1)}, u32[]{:S(2)}, u32[]{:S(2)}) collective-permute-start(bf16[24,896]{1,0:T(8,128)(2,1)S(1)} %get-tuple-element.22.m0_ref), channel_id=1, source_target_pairs={{0,8},{4,12},{8,0},{12,4},{16,24},{20,28},{24,16},{28,20},{1,9},{5... | collective-permute-start | bytes 129032 | tf_op jit(solution)/shard_map/ppermute | solution.py:632
  27.2 0.0 collective-permute-done.7.pair_ref
  27.2 0.0 collective-permute-start.8
  27.2 0.0 collective-permute-done.9.kv2_ref
  27.2 0.5 %collective-permute-start.10 = (bf16[128,1024]{1,0:T(8,128)(2,1)S(1)}, bf16[128,1024]{1,0:T(8,128)(2,1)S(1)}, u32[]{:S(2)}, u32[]{:S(2)}) collective-permute-start(bf16[128,1024]{1,0:T(8,128)(2,1)S(1)} %collective-permute-done.9.kv2_ref), channel_id=1, source_target_pairs={{0,1},{1,0},{2,3},{3,2},{4,5},{5,4},{6,7},{7,6},{8,9},{9,8},{10,11... | collective-permute-start | bytes 786440 | tf_op jit(solution)/shard_map/ppermute | solution.py:626
  27.7 1.4 %collective-permute-done.4.m1_ref = bf16[24,896]{1,0:T(8,128)(2,1)S(1)} collective-permute-done((bf16[24,896]{1,0:T(8,128)(2,1)S(1)}, bf16[24,896]{1,0:T(8,128)(2,1)S(1)}, u32[]{:S(2)}, u32[]{:S(2)}) %collective-permute-start.4) | collective-permute-done | bytes 43040 | tf_op jit(solution)/shard_map/ppermute | solution.py:632
  29.1 0.9 %collective-permute-done.5.m2_ref = bf16[24,896]{1,0:T(8,128)(2,1)S(1)} collective-permute-done((bf16[24,896]{1,0:T(8,128)(2,1)S(1)}, bf16[24,896]{1,0:T(8,128)(2,1)S(1)}, u32[]{:S(2)}, u32[]{:S(2)}) %collective-permute-start.5) | collective-permute-done | bytes 43040 | tf_op jit(solution)/shard_map/ppermute | solution.py:632
  30.1 0.0 collective-permute-done.6.m3_ref
  30.1 1.0 %shard_map.191 = bf16[32,16,128]{2,1,0:T(8,128)(2,1)} custom-call(bf16[24,896]{1,0:T(8,128)(2,1)S(1)} %get-tuple-element.22.m0_ref, bf16[24,896]{1,0:T(8,128)(2,1)S(1)} %collective-permute-done.4.m1_ref, bf16[24,896]{1,0:T(8,128)(2,1)S(1)} %collective-permute-done.5.m2_ref, bf16[24,896]{1,0:T(8,128)(2,1)S(1)} %collective-permute-done.6.m3_ref, ...), custom_call_target="tpu_custom_call" | custom-call | flops 3000000000 | bytes 811008 | tf_op jit(solution)/shard_map/pallas_call | solution.py:563
  31.1 2.9 %all-to-all-start.1 = ((bf16[32,16,128]{2,1,0:T(8,128)(2,1)}), bf16[32,16,128]{2,1,0:T(8,128)(2,1)S(1)}, u32[]{:S(2)}, u32[]{:S(2)}) async-start(bf16[32,16,128]{2,1,0:T(8,128)(2,1)} %shard_map.191), calls=%async_computation.1 | async-start | bytes 262144 | tf_op jit(solution)/shard_map/all_to_all | solution.py:715
  34.0 0.0 copy-start.5
  34.0 0.0 copy-start.6
  34.0 0.0 copy-start.7
  34.0 0.1 copy.20.g_ref
  34.1 0.0 collective-permute-done.8.kv1_ref
  34.1 0.0 collective-permute-done.10.kv3_ref
  34.2 0.5 %copy-done.5 = s32[1,3]{1,0:T(1,128)S(1)} copy-done((s32[1,3]{1,0:T(1,128)S(1)}, s32[1,3]{1,0:T(1,128)}, u32[]{:S(2)}) %copy-start.5) | copy-done | bytes 36
  34.6 0.0 copy-done.6
  34.7 0.0 copy-done.7
  34.7 3.3 %shard_map.192 = bf16[128,1024]{1,0:T(8,128)(2,1)} custom-call(s32[1,3]{1,0:T(1,128)S(1)} %copy-done.5, bf16[128,1024]{1,0:T(8,128)(2,1)S(1)} %copy-done.8, bf16[128,8]{1,0:T(8,128)(2,1)S(1)} %copy.20.g_ref, bf16[128,1024]{1,0:T(8,128)(2,1)S(1)} %copy-done.9, bf16[128,1024]{1,0:T(8,128)(2,1)S(1)} %collective-permute-done.8.kv1_ref, ...), custom_call_target="tpu_custom_call" | custom-call | flops 1000000000 | bytes 1313804 | tf_op jit(solution)/shard_map/pallas_call | solution.py:563
  38.0 4.2 %all-to-all-done.1.back_ref = bf16[32,16,128]{2,1,0:T(8,128)(2,1)S(1)} async-done(((bf16[32,16,128]{2,1,0:T(8,128)(2,1)}), bf16[32,16,128]{2,1,0:T(8,128)(2,1)S(1)}, u32[]{:S(2)}, u32[]{:S(2)}) %all-to-all-start.1) | async-done | bytes 131104 | tf_op jit(solution)/shard_map/all_to_all | solution.py:715
  42.2 0.7 %shard_map.193 = bf16[3,2048]{1,0:T(4,128)(2,1)} custom-call(bf16[32,16,128]{2,1,0:T(8,128)(2,1)S(1)} %all-to-all-done.1.back_ref), custom_call_target="tpu_custom_call" | custom-call | flops 1000000 | bytes 131072 | tf_op jit(solution)/shard_map/pallas_call | solution.py:563
  (14 shorter events, 0.1 us)
Async XLA Ops:
  0.6 12.0 %copy-start = (bf16[256,2048]{1,0:T(8,128)(2,1)S(1)}, bf16[256,2048]{1,0:T(8,128)(2,1)}, u32[]{:S(2)}) copy-start(bf16[256,2048]{1,0:T(8,128)(2,1)} %w_hbm.3) | copy-start | bytes 3145732
  3.7 8.5 %copy-start.11 = (bf16[256,512]{1,0:T(8,128)(2,1)S(1)}, bf16[256,512]{1,0:T(8,128)(2,1)}, u32[]{:S(2)}) copy-start(bf16[256,512]{1,0:T(8,128)(2,1)} %get-tuple-element.17) | copy-start | bytes 786436
  3.7 13.8 %collective-permute-start.3 = (bf16[256,768]{1,0:T(8,128)(2,1)}, bf16[256,768]{1,0:T(8,128)(2,1)S(1)}, u32[]{:S(2)}, u32[]{:S(2)}) collective-permute-start(bf16[256,768]{1,0:T(8,128)(2,1)} %get-tuple-element.20), channel_id=1, source_target_pairs={{0,4},{4,0},{8,12},{12,8},{16,20},{20,16},{24,28},{28,24},{1,5},{5... | collective-permute-start | bytes 1179656 | tf_op jit(solution)/shard_map/ppermute | solution.py:629
  6.8 8.0 %collective-permute-start.1 = (bf16[256,512]{1,0:T(8,128)(2,1)}, bf16[256,512]{1,0:T(8,128)(2,1)S(1)}, u32[]{:S(2)}, u32[]{:S(2)}) collective-permute-start(bf16[256,512]{1,0:T(8,128)(2,1)} %get-tuple-element.17), channel_id=1, source_target_pairs={{0,2},{1,3},{2,0},{3,1},{4,6},{5,7},{6,4},{7,5},{8,10},{9,11},{10,... | collective-permute-start | bytes 786440 | tf_op jit(solution)/shard_map/ppermute | solution.py:626
  8.3 13.8 %all-to-all-start = ((bf16[32,7,4,128]{3,2,1,0:T(4,128)(2,1)}), bf16[32,7,4,128]{3,2,1,0:T(4,128)(2,1)S(1)}, u32[]{:S(2)}, u32[]{:S(2)}) async-start(bf16[32,7,4,128]{3,2,1,0:T(4,128)(2,1)} %get-tuple-element.16), calls=%async_computation | async-start | bytes 458752 | tf_op jit(solution)/shard_map/all_to_all | solution.py:680
  12.3 1.0 %copy-start.1 = (bf16[256,768]{1,0:T(8,128)(2,1)S(1)}, bf16[256,768]{1,0:T(8,128)(2,1)}, u32[]{:S(2)}) copy-start(bf16[256,768]{1,0:T(8,128)(2,1)} %gate_hbm.3) | copy-start | bytes 1179652
  12.3 1.1 %copy-start.2 = (bf16[256,768]{1,0:T(8,128)(2,1)S(1)}, bf16[256,768]{1,0:T(8,128)(2,1)}, u32[]{:S(2)}) copy-start(bf16[256,768]{1,0:T(8,128)(2,1)} %up_hbm.3) | copy-start | bytes 1179652
  12.3 1.1 %copy-start.4 = (f32[2048]{0:T(1024)S(1)}, f32[2048]{0:T(1024)}, u32[]{:S(2)}) copy-start(f32[2048]{0:T(1024)} %param.31) | copy-start | bytes 24580
  12.3 5.3 %collective-permute-start = (bf16[256,512]{1,0:T(8,128)(2,1)S(1)}, bf16[256,512]{1,0:T(8,128)(2,1)S(1)}, u32[]{:S(2)}, u32[]{:S(2)}) collective-permute-start(bf16[256,512]{1,0:T(8,128)(2,1)S(1)} %copy-done.11), channel_id=1, source_target_pairs={{0,1},{1,0},{2,3},{3,2},{4,5},{5,4},{6,7},{7,6},{8,9},{9,8},{10,11... | collective-permute-start | bytes 786440 | tf_op jit(solution)/shard_map/ppermute | solution.py:626
  13.4 1.4 %copy-start.12 = (bf16[384,256]{1,0:T(8,128)(2,1)S(1)}, bf16[384,256]{1,0:T(8,128)(2,1)}, u32[]{:S(2)}) copy-start(bf16[384,256]{1,0:T(8,128)(2,1)} %get-tuple-element.25) | copy-start | bytes 589828
  13.4 2.7 %copy-start.9 = (bf16[128,1024]{1,0:T(8,128)(2,1)S(1)}, bf16[128,1024]{1,0:T(8,128)(2,1)}, u32[]{:S(2)}) copy-start(bf16[128,1024]{1,0:T(8,128)(2,1)} %get-tuple-element.27.kv0_ref) | copy-start | bytes 786436
  14.8 2.8 %collective-permute-start.2 = (bf16[256,512]{1,0:T(8,128)(2,1)S(1)}, bf16[256,512]{1,0:T(8,128)(2,1)S(1)}, u32[]{:S(2)}, u32[]{:S(2)}) collective-permute-start(bf16[256,512]{1,0:T(8,128)(2,1)S(1)} %collective-permute-done.1.w2_ref), channel_id=1, source_target_pairs={{0,1},{1,0},{2,3},{3,2},{4,5},{5,4},{6,7},{7,6},{8,9},{9,8},{10,11... | collective-permute-start | bytes 786440 | tf_op jit(solution)/shard_map/ppermute | solution.py:626
  14.8 12.4 %collective-permute-start.7 = (bf16[384,256]{1,0:T(8,128)(2,1)S(1)}, bf16[384,256]{1,0:T(8,128)(2,1)S(1)}, u32[]{:S(2)}, u32[]{:S(2)}) collective-permute-start(bf16[384,256]{1,0:T(8,128)(2,1)S(1)} %copy-done.12), channel_id=1, source_target_pairs={{0,4},{4,0},{8,12},{12,8},{16,20},{20,16},{24,28},{28,24},{1,5},{5... | collective-permute-start | bytes 589832 | tf_op jit(solution)/shard_map/ppermute | solution.py:629
  16.1 11.1 %collective-permute-start.9 = (bf16[128,1024]{1,0:T(8,128)(2,1)S(1)}, bf16[128,1024]{1,0:T(8,128)(2,1)S(1)}, u32[]{:S(2)}, u32[]{:S(2)}) collective-permute-start(bf16[128,1024]{1,0:T(8,128)(2,1)S(1)} %copy-done.9), channel_id=1, source_target_pairs={{0,2},{1,3},{2,0},{3,1},{4,6},{5,7},{6,4},{7,5},{8,10},{9,11},{10,... | collective-permute-start | bytes 786440 | tf_op jit(solution)/shard_map/ppermute | solution.py:626
  22.1 8.0 %copy-start.3 = (bf16[768,256]{1,0:T(8,128)(2,1)S(1)}, bf16[768,256]{1,0:T(8,128)(2,1)}, u32[]{:S(2)}) copy-start(bf16[768,256]{1,0:T(8,128)(2,1)} %down_ref.1) | copy-start | bytes 1179652
  22.7 6.4 %collective-permute-start.4 = (bf16[24,896]{1,0:T(8,128)(2,1)S(1)}, bf16[24,896]{1,0:T(8,128)(2,1)S(1)}, u32[]{:S(2)}, u32[]{:S(2)}) collective-permute-start(bf16[24,896]{1,0:T(8,128)(2,1)S(1)} %get-tuple-element.22.m0_ref), channel_id=1, source_target_pairs={{0,24},{4,28},{8,16},{12,20},{16,8},{20,12},{24,0},{28,4},{1,25},{... | collective-permute-start | bytes 129032 | tf_op jit(solution)/shard_map/ppermute | solution.py:632
  24.3 5.7 %collective-permute-start.5 = (bf16[24,896]{1,0:T(8,128)(2,1)S(1)}, bf16[24,896]{1,0:T(8,128)(2,1)S(1)}, u32[]{:S(2)}, u32[]{:S(2)}) collective-permute-start(bf16[24,896]{1,0:T(8,128)(2,1)S(1)} %get-tuple-element.22.m0_ref), channel_id=1, source_target_pairs={{0,16},{4,20},{8,24},{12,28},{16,0},{20,4},{24,8},{28,12},{1,17},{... | collective-permute-start | bytes 129032 | tf_op jit(solution)/shard_map/ppermute | solution.py:632
  25.3 4.8 %collective-permute-start.6 = (bf16[24,896]{1,0:T(8,128)(2,1)S(1)}, bf16[24,896]{1,0:T(8,128)(2,1)S(1)}, u32[]{:S(2)}, u32[]{:S(2)}) collective-permute-start(bf16[24,896]{1,0:T(8,128)(2,1)S(1)} %get-tuple-element.22.m0_ref), channel_id=1, source_target_pairs={{0,8},{4,12},{8,0},{12,4},{16,24},{20,28},{24,16},{28,20},{1,9},{5... | collective-permute-start | bytes 129032 | tf_op jit(solution)/shard_map/ppermute | solution.py:632
  27.2 6.9 %collective-permute-start.8 = (bf16[128,1024]{1,0:T(8,128)(2,1)S(1)}, bf16[128,1024]{1,0:T(8,128)(2,1)S(1)}, u32[]{:S(2)}, u32[]{:S(2)}) collective-permute-start(bf16[128,1024]{1,0:T(8,128)(2,1)S(1)} %copy-done.9), channel_id=1, source_target_pairs={{0,1},{1,0},{2,3},{3,2},{4,5},{5,4},{6,7},{7,6},{8,9},{9,8},{10,11... | collective-permute-start | bytes 786440 | tf_op jit(solution)/shard_map/ppermute | solution.py:626
  27.2 6.9 %collective-permute-start.10 = (bf16[128,1024]{1,0:T(8,128)(2,1)S(1)}, bf16[128,1024]{1,0:T(8,128)(2,1)S(1)}, u32[]{:S(2)}, u32[]{:S(2)}) collective-permute-start(bf16[128,1024]{1,0:T(8,128)(2,1)S(1)} %collective-permute-done.9.kv2_ref), channel_id=1, source_target_pairs={{0,1},{1,0},{2,3},{3,2},{4,5},{5,4},{6,7},{7,6},{8,9},{9,8},{10,11... | collective-permute-start | bytes 786440 | tf_op jit(solution)/shard_map/ppermute | solution.py:626
  30.1 3.9 %copy-start.10 = (bf16[128,8]{0,1:T(8,128)(2,1)S(1)}, bf16[128,8]{0,1:T(8,128)(2,1)}, u32[]{:S(2)}) copy-start(bf16[128,8]{0,1:T(8,128)(2,1)} %param.19) | copy-start | bytes 6148
  31.1 3.1 %copy-start.8 = (bf16[128,1024]{1,0:T(8,128)(2,1)S(1)}, bf16[128,1024]{1,0:T(8,128)(2,1)}, u32[]{:S(2)}) copy-start(bf16[128,1024]{1,0:T(8,128)(2,1)} %q_ref.1) | copy-start | bytes 786436
  31.1 11.1 %all-to-all-start.1 = ((bf16[32,16,128]{2,1,0:T(8,128)(2,1)}), bf16[32,16,128]{2,1,0:T(8,128)(2,1)S(1)}, u32[]{:S(2)}, u32[]{:S(2)}) async-start(bf16[32,16,128]{2,1,0:T(8,128)(2,1)} %shard_map.191), calls=%async_computation.1 | async-start | bytes 262144 | tf_op jit(solution)/shard_map/all_to_all | solution.py:715
  34.0 0.7 %copy-start.5 = (s32[1,3]{1,0:T(1,128)S(1)}, s32[1,3]{1,0:T(1,128)}, u32[]{:S(2)}) copy-start(s32[1,3]{1,0:T(1,128)} %len_ref.1) | copy-start | bytes 40
  34.0 0.7 %copy-start.6 = (f32[128]{0:T(128)S(1)}, f32[128]{0:T(128)}, u32[]{:S(2)}) copy-start(f32[128]{0:T(128)} %param.22) | copy-start | bytes 1540
  34.0 0.7 %copy-start.7 = (f32[1,128]{1,0:T(1,128)S(1)}, f32[1,128]{1,0:T(1,128)}, u32[]{:S(2)}) copy-start(f32[1,128]{1,0:T(1,128)} %constant.2.clone.freq_hbm.freq_ref) | copy-start | bytes 1540

commit v5 on v4

--- a/solution.py
+++ b/solution.py
@@ -258,8 +258,9 @@
 def partial_kernel(
     len_hbm, k_hbm, v_hbm, qn_hbm, kn_hbm, vn_hbm, gn_hbm, resid_hbm, qg_hbm, kg_hbm, freq_hbm,
     w_hbm, gate_hbm, up_hbm, down_hbm,
+    kv_hbm, pay_hbm, own_hbm, pair_hbm, down_pair_hbm,
     kv_ref, pay_ref, own_ref, pair_ref, down_pair_ref, row_q, row_k, row_v, row_g, pay, len_ref, k_ref, v_ref, qn_ref, kn_ref, vn_ref, gn_ref,
-    resid_ref, qg_ref, kg_ref, freq_ref, sems,
+    resid_ref, qg_ref, kg_ref, freq_ref, sems, out_sems,
 ):
     tp = lax.axis_index("tp")
     req = lax.axis_index("req")
@@ -280,6 +281,11 @@
     copies = [pltpu.make_async_copy(a, b, sems.at[i]) for i, (a, b) in enumerate(moves)]
     for copy in copies:
         copy.start()
+    ends = (
+        (pair_ref, pair_hbm), (own_ref, own_hbm), (down_pair_ref, down_pair_hbm),
+        (kv_ref, kv_hbm), (pay_ref, pay_hbm),
+    )
+    leave = [pltpu.make_async_copy(a, b, out_sems.at[i]) for i, (a, b) in enumerate(ends)]
     tok = k_ref.shape[0]
     rpg = qn_ref.shape[0]
     heads = qn_ref.shape[1] // lanes
@@ -300,6 +306,10 @@
         keys.append(norm_rope(k_ref[:, at].astype(f32), kg, factors))
         kv_ref[:, at] = keys[-1]
     kv_ref[:, kvs * lanes :] = v_ref[...]
+    for copy in copies[11:]:
+        copy.wait()
+    for copy in leave[:4]:
+        copy.start()
     qn, kn = qn_ref[...].astype(f32), kn_ref[...].astype(f32)
     vn, gn = vn_ref[...].astype(f32), gn_ref[...].astype(f32)
     for h in range(heads):
@@ -362,7 +372,8 @@
             out = pay[4 * g : 4 * g + 4, :].astype(bf16)
             for peer in range(z * peers // slices, (z + 1) * peers // slices):
                 pay_ref[peer, g] = out
-    for copy in copies[11:]:
+    leave[4].start()
+    for copy in leave:
         copy.wait()
 
 
@@ -399,7 +410,7 @@
 
 def hidden_kernel(
     pay_ref, w0_ref, w1_ref, w2_ref, w3_ref, mine_ref, pair_ref, ng_ref, _,
-    hid_ref, msg_ref, att, hid, xs, acc,
+    hid_ref, msg_ref, att, hid, xs, acc, out,
 ):
     tp = lax.axis_index("tp")
     req = lax.axis_index("req")
@@ -447,16 +458,23 @@
     units = pair_ref.shape[1] // 2
     gate = dot(own, mine_ref[:, :units]) + dot(other, pair_ref[:, :units])
     up = dot(own, mine_ref[:, units:]) + dot(other, pair_ref[:, units:])
-    high = sums.astype(bf16).astype(f32)
-    lane = iota((toks, lanes), 1)
-    msg_ref[:, :units] = gate.astype(bf16)
-    msg_ref[:, units : 2 * units] = up.astype(bf16)
-    msg_ref[:, 2 * units :] = jnp.where(
-        lane == 0, high, jnp.where(lane == 1, sums - high, 0.0)
-    ).astype(bf16)
-
-
-def down_kernel(m0_ref, m1_ref, m2_ref, m3_ref, hid_ref, down_ref, pair_ref, back_ref, part, pay):
+    square = iota((toks, lanes), 0) == iota((toks, lanes), 1)
+    sums_row = jnp.sum(jnp.where(square, sums, 0.0), axis=0, keepdims=True)
+    high = sums_row.astype(bf16).astype(f32)
+    blocks = units // lanes
+    for i in range(blocks):
+        at = slice(i * lanes, (i + 1) * lanes)
+        out[i * toks : (i + 1) * toks, :] = gate[:, at]
+        out[(blocks + i) * toks : (blocks + i + 1) * toks, :] = up[:, at]
+    base = 2 * blocks * toks
+    first = iota((8, lanes), 0)
+    out[base : base + 8, :] = jnp.where(
+        first == 0, high, jnp.where(first == 1, sums_row - high, 0.0)
+    )
+    msg_ref[...] = out[...].astype(bf16)
+
+
+def down_kernel(m0_ref, m1_ref, m2_ref, m3_ref, hid_ref, down_ref, pair_ref, back_ref, part, pay, whole):
     tp = lax.axis_index("tp")
     tps = lax.axis_size("tp")
     y = lax.rem(lax.axis_index("req"), 2)
@@ -465,10 +483,21 @@
     total = m0_ref[...].astype(f32)
     for m_ref in (m1_ref, m2_ref, m3_ref):
         total = total + m_ref[...].astype(f32)
-    sums = total[:, 2 * units : 2 * units + 1] + total[:, 2 * units + 1 : 2 * units + 2]
+    whole[...] = total
+    blocks = units // lanes
+    base = 2 * blocks * toks
+    square = iota((toks, lanes), 0) == iota((toks, lanes), 1)
+    sums_row = whole[base : base + 1, :] + whole[base + 1 : base + 2, :]
+    sums = jnp.sum(
+        jnp.where(square, jnp.broadcast_to(sums_row, (toks, lanes)), 0.0), axis=-1, keepdims=True
+    )
     factor = lax.rsqrt(sums / (width * 4) + norm_eps)
-    gate = total[:, :units] * factor
-    hidden = (gate / (1.0 + jnp.exp(-gate)) * (total[:, units : 2 * units] * factor)).astype(bf16)
+    pieces = []
+    for i in range(blocks):
+        gate = whole[i * toks : (i + 1) * toks, :] * factor
+        up = whole[(blocks + i) * toks : (blocks + i + 1) * toks, :] * factor
+        pieces.append((gate / (1.0 + jnp.exp(-gate)) * up).astype(bf16))
+    hidden = jnp.concatenate(pieces, axis=1)
     own_rows = pl.ds(pl.multiple_of(y * units, lanes), units)
     part[y] = dot(hidden, down_ref[own_rows, :])
     part[1 - y] = dot(hidden, pair_ref[...])
@@ -555,7 +584,7 @@
         out_ref[:, at] = (mixed / totals * gates[:, h : h + 1]).astype(bf16)
 
 
-def call(body, out_shape, args, scratch=(), hbm=False, smem=0, flops=0, limit=12, **more):
+def call(body, out_shape, args, scratch=(), hbm=False, out_any=False, smem=0, flops=0, limit=12):
     specs = [pl.BlockSpec(memory_space=pltpu.SMEM)] * smem
     space = pltpu.HBM if hbm else pltpu.VMEM
     specs += [pl.BlockSpec(memory_space=space)] * (len(args) - smem)
@@ -564,7 +593,9 @@
         body,
         out_shape=out_shape,
         in_specs=specs,
-        out_specs=jax.tree.map(lambda _: pl.BlockSpec(memory_space=pltpu.VMEM), out_shape),
+        out_specs=jax.tree.map(
+            lambda _: pl.BlockSpec(memory_space=pl.ANY if out_any else pltpu.VMEM), out_shape
+        ),
         scratch_shapes=[pltpu.VMEM(s, f32) if isinstance(s, tuple) else s for s in scratch],
         compiler_params=pltpu.CompilerParams(vmem_limit_bytes=limit * 2**20),
         cost_estimate=pl.CostEstimate(flops=flops, bytes_accessed=size, transcendentals=0),
@@ -635,21 +666,24 @@
         lengths, k_pre, v_pre, q_new, k_new, v_new, gate_new, resid, qg, kg, freqs,
         w_out, w_gate, w_up, w_down,
     )
+    outputs = (
+        jax.ShapeDtypeStruct((tok, 2 * k_pre.shape[1]), bf16),
+        jax.ShapeDtypeStruct((peers, pay_rows // 4, 4, lanes), bf16),
+        jax.ShapeDtypeStruct((w_out.shape[0], part), bf16),
+        jax.ShapeDtypeStruct((w_gate.shape[0], 2 * units), bf16),
+        jax.ShapeDtypeStruct((units, w_down.shape[1]), bf16),
+    )
     kv, pay, w_own, pair, down_pair = call(
         partial_kernel,
-        (
-            jax.ShapeDtypeStruct((tok, 2 * k_pre.shape[1]), bf16),
-            jax.ShapeDtypeStruct((peers, pay_rows // 4, 4, lanes), bf16),
-            jax.ShapeDtypeStruct((w_out.shape[0], part), bf16),
-            jax.ShapeDtypeStruct((w_gate.shape[0], 2 * units), bf16),
-            jax.ShapeDtypeStruct((units, w_down.shape[1]), bf16),
-        ),
+        outputs,
         inputs,
-        scratch=[(heads * rpg, lanes)] * 4
+        scratch=[pltpu.VMEM(o.shape, o.dtype) for o in outputs]
+        + [(heads * rpg, lanes)] * 4
         + [(pay_rows, lanes), pltpu.SMEM(lengths.shape, jnp.int32)]
         + [pltpu.VMEM(a.shape, a.dtype) for a in inputs[1:11]]
-        + [pltpu.SemaphoreType.DMA((len(inputs),))],
+        + [pltpu.SemaphoreType.DMA((len(inputs),)), pltpu.SemaphoreType.DMA((len(outputs),))],
         hbm=True,
+        out_any=True,
         flops=10**7,
         limit=56,
     )
@@ -680,11 +714,12 @@
     got = lax.all_to_all(pay, ("req", "tp"), 0, 0, tiled=True)
     landed = hold((pair,), 2 * 10**9)
     token = hold((landed, w_near, w_both), 10**9)
+    msg_shape = (2 * units // lanes * toks + 8, lanes)
     hid, msg = call(
         hidden_kernel,
         (
             jax.ShapeDtypeStruct((toks, part), f32),
-            jax.ShapeDtypeStruct((toks, 2 * units + lanes), bf16),
+            jax.ShapeDtypeStruct(msg_shape, bf16),
         ),
         (got, w_here, w_near, w_far, w_both, mine, pair, ng, token),
         scratch=[
@@ -692,6 +727,7 @@
             (toks, part),
             (2, toks, part // 2),
             (reqs, pay_rows, lanes),
+            msg_shape,
         ],
         flops=10**7,
     )
@@ -709,7 +745,7 @@
         down_kernel,
         jax.ShapeDtypeStruct((peers, back_rows, lanes), bf16),
         (*msgs, hid, w_down, down_pair),
-        scratch=[(2, toks, part // 2), (reqs, back_rows, lanes)],
+        scratch=[(2, toks, part // 2), (reqs, back_rows, lanes), msg_shape],
         flops=3 * 10**9,
     )
     returned = lax.all_to_all(back, ("req", "tp"), 0, 0, tiled=True)

time: 43.2 us -> 42.8 us (level)
  no operation moved by 1% of the time
where the time goes in v5:
time: 42.8 us; the launch traced here: 42.5 us
  starting transfers between devices  19.6 us (46%)
  waiting for transfers between devices  12 us (28%)
  Pallas kernels  8.69 us (20%)
  local copies, waits for them, and re-layouts  1.41 us (3%)
  between operations  0.82 us (2%)
    pallas_call x7, Pallas kernels, call(): pl.pallas_call(body, out_shape=out_shape, in_specs=specs, out_specs=jax.t...  8.69 us
    all_to_all x1, waiting for transfers between devices, local(): got = lax.all_to_all(pay, ('req', 'tp'), 0, 0, tiled=True)  4.49 us
    ppermute x3, starting transfers between devices, along(): return lax.ppermute(array, 'req', [(i, i ^ 2 * by) for i in range(reqs)])  4.45 us
    ppermute x2, starting transfers between devices, swap(): return lax.ppermute(array, 'req', [(i, i ^ 1) for i in range(reqs)])  4.34 us
    all_to_all x1, waiting for transfers between devices, local(): returned = lax.all_to_all(back, ('req', 'tp'), 0, 0, tiled=True)  4.21 us
    all_to_all x1, starting transfers between devices, local(): got = lax.all_to_all(pay, ('req', 'tp'), 0, 0, tiled=True)  3.97 us
    ppermute x6, starting transfers between devices, cross(): return lax.ppermute(array, 'tp', [(i, i ^ by) for i in range(tps)])  3.78 us
    all_to_all x1, starting transfers between devices, local(): returned = lax.all_to_all(back, ('req', 'tp'), 0, 0, tiled=True)  3.01 us
  transfers between devices with their start and end apart: 13, of which 5 were waited for; matrix products, arithmetic and copies ran while one was open for 0% of the time, Pallas kernels for 12%

profile of v5, /device:TPU:0, one launch (start us, length us, event | category | flops | bytes accessed | tf_op | source)
XLA Modules:
  0.0 42.5 jit_solution(12632716352956639250)
XLA Ops:
  0.6 0.0 copy-start
  0.6 2.9 %shard_map.185 = (bf16[128,1024]{1,0:T(8,128)(2,1)}, bf16[32,7,4,128]{3,2,1,0:T(4,128)(2,1)}, bf16[256,512]{1,0:T(8,128)(2,1)}, bf16[256,768]{1,0:T(8,128)(2,1)}, bf16[384,256]{1,0:T(8,128)(2,1)}) custom-call(s32[1,3]{1,0:T(1,128)} %len_ref.1, bf16[128,512]{1,0:T(8,128)(2,1)} %k_hbm.1, bf16[128,512]{1,0:T(8,128)(2,1)} %v_hbm.1, bf16[3,1024]{1,0:T(4,128)(2,1)} %qn_hbm.1, ...), custom_call_target="tpu_custom_call" | custom-call | flops 10000000 | bytes 2516540 | tf_op jit(solution)/shard_map/pallas_call | solution.py:592
  3.6 0.0 copy-start.11
  3.6 3.0 %collective-permute-start.3 = (bf16[256,768]{1,0:T(8,128)(2,1)}, bf16[256,768]{1,0:T(8,128)(2,1)S(1)}, u32[]{:S(2)}, u32[]{:S(2)}) collective-permute-start(bf16[256,768]{1,0:T(8,128)(2,1)} %get-tuple-element.20), channel_id=1, source_target_pairs={{0,4},{4,0},{8,12},{12,8},{16,20},{20,16},{24,28},{28,24},{1,5},{5... | collective-permute-start | bytes 1179656 | tf_op jit(solution)/shard_map/ppermute | solution.py:660
  6.6 1.5 %collective-permute-start.1 = (bf16[256,512]{1,0:T(8,128)(2,1)}, bf16[256,512]{1,0:T(8,128)(2,1)S(1)}, u32[]{:S(2)}, u32[]{:S(2)}) collective-permute-start(bf16[256,512]{1,0:T(8,128)(2,1)} %get-tuple-element.17), channel_id=1, source_target_pairs={{0,2},{1,3},{2,0},{3,1},{4,6},{5,7},{6,4},{7,5},{8,10},{9,11},{10,... | collective-permute-start | bytes 786440 | tf_op jit(solution)/shard_map/ppermute | solution.py:657
  8.1 4.0 %all-to-all-start = ((bf16[32,7,4,128]{3,2,1,0:T(4,128)(2,1)}), bf16[32,7,4,128]{3,2,1,0:T(4,128)(2,1)S(1)}, u32[]{:S(2)}, u32[]{:S(2)}) async-start(bf16[32,7,4,128]{3,2,1,0:T(4,128)(2,1)} %get-tuple-element.16), calls=%async_computation | async-start | bytes 458752 | tf_op jit(solution)/shard_map/all_to_all | solution.py:714
  12.1 0.0 copy-start.1
  12.1 0.0 copy-start.2
  12.1 0.0 copy-start.4
  12.1 0.3 collective-permute-start
  12.5 0.0 copy-done
  12.5 0.6 %copy-done.1 = bf16[256,768]{1,0:T(8,128)(2,1)S(1)} copy-done((bf16[256,768]{1,0:T(8,128)(2,1)S(1)}, bf16[256,768]{1,0:T(8,128)(2,1)}, u32[]{:S(2)}) %copy-start.1) | copy-done | bytes 393240
  13.1 0.1 copy-done.2
  13.2 0.1 shard_map.187
  13.3 1.3 %collective-permute-done.1.w2_ref = bf16[256,512]{1,0:T(8,128)(2,1)S(1)} collective-permute-done((bf16[256,512]{1,0:T(8,128)(2,1)}, bf16[256,512]{1,0:T(8,128)(2,1)S(1)}, u32[]{:S(2)}, u32[]{:S(2)}) %collective-permute-start.1) | collective-permute-done | bytes 262176 | tf_op jit(solution)/shard_map/ppermute | solution.py:657
  14.6 0.0 collective-permute-start.2
  14.6 1.3 %collective-permute-start.7 = (bf16[384,256]{1,0:T(8,128)(2,1)S(1)}, bf16[384,256]{1,0:T(8,128)(2,1)S(1)}, u32[]{:S(2)}, u32[]{:S(2)}) collective-permute-start(bf16[384,256]{1,0:T(8,128)(2,1)S(1)} %copy-done.12), channel_id=1, source_target_pairs={{0,4},{4,0},{8,12},{12,8},{16,20},{20,16},{24,28},{28,24},{1,5},{5... | collective-permute-start | bytes 589832 | tf_op jit(solution)/shard_map/ppermute | solution.py:660
  15.9 1.5 %collective-permute-start.9 = (bf16[128,1024]{1,0:T(8,128)(2,1)S(1)}, bf16[128,1024]{1,0:T(8,128)(2,1)S(1)}, u32[]{:S(2)}, u32[]{:S(2)}) collective-permute-start(bf16[128,1024]{1,0:T(8,128)(2,1)S(1)} %copy-done.9), channel_id=1, source_target_pairs={{0,2},{1,3},{2,0},{3,1},{4,6},{5,7},{6,4},{7,5},{8,10},{9,11},{10,... | collective-permute-start | bytes 786440 | tf_op jit(solution)/shard_map/ppermute | solution.py:657
  17.4 0.0 collective-permute-done.3.refs_0_.pair_ref
  17.4 0.0 collective-permute-done.refs_1_.w1_ref
  17.4 0.0 collective-permute-done.2.refs_2_.w3_ref
  17.4 4.5 %all-to-all-done.pay_ref = bf16[32,7,4,128]{3,2,1,0:T(4,128)(2,1)S(1)} async-done(((bf16[32,7,4,128]{3,2,1,0:T(4,128)(2,1)}), bf16[32,7,4,128]{3,2,1,0:T(4,128)(2,1)S(1)}, u32[]{:S(2)}, u32[]{:S(2)}) %all-to-all-start) | async-done | bytes 229408 | tf_op jit(solution)/shard_map/all_to_all | solution.py:714
  21.9 0.7 %shard_map.190 = (f32[24,512]{1,0:T(8,128)S(1)}, bf16[152,128]{1,0:T(8,128)(2,1)S(1)}) custom-call(bf16[32,7,4,128]{3,2,1,0:T(4,128)(2,1)S(1)} %all-to-all-done.pay_ref, bf16[256,512]{1,0:T(8,128)(2,1)S(1)} %shard_map.186.w0_ref, bf16[256,512]{1,0:T(8,128)(2,1)S(1)} %collective-permute-done.refs_1_.w1_ref, ...), custom_call_target="tpu_custom_call" | custom-call | flops 10000000 | bytes 2070528 | tf_op jit(solution)/shard_map/pallas_call | solution.py:592
  22.6 1.6 %collective-permute-start.4 = (bf16[152,128]{1,0:T(8,128)(2,1)S(1)}, bf16[152,128]{1,0:T(8,128)(2,1)S(1)}, u32[]{:S(2)}, u32[]{:S(2)}) collective-permute-start(bf16[152,128]{1,0:T(8,128)(2,1)S(1)} %get-tuple-element.22.m0_ref), channel_id=1, source_target_pairs={{0,24},{4,28},{8,16},{12,20},{16,8},{20,12},{24,0},{28,4},{1,25},{... | collective-permute-start | bytes 116744 | tf_op jit(solution)/shard_map/ppermute | solution.py:663
  24.2 1.0 %collective-permute-start.5 = (bf16[152,128]{1,0:T(8,128)(2,1)S(1)}, bf16[152,128]{1,0:T(8,128)(2,1)S(1)}, u32[]{:S(2)}, u32[]{:S(2)}) collective-permute-start(bf16[152,128]{1,0:T(8,128)(2,1)S(1)} %get-tuple-element.22.m0_ref), channel_id=1, source_target_pairs={{0,16},{4,20},{8,24},{12,28},{16,0},{20,4},{24,8},{28,12},{1,17},{... | collective-permute-start | bytes 116744 | tf_op jit(solution)/shard_map/ppermute | solution.py:663
  25.1 1.9 %collective-permute-start.6 = (bf16[152,128]{1,0:T(8,128)(2,1)S(1)}, bf16[152,128]{1,0:T(8,128)(2,1)S(1)}, u32[]{:S(2)}, u32[]{:S(2)}) collective-permute-start(bf16[152,128]{1,0:T(8,128)(2,1)S(1)} %get-tuple-element.22.m0_ref), channel_id=1, source_target_pairs={{0,8},{4,12},{8,0},{12,4},{16,24},{20,28},{24,16},{28,20},{1,9},{5... | collective-permute-start | bytes 116744 | tf_op jit(solution)/shard_map/ppermute | solution.py:663
  27.1 0.0 collective-permute-done.7.pair_ref
  27.1 0.0 collective-permute-start.8
  27.1 0.0 collective-permute-done.9.kv2_ref
  27.1 0.5 %collective-permute-start.10 = (bf16[128,1024]{1,0:T(8,128)(2,1)S(1)}, bf16[128,1024]{1,0:T(8,128)(2,1)S(1)}, u32[]{:S(2)}, u32[]{:S(2)}) collective-permute-start(bf16[128,1024]{1,0:T(8,128)(2,1)S(1)} %collective-permute-done.9.kv2_ref), channel_id=1, source_target_pairs={{0,1},{1,0},{2,3},{3,2},{4,5},{5,4},{6,7},{7,6},{8,9},{9,8},{10,11... | collective-permute-start | bytes 786440 | tf_op jit(solution)/shard_map/ppermute | solution.py:657
  27.6 1.3 %collective-permute-done.4.m1_ref = bf16[152,128]{1,0:T(8,128)(2,1)S(1)} collective-permute-done((bf16[152,128]{1,0:T(8,128)(2,1)S(1)}, bf16[152,128]{1,0:T(8,128)(2,1)S(1)}, u32[]{:S(2)}, u32[]{:S(2)}) %collective-permute-start.4) | collective-permute-done | bytes 38944 | tf_op jit(solution)/shard_map/ppermute | solution.py:663
  28.8 0.8 %collective-permute-done.5.m2_ref = bf16[152,128]{1,0:T(8,128)(2,1)S(1)} collective-permute-done((bf16[152,128]{1,0:T(8,128)(2,1)S(1)}, bf16[152,128]{1,0:T(8,128)(2,1)S(1)}, u32[]{:S(2)}, u32[]{:S(2)}) %collective-permute-start.5) | collective-permute-done | bytes 38944 | tf_op jit(solution)/shard_map/ppermute | solution.py:663
  29.6 0.0 collective-permute-done.6.m3_ref
  29.6 0.0 copy-done.3
  29.6 0.9 %shard_map.191 = bf16[32,16,128]{2,1,0:T(8,128)(2,1)} custom-call(bf16[152,128]{1,0:T(8,128)(2,1)S(1)} %get-tuple-element.22.m0_ref, bf16[152,128]{1,0:T(8,128)(2,1)S(1)} %collective-permute-done.4.m1_ref, bf16[152,128]{1,0:T(8,128)(2,1)S(1)} %collective-permute-done.5.m2_ref, bf16[152,128]{1,0:T(8,128)(2,1)S(1)} %collective-permute-done.6.m3_ref, ...), custom_call_target="tpu_custom_call" | custom-call | flops 3000000000 | bytes 794624 | tf_op jit(solution)/shard_map/pallas_call | solution.py:592
  30.6 3.0 %all-to-all-start.1 = ((bf16[32,16,128]{2,1,0:T(8,128)(2,1)}), bf16[32,16,128]{2,1,0:T(8,128)(2,1)S(1)}, u32[]{:S(2)}, u32[]{:S(2)}) async-start(bf16[32,16,128]{2,1,0:T(8,128)(2,1)} %shard_map.191), calls=%async_computation.1 | async-start | bytes 262144 | tf_op jit(solution)/shard_map/all_to_all | solution.py:751
  33.6 0.0 copy-start.5
  33.6 0.0 copy-start.6
  33.6 0.0 copy-start.7
  33.6 0.1 copy.20.g_ref
  33.8 0.0 collective-permute-done.8.kv1_ref
  33.8 0.0 collective-permute-done.10.kv3_ref
  33.8 0.5 %copy-done.5 = s32[1,3]{1,0:T(1,128)S(1)} copy-done((s32[1,3]{1,0:T(1,128)S(1)}, s32[1,3]{1,0:T(1,128)}, u32[]{:S(2)}) %copy-start.5) | copy-done | bytes 36
  34.2 0.0 copy-done.6
  34.3 0.0 copy-done.7
  34.3 3.3 %shard_map.192 = bf16[128,1024]{1,0:T(8,128)(2,1)} custom-call(s32[1,3]{1,0:T(1,128)S(1)} %copy-done.5, bf16[128,1024]{1,0:T(8,128)(2,1)S(1)} %copy-done.8, bf16[128,8]{1,0:T(8,128)(2,1)S(1)} %copy.20.g_ref, bf16[128,1024]{1,0:T(8,128)(2,1)S(1)} %copy-done.9, bf16[128,1024]{1,0:T(8,128)(2,1)S(1)} %collective-permute-done.8.kv1_ref, ...), custom_call_target="tpu_custom_call" | custom-call | flops 1000000000 | bytes 1313804 | tf_op jit(solution)/shard_map/pallas_call | solution.py:592
  37.6 4.2 %all-to-all-done.1.back_ref = bf16[32,16,128]{2,1,0:T(8,128)(2,1)S(1)} async-done(((bf16[32,16,128]{2,1,0:T(8,128)(2,1)}), bf16[32,16,128]{2,1,0:T(8,128)(2,1)S(1)}, u32[]{:S(2)}, u32[]{:S(2)}) %all-to-all-start.1) | async-done | bytes 131104 | tf_op jit(solution)/shard_map/all_to_all | solution.py:751
  41.8 0.7 %shard_map.193 = bf16[3,2048]{1,0:T(4,128)(2,1)} custom-call(bf16[32,16,128]{2,1,0:T(8,128)(2,1)S(1)} %all-to-all-done.1.back_ref), custom_call_target="tpu_custom_call" | custom-call | flops 1000000 | bytes 131072 | tf_op jit(solution)/shard_map/pallas_call | solution.py:592
  (14 shorter events, 0.1 us)
Async XLA Ops:
  0.6 11.8 %copy-start = (bf16[256,2048]{1,0:T(8,128)(2,1)S(1)}, bf16[256,2048]{1,0:T(8,128)(2,1)}, u32[]{:S(2)}) copy-start(bf16[256,2048]{1,0:T(8,128)(2,1)} %w_hbm.3) | copy-start | bytes 3145732
  3.6 8.5 %copy-start.11 = (bf16[256,512]{1,0:T(8,128)(2,1)S(1)}, bf16[256,512]{1,0:T(8,128)(2,1)}, u32[]{:S(2)}) copy-start(bf16[256,512]{1,0:T(8,128)(2,1)} %get-tuple-element.17) | copy-start | bytes 786436
  3.6 13.8 %collective-permute-start.3 = (bf16[256,768]{1,0:T(8,128)(2,1)}, bf16[256,768]{1,0:T(8,128)(2,1)S(1)}, u32[]{:S(2)}, u32[]{:S(2)}) collective-permute-start(bf16[256,768]{1,0:T(8,128)(2,1)} %get-tuple-element.20), channel_id=1, source_target_pairs={{0,4},{4,0},{8,12},{12,8},{16,20},{20,16},{24,28},{28,24},{1,5},{5... | collective-permute-start | bytes 1179656 | tf_op jit(solution)/shard_map/ppermute | solution.py:660
  6.6 8.0 %collective-permute-start.1 = (bf16[256,512]{1,0:T(8,128)(2,1)}, bf16[256,512]{1,0:T(8,128)(2,1)S(1)}, u32[]{:S(2)}, u32[]{:S(2)}) collective-permute-start(bf16[256,512]{1,0:T(8,128)(2,1)} %get-tuple-element.17), channel_id=1, source_target_pairs={{0,2},{1,3},{2,0},{3,1},{4,6},{5,7},{6,4},{7,5},{8,10},{9,11},{10,... | collective-permute-start | bytes 786440 | tf_op jit(solution)/shard_map/ppermute | solution.py:657
  8.1 13.8 %all-to-all-start = ((bf16[32,7,4,128]{3,2,1,0:T(4,128)(2,1)}), bf16[32,7,4,128]{3,2,1,0:T(4,128)(2,1)S(1)}, u32[]{:S(2)}, u32[]{:S(2)}) async-start(bf16[32,7,4,128]{3,2,1,0:T(4,128)(2,1)} %get-tuple-element.16), calls=%async_computation | async-start | bytes 458752 | tf_op jit(solution)/shard_map/all_to_all | solution.py:714
  12.1 1.0 %copy-start.1 = (bf16[256,768]{1,0:T(8,128)(2,1)S(1)}, bf16[256,768]{1,0:T(8,128)(2,1)}, u32[]{:S(2)}) copy-start(bf16[256,768]{1,0:T(8,128)(2,1)} %gate_hbm.3) | copy-start | bytes 1179652
  12.1 1.1 %copy-start.2 = (bf16[256,768]{1,0:T(8,128)(2,1)S(1)}, bf16[256,768]{1,0:T(8,128)(2,1)}, u32[]{:S(2)}) copy-start(bf16[256,768]{1,0:T(8,128)(2,1)} %up_hbm.3) | copy-start | bytes 1179652
  12.1 1.1 %copy-start.4 = (f32[2048]{0:T(1024)S(1)}, f32[2048]{0:T(1024)}, u32[]{:S(2)}) copy-start(f32[2048]{0:T(1024)} %param.31) | copy-start | bytes 24580
  12.1 5.3 %collective-permute-start = (bf16[256,512]{1,0:T(8,128)(2,1)S(1)}, bf16[256,512]{1,0:T(8,128)(2,1)S(1)}, u32[]{:S(2)}, u32[]{:S(2)}) collective-permute-start(bf16[256,512]{1,0:T(8,128)(2,1)S(1)} %copy-done.11), channel_id=1, source_target_pairs={{0,1},{1,0},{2,3},{3,2},{4,5},{5,4},{6,7},{7,6},{8,9},{9,8},{10,11... | collective-permute-start | bytes 786440 | tf_op jit(solution)/shard_map/ppermute | solution.py:657
  13.2 1.4 %copy-start.12 = (bf16[384,256]{1,0:T(8,128)(2,1)S(1)}, bf16[384,256]{1,0:T(8,128)(2,1)}, u32[]{:S(2)}) copy-start(bf16[384,256]{1,0:T(8,128)(2,1)} %get-tuple-element.25) | copy-start | bytes 589828
  13.2 2.7 %copy-start.9 = (bf16[128,1024]{1,0:T(8,128)(2,1)S(1)}, bf16[128,1024]{1,0:T(8,128)(2,1)}, u32[]{:S(2)}) copy-start(bf16[128,1024]{1,0:T(8,128)(2,1)} %get-tuple-element.27.kv0_ref) | copy-start | bytes 786436
  14.6 2.8 %collective-permute-start.2 = (bf16[256,512]{1,0:T(8,128)(2,1)S(1)}, bf16[256,512]{1,0:T(8,128)(2,1)S(1)}, u32[]{:S(2)}, u32[]{:S(2)}) collective-permute-start(bf16[256,512]{1,0:T(8,128)(2,1)S(1)} %collective-permute-done.1.w2_ref), channel_id=1, source_target_pairs={{0,1},{1,0},{2,3},{3,2},{4,5},{5,4},{6,7},{7,6},{8,9},{9,8},{10,11... | collective-permute-start | bytes 786440 | tf_op jit(solution)/shard_map/ppermute | solution.py:657
  14.6 12.4 %collective-permute-start.7 = (bf16[384,256]{1,0:T(8,128)(2,1)S(1)}, bf16[384,256]{1,0:T(8,128)(2,1)S(1)}, u32[]{:S(2)}, u32[]{:S(2)}) collective-permute-start(bf16[384,256]{1,0:T(8,128)(2,1)S(1)} %copy-done.12), channel_id=1, source_target_pairs={{0,4},{4,0},{8,12},{12,8},{16,20},{20,16},{24,28},{28,24},{1,5},{5... | collective-permute-start | bytes 589832 | tf_op jit(solution)/shard_map/ppermute | solution.py:660
  15.9 11.1 %collective-permute-start.9 = (bf16[128,1024]{1,0:T(8,128)(2,1)S(1)}, bf16[128,1024]{1,0:T(8,128)(2,1)S(1)}, u32[]{:S(2)}, u32[]{:S(2)}) collective-permute-start(bf16[128,1024]{1,0:T(8,128)(2,1)S(1)} %copy-done.9), channel_id=1, source_target_pairs={{0,2},{1,3},{2,0},{3,1},{4,6},{5,7},{6,4},{7,5},{8,10},{9,11},{10,... | collective-permute-start | bytes 786440 | tf_op jit(solution)/shard_map/ppermute | solution.py:657
  21.9 7.7 %copy-start.3 = (bf16[768,256]{1,0:T(8,128)(2,1)S(1)}, bf16[768,256]{1,0:T(8,128)(2,1)}, u32[]{:S(2)}) copy-start(bf16[768,256]{1,0:T(8,128)(2,1)} %down_ref.1) | copy-start | bytes 1179652
  22.6 6.2 %collective-permute-start.4 = (bf16[152,128]{1,0:T(8,128)(2,1)S(1)}, bf16[152,128]{1,0:T(8,128)(2,1)S(1)}, u32[]{:S(2)}, u32[]{:S(2)}) collective-permute-start(bf16[152,128]{1,0:T(8,128)(2,1)S(1)} %get-tuple-element.22.m0_ref), channel_id=1, source_target_pairs={{0,24},{4,28},{8,16},{12,20},{16,8},{20,12},{24,0},{28,4},{1,25},{... | collective-permute-start | bytes 116744 | tf_op jit(solution)/shard_map/ppermute | solution.py:663
  24.2 5.4 %collective-permute-start.5 = (bf16[152,128]{1,0:T(8,128)(2,1)S(1)}, bf16[152,128]{1,0:T(8,128)(2,1)S(1)}, u32[]{:S(2)}, u32[]{:S(2)}) collective-permute-start(bf16[152,128]{1,0:T(8,128)(2,1)S(1)} %get-tuple-element.22.m0_ref), channel_id=1, source_target_pairs={{0,16},{4,20},{8,24},{12,28},{16,0},{20,4},{24,8},{28,12},{1,17},{... | collective-permute-start | bytes 116744 | tf_op jit(solution)/shard_map/ppermute | solution.py:663
  25.1 4.5 %collective-permute-start.6 = (bf16[152,128]{1,0:T(8,128)(2,1)S(1)}, bf16[152,128]{1,0:T(8,128)(2,1)S(1)}, u32[]{:S(2)}, u32[]{:S(2)}) collective-permute-start(bf16[152,128]{1,0:T(8,128)(2,1)S(1)} %get-tuple-element.22.m0_ref), channel_id=1, source_target_pairs={{0,8},{4,12},{8,0},{12,4},{16,24},{20,28},{24,16},{28,20},{1,9},{5... | collective-permute-start | bytes 116744 | tf_op jit(solution)/shard_map/ppermute | solution.py:663
  27.1 6.7 %collective-permute-start.8 = (bf16[128,1024]{1,0:T(8,128)(2,1)S(1)}, bf16[128,1024]{1,0:T(8,128)(2,1)S(1)}, u32[]{:S(2)}, u32[]{:S(2)}) collective-permute-start(bf16[128,1024]{1,0:T(8,128)(2,1)S(1)} %copy-done.9), channel_id=1, source_target_pairs={{0,1},{1,0},{2,3},{3,2},{4,5},{5,4},{6,7},{7,6},{8,9},{9,8},{10,11... | collective-permute-start | bytes 786440 | tf_op jit(solution)/shard_map/ppermute | solution.py:657
  27.1 6.7 %collective-permute-start.10 = (bf16[128,1024]{1,0:T(8,128)(2,1)S(1)}, bf16[128,1024]{1,0:T(8,128)(2,1)S(1)}, u32[]{:S(2)}, u32[]{:S(2)}) collective-permute-start(bf16[128,1024]{1,0:T(8,128)(2,1)S(1)} %collective-permute-done.9.kv2_ref), channel_id=1, source_target_pairs={{0,1},{1,0},{2,3},{3,2},{4,5},{5,4},{6,7},{7,6},{8,9},{9,8},{10,11... | collective-permute-start | bytes 786440 | tf_op jit(solution)/shard_map/ppermute | solution.py:657
  29.6 4.0 %copy-start.10 = (bf16[128,8]{0,1:T(8,128)(2,1)S(1)}, bf16[128,8]{0,1:T(8,128)(2,1)}, u32[]{:S(2)}) copy-start(bf16[128,8]{0,1:T(8,128)(2,1)} %param.19) | copy-start | bytes 6148
  30.6 3.2 %copy-start.8 = (bf16[128,1024]{1,0:T(8,128)(2,1)S(1)}, bf16[128,1024]{1,0:T(8,128)(2,1)}, u32[]{:S(2)}) copy-start(bf16[128,1024]{1,0:T(8,128)(2,1)} %q_ref.1) | copy-start | bytes 786436
  30.6 11.2 %all-to-all-start.1 = ((bf16[32,16,128]{2,1,0:T(8,128)(2,1)}), bf16[32,16,128]{2,1,0:T(8,128)(2,1)S(1)}, u32[]{:S(2)}, u32[]{:S(2)}) async-start(bf16[32,16,128]{2,1,0:T(8,128)(2,1)} %shard_map.191), calls=%async_computation.1 | async-start | bytes 262144 | tf_op jit(solution)/shard_map/all_to_all | solution.py:751
  33.6 0.7 %copy-start.5 = (s32[1,3]{1,0:T(1,128)S(1)}, s32[1,3]{1,0:T(1,128)}, u32[]{:S(2)}) copy-start(s32[1,3]{1,0:T(1,128)} %len_ref.1) | copy-start | bytes 40
  33.6 0.7 %copy-start.6 = (f32[128]{0:T(128)S(1)}, f32[128]{0:T(128)}, u32[]{:S(2)}) copy-start(f32[128]{0:T(128)} %param.22) | copy-start | bytes 1540
  33.6 0.7 %copy-start.7 = (f32[1,128]{1,0:T(1,128)S(1)}, f32[1,128]{1,0:T(1,128)}, u32[]{:S(2)}) copy-start(f32[1,128]{1,0:T(1,128)} %constant.2.clone.freq_hbm.freq_ref) | copy-start | bytes 1540

commit v6 on v5

--- a/solution.py
+++ b/solution.py
@@ -205,7 +205,7 @@
 bf16 = jnp.bfloat16
 lanes = 128
 pay_rows = 28
-back_rows = 16
+back_rows = 12
 
 
 def dot(a, b):
@@ -504,45 +504,37 @@
     chunks = width // lanes
     groups = pay.shape[0]
     rpg = toks // groups
-    piece = hid_ref[:, pl.ds(pl.multiple_of(tp * lanes, lanes), lanes)]
-    high = piece.astype(bf16).astype(f32)
-    piece = jnp.where(y == 0, high, piece - high)
-    pay[...] = jnp.zeros_like(pay)
-    for c in range(chunks + 1):
-        if c < chunks:
-            at = (c * lanes) % half
-            block = part[c * lanes // half][:, at : at + lanes]
-        else:
-            block = piece
+    for c in range(chunks):
+        at = (c * lanes) % half
+        block = part[c * lanes // half][:, at : at + lanes]
+        adds = (y == 0) & (tp == c)
+        block = block + jnp.where(adds, hid_ref[:, c * lanes : (c + 1) * lanes], 0.0)
         for r in range(groups):
             pay[r, c * rpg : (c + 1) * rpg, :] = block[r * rpg : (r + 1) * rpg, :]
     for r in range(groups):
-        out = pay[r].astype(bf16)
-        for t in range(tps):
-            back_ref[r * tps + t] = out
-
-
-def final_kernel(back_ref, out_ref, acc, tail, rows_out):
+        for g in range(back_ref.shape[1]):
+            out = pay[r, 4 * g : 4 * g + 4, :].astype(bf16)
+            for t in range(tps):
+                back_ref[r * tps + t, g] = out
+
+
+def final_kernel(back_ref, out_ref, acc, rows_out):
     tps = lax.axis_size("tp")
     peers = back_ref.shape[0]
     rpg, width = out_ref.shape
-    chunks = tps
-    slices = width // (chunks * lanes)
+    slices = acc.shape[0]
     group = peers // slices
+    chunks = width // (slices * lanes)
     for z in range(slices):
-        total = jnp.zeros(acc.shape, f32)
-        by_tp = [jnp.zeros(acc.shape, f32) for _ in range(tps)]
-        for p in range(group):
-            piece = back_ref[z * group + p].astype(f32)
-            total = total + piece
-            by_tp[p % tps] = by_tp[p % tps] + piece
-        acc[...] = total
+        for g in range(back_ref.shape[1]):
+            total = back_ref[z * group, g].astype(f32)
+            for p in range(1, group):
+                total = total + back_ref[z * group + p, g].astype(f32)
+            acc[z, 4 * g : 4 * g + 4, :] = total
+    for z in range(slices):
         for c in range(chunks):
-            tail[...] = by_tp[c]
             at = slice((z * chunks + c) * lanes, (z * chunks + c + 1) * lanes)
-            rows_out[0:rpg, at] = (
-                acc[c * rpg : (c + 1) * rpg, :] + tail[chunks * rpg : (chunks + 1) * rpg, :]
-            )
+            rows_out[0:rpg, at] = acc[z, c * rpg : (c + 1) * rpg, :]
     out_ref[...] = rows_out[0:rpg, :].astype(bf16)
 
 
@@ -709,7 +701,7 @@
     kv_near = cross(kv, 1)
     late_kv, _ = lax.optimization_barrier((kv, w_far))
     kv_far = cross(late_kv, 2)
-    late_down, _ = lax.optimization_barrier((down_pair, w_far))
+    late_down, _ = lax.optimization_barrier((down_pair, pair))
     down_pair = swap(late_down)
     got = lax.all_to_all(pay, ("req", "tp"), 0, 0, tiled=True)
     landed = hold((pair,), 2 * 10**9)
@@ -743,7 +735,7 @@
     )
     back = call(
         down_kernel,
-        jax.ShapeDtypeStruct((peers, back_rows, lanes), bf16),
+        jax.ShapeDtypeStruct((peers, back_rows // 4, 4, lanes), bf16),
         (*msgs, hid, w_down, down_pair),
         scratch=[(2, toks, part // 2), (reqs, back_rows, lanes), msg_shape],
         flops=3 * 10**9,
@@ -754,7 +746,7 @@
         final_kernel,
         jax.ShapeDtypeStruct((rpg, width), bf16),
         (returned,),
-        scratch=[(back_rows, lanes), (back_rows, lanes), (8, width)],
+        scratch=[(slices, back_rows, lanes), (8, width)],
         flops=10**6,
     )
     return (prefill_out, decode_out)

time: 42.8 us -> 42.3 us (0.988)
  waiting for transfers between devices: 12 us -> 10.7 us
  starting transfers between devices: 19.6 us -> 20.4 us
    all_to_all x1, waiting for transfers between devices: 4.49 us -> 2.75 us  [local(): got = lax.all_to_all(pay, ('req', 'tp'), 0, 0, tiled=True)]
    ppermute x2, starting transfers between devices: 4.34 us -> 5.44 us  [swap(): return lax.ppermute(array, 'req', [(i, i ^ 1) for i in range(reqs)])]
    ppermute x3, waiting for transfers between devices: 2.04 us -> 2.54 us  [along(): return lax.ppermute(array, 'req', [(i, i ^ 2 * by) for i in range(reqs)])]
  transfers between devices with their start and end apart: 13 -> 13, of which waited for: 5 -> 6; matrix products, arithmetic and copies ran while one was open for 0% -> 0% of each run, Pallas kernels for 12% -> 12%
where the time goes in v6:
time: 42.3 us; the launch traced here: 42 us
  starting transfers between devices  20.4 us (48%)
  waiting for transfers between devices  10.7 us (25%)
  Pallas kernels  8.65 us (20%)
  local copies, waits for them, and re-layouts  1.41 us (3%)
  between operations  0.82 us (2%)
    pallas_call x7, Pallas kernels, call(): pl.pallas_call(body, out_shape=out_shape, in_specs=specs, out_specs=jax.t...  8.64 us
    ppermute x2, starting transfers between devices, swap(): return lax.ppermute(array, 'req', [(i, i ^ 1) for i in range(reqs)])  5.44 us
    ppermute x3, starting transfers between devices, along(): return lax.ppermute(array, 'req', [(i, i ^ 2 * by) for i in range(reqs)])  4.45 us
    all_to_all x1, starting transfers between devices, local(): got = lax.all_to_all(pay, ('req', 'tp'), 0, 0, tiled=True)  3.97 us
    all_to_all x1, waiting for transfers between devices, local(): returned = lax.all_to_all(back, ('req', 'tp'), 0, 0, tiled=True)  3.8 us
    ppermute x6, starting transfers between devices, cross(): return lax.ppermute(array, 'tp', [(i, i ^ by) for i in range(tps)])  3.61 us
    all_to_all x1, starting transfers between devices, local(): returned = lax.all_to_all(back, ('req', 'tp'), 0, 0, tiled=True)  2.91 us
    all_to_all x1, waiting for transfers between devices, local(): got = lax.all_to_all(pay, ('req', 'tp'), 0, 0, tiled=True)  2.75 us
  transfers between devices with their start and end apart: 13, of which 6 were waited for; matrix products, arithmetic and copies ran while one was open for 0% of the time, Pallas kernels for 12%

profile of v6, /device:TPU:0, one launch (start us, length us, event | category | flops | bytes accessed | tf_op | source)
XLA Modules:
  0.0 42.0 jit_solution(10711908838534723392)
XLA Ops:
  0.6 2.9 %shard_map.185 = (bf16[128,1024]{1,0:T(8,128)(2,1)}, bf16[32,7,4,128]{3,2,1,0:T(4,128)(2,1)}, bf16[256,512]{1,0:T(8,128)(2,1)}, bf16[256,768]{1,0:T(8,128)(2,1)}, bf16[384,256]{1,0:T(8,128)(2,1)}) custom-call(s32[1,3]{1,0:T(1,128)} %len_ref.1, bf16[128,512]{1,0:T(8,128)(2,1)} %k_hbm.1, bf16[128,512]{1,0:T(8,128)(2,1)} %v_hbm.1, bf16[3,1024]{1,0:T(4,128)(2,1)} %qn_hbm.1, ...), custom_call_target="tpu_custom_call" | custom-call | flops 10000000 | bytes 2516540 | tf_op jit(solution)/shard_map/pallas_call | solution.py:584
  3.6 0.0 copy-start.11
  3.6 3.0 %collective-permute-start.3 = (bf16[256,768]{1,0:T(8,128)(2,1)}, bf16[256,768]{1,0:T(8,128)(2,1)S(1)}, u32[]{:S(2)}, u32[]{:S(2)}) collective-permute-start(bf16[256,768]{1,0:T(8,128)(2,1)} %get-tuple-element.20), channel_id=1, source_target_pairs={{0,4},{4,0},{8,12},{12,8},{16,20},{20,16},{24,28},{28,24},{1,5},{5... | collective-permute-start | bytes 1179656 | tf_op jit(solution)/shard_map/ppermute | solution.py:652
  6.6 1.5 %collective-permute-start.1 = (bf16[256,512]{1,0:T(8,128)(2,1)}, bf16[256,512]{1,0:T(8,128)(2,1)S(1)}, u32[]{:S(2)}, u32[]{:S(2)}) collective-permute-start(bf16[256,512]{1,0:T(8,128)(2,1)} %get-tuple-element.17), channel_id=1, source_target_pairs={{0,2},{1,3},{2,0},{3,1},{4,6},{5,7},{6,4},{7,5},{8,10},{9,11},{10,... | collective-permute-start | bytes 786440 | tf_op jit(solution)/shard_map/ppermute | solution.py:649
  8.1 4.0 %all-to-all-start = ((bf16[32,7,4,128]{3,2,1,0:T(4,128)(2,1)}), bf16[32,7,4,128]{3,2,1,0:T(4,128)(2,1)S(1)}, u32[]{:S(2)}, u32[]{:S(2)}) async-start(bf16[32,7,4,128]{3,2,1,0:T(4,128)(2,1)} %get-tuple-element.16), calls=%async_computation | async-start | bytes 458752 | tf_op jit(solution)/shard_map/all_to_all | solution.py:706
  12.1 0.0 copy-start.1
  12.1 0.0 copy-start.2
  12.1 0.0 copy-start.4
  12.1 0.3 collective-permute-start
  12.5 0.0 copy-done
  12.5 0.6 %copy-done.1 = bf16[256,768]{1,0:T(8,128)(2,1)S(1)} copy-done((bf16[256,768]{1,0:T(8,128)(2,1)S(1)}, bf16[256,768]{1,0:T(8,128)(2,1)}, u32[]{:S(2)}) %copy-start.1) | copy-done | bytes 393240
  13.1 0.1 copy-done.2
  13.2 0.1 shard_map.187
  13.3 1.3 %collective-permute-done.1.w2_ref = bf16[256,512]{1,0:T(8,128)(2,1)S(1)} collective-permute-done((bf16[256,512]{1,0:T(8,128)(2,1)}, bf16[256,512]{1,0:T(8,128)(2,1)S(1)}, u32[]{:S(2)}, u32[]{:S(2)}) %collective-permute-start.1) | collective-permute-done | bytes 262176 | tf_op jit(solution)/shard_map/ppermute | solution.py:649
  14.6 0.0 collective-permute-start.2
  14.6 1.8 %collective-permute-start.9 = (bf16[128,1024]{1,0:T(8,128)(2,1)S(1)}, bf16[128,1024]{1,0:T(8,128)(2,1)S(1)}, u32[]{:S(2)}, u32[]{:S(2)}) collective-permute-start(bf16[128,1024]{1,0:T(8,128)(2,1)S(1)} %copy-done.9), channel_id=1, source_target_pairs={{0,2},{1,3},{2,0},{3,1},{4,6},{5,7},{6,4},{7,5},{8,10},{9,11},{10,... | collective-permute-start | bytes 786440 | tf_op jit(solution)/shard_map/ppermute | solution.py:649
  16.4 0.3 collective-permute-done.3.refs_0_.pair_ref
  16.7 2.4 %collective-permute-start.7 = (bf16[384,256]{1,0:T(8,128)(2,1)S(1)}, bf16[384,256]{1,0:T(8,128)(2,1)S(1)}, u32[]{:S(2)}, u32[]{:S(2)}) collective-permute-start(bf16[384,256]{1,0:T(8,128)(2,1)S(1)} %copy-done.12), channel_id=1, source_target_pairs={{0,4},{4,0},{8,12},{12,8},{16,20},{20,16},{24,28},{28,24},{1,5},{5... | collective-permute-start | bytes 589832 | tf_op jit(solution)/shard_map/ppermute | solution.py:652
  19.2 0.0 collective-permute-done.refs_1_.w1_ref
  19.2 0.0 collective-permute-done.2.refs_2_.w3_ref
  19.2 2.8 %all-to-all-done.pay_ref = bf16[32,7,4,128]{3,2,1,0:T(4,128)(2,1)S(1)} async-done(((bf16[32,7,4,128]{3,2,1,0:T(4,128)(2,1)}), bf16[32,7,4,128]{3,2,1,0:T(4,128)(2,1)S(1)}, u32[]{:S(2)}, u32[]{:S(2)}) %all-to-all-start) | async-done | bytes 229408 | tf_op jit(solution)/shard_map/all_to_all | solution.py:706
  21.9 0.7 %shard_map.190 = (f32[24,512]{1,0:T(8,128)S(1)}, bf16[152,128]{1,0:T(8,128)(2,1)S(1)}) custom-call(bf16[32,7,4,128]{3,2,1,0:T(4,128)(2,1)S(1)} %all-to-all-done.pay_ref, bf16[256,512]{1,0:T(8,128)(2,1)S(1)} %shard_map.186.w0_ref, bf16[256,512]{1,0:T(8,128)(2,1)S(1)} %collective-permute-done.refs_1_.w1_ref, ...), custom_call_target="tpu_custom_call" | custom-call | flops 10000000 | bytes 2070528 | tf_op jit(solution)/shard_map/pallas_call | solution.py:584
  22.6 1.6 %collective-permute-start.4 = (bf16[152,128]{1,0:T(8,128)(2,1)S(1)}, bf16[152,128]{1,0:T(8,128)(2,1)S(1)}, u32[]{:S(2)}, u32[]{:S(2)}) collective-permute-start(bf16[152,128]{1,0:T(8,128)(2,1)S(1)} %get-tuple-element.22.m0_ref), channel_id=1, source_target_pairs={{0,24},{4,28},{8,16},{12,20},{16,8},{20,12},{24,0},{28,4},{1,25},{... | collective-permute-start | bytes 116744 | tf_op jit(solution)/shard_map/ppermute | solution.py:655
  24.2 0.9 %collective-permute-start.5 = (bf16[152,128]{1,0:T(8,128)(2,1)S(1)}, bf16[152,128]{1,0:T(8,128)(2,1)S(1)}, u32[]{:S(2)}, u32[]{:S(2)}) collective-permute-start(bf16[152,128]{1,0:T(8,128)(2,1)S(1)} %get-tuple-element.22.m0_ref), channel_id=1, source_target_pairs={{0,16},{4,20},{8,24},{12,28},{16,0},{20,4},{24,8},{28,12},{1,17},{... | collective-permute-start | bytes 116744 | tf_op jit(solution)/shard_map/ppermute | solution.py:655
  25.2 1.9 %collective-permute-start.6 = (bf16[152,128]{1,0:T(8,128)(2,1)S(1)}, bf16[152,128]{1,0:T(8,128)(2,1)S(1)}, u32[]{:S(2)}, u32[]{:S(2)}) collective-permute-start(bf16[152,128]{1,0:T(8,128)(2,1)S(1)} %get-tuple-element.22.m0_ref), channel_id=1, source_target_pairs={{0,8},{4,12},{8,0},{12,4},{16,24},{20,28},{24,16},{28,20},{1,9},{5... | collective-permute-start | bytes 116744 | tf_op jit(solution)/shard_map/ppermute | solution.py:655
  27.1 0.0 collective-permute-done.9.kv2_ref
  27.1 0.0 collective-permute-start.8
  27.1 1.8 %collective-permute-done.4.m1_ref = bf16[152,128]{1,0:T(8,128)(2,1)S(1)} collective-permute-done((bf16[152,128]{1,0:T(8,128)(2,1)S(1)}, bf16[152,128]{1,0:T(8,128)(2,1)S(1)}, u32[]{:S(2)}, u32[]{:S(2)}) %collective-permute-start.4) | collective-permute-done | bytes 38944 | tf_op jit(solution)/shard_map/ppermute | solution.py:655
  28.8 0.0 collective-permute-start.10
  28.8 0.8 %collective-permute-done.5.m2_ref = bf16[152,128]{1,0:T(8,128)(2,1)S(1)} collective-permute-done((bf16[152,128]{1,0:T(8,128)(2,1)S(1)}, bf16[152,128]{1,0:T(8,128)(2,1)S(1)}, u32[]{:S(2)}, u32[]{:S(2)}) %collective-permute-start.5) | collective-permute-done | bytes 38944 | tf_op jit(solution)/shard_map/ppermute | solution.py:655
  29.6 0.0 collective-permute-done.6.m3_ref
  29.6 0.0 collective-permute-done.7.pair_ref
  29.6 0.0 copy-done.3
  29.6 0.0 copy-start.8
  29.6 1.0 %shard_map.191 = bf16[32,3,4,128]{3,2,1,0:T(4,128)(2,1)} custom-call(bf16[152,128]{1,0:T(8,128)(2,1)S(1)} %get-tuple-element.22.m0_ref, bf16[152,128]{1,0:T(8,128)(2,1)S(1)} %collective-permute-done.4.m1_ref, bf16[152,128]{1,0:T(8,128)(2,1)S(1)} %collective-permute-done.5.m2_ref, bf16[152,128]{1,0:T(8,128)(2,1)S(1)} %collective-permute-done.6.m3_ref, ...), custom_call_target="tpu_custom_call" | custom-call | flops 3000000000 | bytes 794624 | tf_op jit(solution)/shard_map/pallas_call | solution.py:584
  30.6 2.9 %all-to-all-start.1 = ((bf16[32,3,4,128]{3,2,1,0:T(4,128)(2,1)}), bf16[32,3,4,128]{3,2,1,0:T(4,128)(2,1)S(1)}, u32[]{:S(2)}, u32[]{:S(2)}) async-start(bf16[32,3,4,128]{3,2,1,0:T(4,128)(2,1)} %shard_map.191), calls=%async_computation.1 | async-start | bytes 196608 | tf_op jit(solution)/shard_map/all_to_all | solution.py:743
  33.5 0.0 copy-start.5
  33.5 0.0 copy-start.6
  33.5 0.0 copy-start.7
  33.6 0.1 copy.20.g_ref
  33.7 0.0 collective-permute-done.8.kv1_ref
  33.7 0.0 collective-permute-done.10.kv3_ref
  33.7 0.5 %copy-done.5 = s32[1,3]{1,0:T(1,128)S(1)} copy-done((s32[1,3]{1,0:T(1,128)S(1)}, s32[1,3]{1,0:T(1,128)}, u32[]{:S(2)}) %copy-start.5) | copy-done | bytes 36
  34.2 0.0 copy-done.6
  34.2 0.0 copy-done.7
  34.2 3.3 %shard_map.192 = bf16[128,1024]{1,0:T(8,128)(2,1)} custom-call(s32[1,3]{1,0:T(1,128)S(1)} %copy-done.5, bf16[128,1024]{1,0:T(8,128)(2,1)S(1)} %copy-done.8, bf16[128,8]{1,0:T(8,128)(2,1)S(1)} %copy.20.g_ref, bf16[128,1024]{1,0:T(8,128)(2,1)S(1)} %copy-done.9, bf16[128,1024]{1,0:T(8,128)(2,1)S(1)} %collective-permute-done.8.kv1_ref, ...), custom_call_target="tpu_custom_call" | custom-call | flops 1000000000 | bytes 1313804 | tf_op jit(solution)/shard_map/pallas_call | solution.py:584
  37.5 3.8 %all-to-all-done.1.back_ref = bf16[32,3,4,128]{3,2,1,0:T(4,128)(2,1)S(1)} async-done(((bf16[32,3,4,128]{3,2,1,0:T(4,128)(2,1)}), bf16[32,3,4,128]{3,2,1,0:T(4,128)(2,1)S(1)}, u32[]{:S(2)}, u32[]{:S(2)}) %all-to-all-start.1) | async-done | bytes 98336 | tf_op jit(solution)/shard_map/all_to_all | solution.py:743
  41.3 0.7 %shard_map.193 = bf16[3,2048]{1,0:T(4,128)(2,1)} custom-call(bf16[32,3,4,128]{3,2,1,0:T(4,128)(2,1)S(1)} %all-to-all-done.1.back_ref), custom_call_target="tpu_custom_call" | custom-call | flops 1000000 | bytes 98304 | tf_op jit(solution)/shard_map/pallas_call | solution.py:584
  (14 shorter events, 0.1 us)
Async XLA Ops:
  0.6 11.8 %copy-start = (bf16[256,2048]{1,0:T(8,128)(2,1)S(1)}, bf16[256,2048]{1,0:T(8,128)(2,1)}, u32[]{:S(2)}) copy-start(bf16[256,2048]{1,0:T(8,128)(2,1)} %w_hbm.3) | copy-start | bytes 3145732
  3.6 8.5 %copy-start.11 = (bf16[256,512]{1,0:T(8,128)(2,1)S(1)}, bf16[256,512]{1,0:T(8,128)(2,1)}, u32[]{:S(2)}) copy-start(bf16[256,512]{1,0:T(8,128)(2,1)} %get-tuple-element.17) | copy-start | bytes 786436
  3.6 13.1 %collective-permute-start.3 = (bf16[256,768]{1,0:T(8,128)(2,1)}, bf16[256,768]{1,0:T(8,128)(2,1)S(1)}, u32[]{:S(2)}, u32[]{:S(2)}) collective-permute-start(bf16[256,768]{1,0:T(8,128)(2,1)} %get-tuple-element.20), channel_id=1, source_target_pairs={{0,4},{4,0},{8,12},{12,8},{16,20},{20,16},{24,28},{28,24},{1,5},{5... | collective-permute-start | bytes 1179656 | tf_op jit(solution)/shard_map/ppermute | solution.py:652
  6.6 8.0 %collective-permute-start.1 = (bf16[256,512]{1,0:T(8,128)(2,1)}, bf16[256,512]{1,0:T(8,128)(2,1)S(1)}, u32[]{:S(2)}, u32[]{:S(2)}) collective-permute-start(bf16[256,512]{1,0:T(8,128)(2,1)} %get-tuple-element.17), channel_id=1, source_target_pairs={{0,2},{1,3},{2,0},{3,1},{4,6},{5,7},{6,4},{7,5},{8,10},{9,11},{10,... | collective-permute-start | bytes 786440 | tf_op jit(solution)/shard_map/ppermute | solution.py:649
  8.1 13.8 %all-to-all-start = ((bf16[32,7,4,128]{3,2,1,0:T(4,128)(2,1)}), bf16[32,7,4,128]{3,2,1,0:T(4,128)(2,1)S(1)}, u32[]{:S(2)}, u32[]{:S(2)}) async-start(bf16[32,7,4,128]{3,2,1,0:T(4,128)(2,1)} %get-tuple-element.16), calls=%async_computation | async-start | bytes 458752 | tf_op jit(solution)/shard_map/all_to_all | solution.py:706
  12.1 1.0 %copy-start.1 = (bf16[256,768]{1,0:T(8,128)(2,1)S(1)}, bf16[256,768]{1,0:T(8,128)(2,1)}, u32[]{:S(2)}) copy-start(bf16[256,768]{1,0:T(8,128)(2,1)} %gate_hbm.3) | copy-start | bytes 1179652
  12.1 1.1 %copy-start.2 = (bf16[256,768]{1,0:T(8,128)(2,1)S(1)}, bf16[256,768]{1,0:T(8,128)(2,1)}, u32[]{:S(2)}) copy-start(bf16[256,768]{1,0:T(8,128)(2,1)} %up_hbm.3) | copy-start | bytes 1179652
  12.1 1.1 %copy-start.4 = (f32[2048]{0:T(1024)S(1)}, f32[2048]{0:T(1024)}, u32[]{:S(2)}) copy-start(f32[2048]{0:T(1024)} %param.31) | copy-start | bytes 24580
  12.1 7.0 %collective-permute-start = (bf16[256,512]{1,0:T(8,128)(2,1)S(1)}, bf16[256,512]{1,0:T(8,128)(2,1)S(1)}, u32[]{:S(2)}, u32[]{:S(2)}) collective-permute-start(bf16[256,512]{1,0:T(8,128)(2,1)S(1)} %copy-done.11), channel_id=1, source_target_pairs={{0,1},{1,0},{2,3},{3,2},{4,5},{5,4},{6,7},{7,6},{8,9},{9,8},{10,11... | collective-permute-start | bytes 786440 | tf_op jit(solution)/shard_map/ppermute | solution.py:649
  13.2 1.4 %copy-start.9 = (bf16[128,1024]{1,0:T(8,128)(2,1)S(1)}, bf16[128,1024]{1,0:T(8,128)(2,1)}, u32[]{:S(2)}) copy-start(bf16[128,1024]{1,0:T(8,128)(2,1)} %get-tuple-element.27.kv0_ref) | copy-start | bytes 786436
  13.2 3.5 %copy-start.12 = (bf16[384,256]{1,0:T(8,128)(2,1)S(1)}, bf16[384,256]{1,0:T(8,128)(2,1)}, u32[]{:S(2)}) copy-start(bf16[384,256]{1,0:T(8,128)(2,1)} %get-tuple-element.25) | copy-start | bytes 589828
  14.6 4.5 %collective-permute-start.2 = (bf16[256,512]{1,0:T(8,128)(2,1)S(1)}, bf16[256,512]{1,0:T(8,128)(2,1)S(1)}, u32[]{:S(2)}, u32[]{:S(2)}) collective-permute-start(bf16[256,512]{1,0:T(8,128)(2,1)S(1)} %collective-permute-done.1.w2_ref), channel_id=1, source_target_pairs={{0,1},{1,0},{2,3},{3,2},{4,5},{5,4},{6,7},{7,6},{8,9},{9,8},{10,11... | collective-permute-start | bytes 786440 | tf_op jit(solution)/shard_map/ppermute | solution.py:649
  14.6 12.4 %collective-permute-start.9 = (bf16[128,1024]{1,0:T(8,128)(2,1)S(1)}, bf16[128,1024]{1,0:T(8,128)(2,1)S(1)}, u32[]{:S(2)}, u32[]{:S(2)}) collective-permute-start(bf16[128,1024]{1,0:T(8,128)(2,1)S(1)} %copy-done.9), channel_id=1, source_target_pairs={{0,2},{1,3},{2,0},{3,1},{4,6},{5,7},{6,4},{7,5},{8,10},{9,11},{10,... | collective-permute-start | bytes 786440 | tf_op jit(solution)/shard_map/ppermute | solution.py:649
  16.7 12.9 %collective-permute-start.7 = (bf16[384,256]{1,0:T(8,128)(2,1)S(1)}, bf16[384,256]{1,0:T(8,128)(2,1)S(1)}, u32[]{:S(2)}, u32[]{:S(2)}) collective-permute-start(bf16[384,256]{1,0:T(8,128)(2,1)S(1)} %copy-done.12), channel_id=1, source_target_pairs={{0,4},{4,0},{8,12},{12,8},{16,20},{20,16},{24,28},{28,24},{1,5},{5... | collective-permute-start | bytes 589832 | tf_op jit(solution)/shard_map/ppermute | solution.py:652
  21.9 7.7 %copy-start.3 = (bf16[768,256]{1,0:T(8,128)(2,1)S(1)}, bf16[768,256]{1,0:T(8,128)(2,1)}, u32[]{:S(2)}) copy-start(bf16[768,256]{1,0:T(8,128)(2,1)} %down_ref.1) | copy-start | bytes 1179652
  22.6 6.2 %collective-permute-start.4 = (bf16[152,128]{1,0:T(8,128)(2,1)S(1)}, bf16[152,128]{1,0:T(8,128)(2,1)S(1)}, u32[]{:S(2)}, u32[]{:S(2)}) collective-permute-start(bf16[152,128]{1,0:T(8,128)(2,1)S(1)} %get-tuple-element.22.m0_ref), channel_id=1, source_target_pairs={{0,24},{4,28},{8,16},{12,20},{16,8},{20,12},{24,0},{28,4},{1,25},{... | collective-permute-start | bytes 116744 | tf_op jit(solution)/shard_map/ppermute | solution.py:655
  24.2 5.4 %collective-permute-start.5 = (bf16[152,128]{1,0:T(8,128)(2,1)S(1)}, bf16[152,128]{1,0:T(8,128)(2,1)S(1)}, u32[]{:S(2)}, u32[]{:S(2)}) collective-permute-start(bf16[152,128]{1,0:T(8,128)(2,1)S(1)} %get-tuple-element.22.m0_ref), channel_id=1, source_target_pairs={{0,16},{4,20},{8,24},{12,28},{16,0},{20,4},{24,8},{28,12},{1,17},{... | collective-permute-start | bytes 116744 | tf_op jit(solution)/shard_map/ppermute | solution.py:655
  25.2 4.5 %collective-permute-start.6 = (bf16[152,128]{1,0:T(8,128)(2,1)S(1)}, bf16[152,128]{1,0:T(8,128)(2,1)S(1)}, u32[]{:S(2)}, u32[]{:S(2)}) collective-permute-start(bf16[152,128]{1,0:T(8,128)(2,1)S(1)} %get-tuple-element.22.m0_ref), channel_id=1, source_target_pairs={{0,8},{4,12},{8,0},{12,4},{16,24},{20,28},{24,16},{28,20},{1,9},{5... | collective-permute-start | bytes 116744 | tf_op jit(solution)/shard_map/ppermute | solution.py:655
  27.1 6.6 %collective-permute-start.8 = (bf16[128,1024]{1,0:T(8,128)(2,1)S(1)}, bf16[128,1024]{1,0:T(8,128)(2,1)S(1)}, u32[]{:S(2)}, u32[]{:S(2)}) collective-permute-start(bf16[128,1024]{1,0:T(8,128)(2,1)S(1)} %copy-done.9), channel_id=1, source_target_pairs={{0,1},{1,0},{2,3},{3,2},{4,5},{5,4},{6,7},{7,6},{8,9},{9,8},{10,11... | collective-permute-start | bytes 786440 | tf_op jit(solution)/shard_map/ppermute | solution.py:649
  28.8 4.9 %collective-permute-start.10 = (bf16[128,1024]{1,0:T(8,128)(2,1)S(1)}, bf16[128,1024]{1,0:T(8,128)(2,1)S(1)}, u32[]{:S(2)}, u32[]{:S(2)}) collective-permute-start(bf16[128,1024]{1,0:T(8,128)(2,1)S(1)} %collective-permute-done.9.kv2_ref), channel_id=1, source_target_pairs={{0,1},{1,0},{2,3},{3,2},{4,5},{5,4},{6,7},{7,6},{8,9},{9,8},{10,11... | collective-permute-start | bytes 786440 | tf_op jit(solution)/shard_map/ppermute | solution.py:649
  29.6 4.1 %copy-start.8 = (bf16[128,1024]{1,0:T(8,128)(2,1)S(1)}, bf16[128,1024]{1,0:T(8,128)(2,1)}, u32[]{:S(2)}) copy-start(bf16[128,1024]{1,0:T(8,128)(2,1)} %q_ref.1) | copy-start | bytes 786436
  30.6 2.9 %copy-start.10 = (bf16[128,8]{0,1:T(8,128)(2,1)S(1)}, bf16[128,8]{0,1:T(8,128)(2,1)}, u32[]{:S(2)}) copy-start(bf16[128,8]{0,1:T(8,128)(2,1)} %param.19) | copy-start | bytes 6148
  30.6 10.7 %all-to-all-start.1 = ((bf16[32,3,4,128]{3,2,1,0:T(4,128)(2,1)}), bf16[32,3,4,128]{3,2,1,0:T(4,128)(2,1)S(1)}, u32[]{:S(2)}, u32[]{:S(2)}) async-start(bf16[32,3,4,128]{3,2,1,0:T(4,128)(2,1)} %shard_map.191), calls=%async_computation.1 | async-start | bytes 196608 | tf_op jit(solution)/shard_map/all_to_all | solution.py:743
  33.5 0.7 %copy-start.5 = (s32[1,3]{1,0:T(1,128)S(1)}, s32[1,3]{1,0:T(1,128)}, u32[]{:S(2)}) copy-start(s32[1,3]{1,0:T(1,128)} %len_ref.1) | copy-start | bytes 40
  33.5 0.7 %copy-start.6 = (f32[128]{0:T(128)S(1)}, f32[128]{0:T(128)}, u32[]{:S(2)}) copy-start(f32[128]{0:T(128)} %param.22) | copy-start | bytes 1540
  33.5 0.7 %copy-start.7 = (f32[1,128]{1,0:T(1,128)S(1)}, f32[1,128]{1,0:T(1,128)}, u32[]{:S(2)}) copy-start(f32[1,128]{1,0:T(1,128)} %constant.2.clone.freq_hbm.freq_ref) | copy-start | bytes 1540

commit v7 on v6

--- a/solution.py
+++ b/solution.py
@@ -257,16 +257,16 @@
 
 def partial_kernel(
     len_hbm, k_hbm, v_hbm, qn_hbm, kn_hbm, vn_hbm, gn_hbm, resid_hbm, qg_hbm, kg_hbm, freq_hbm,
-    w_hbm, gate_hbm, up_hbm, down_hbm,
-    kv_hbm, pay_hbm, own_hbm, pair_hbm, down_pair_hbm,
-    kv_ref, pay_ref, own_ref, pair_ref, down_pair_ref, row_q, row_k, row_v, row_g, pay, len_ref, k_ref, v_ref, qn_ref, kn_ref, vn_ref, gn_ref,
+    w_hbm, gate_hbm, up_hbm,
+    kv_hbm, pay_hbm, own_hbm, pair_hbm,
+    kv_ref, pay_ref, own_ref, pair_ref, row_q, row_k, row_v, row_g, pay, len_ref, k_ref, v_ref, qn_ref, kn_ref, vn_ref, gn_ref,
     resid_ref, qg_ref, kg_ref, freq_ref, sems, out_sems,
 ):
     tp = lax.axis_index("tp")
     req = lax.axis_index("req")
     z, other = lax.div(req, 2), 1 - lax.rem(req, 2)
     width = own_ref.shape[1]
-    units = down_pair_ref.shape[0]
+    units = pair_ref.shape[1] // 2
     cols = pl.ds(pl.multiple_of(z * width, lanes), width)
     theirs = pl.ds(pl.multiple_of(other * units, lanes), units)
     moves = (
@@ -276,14 +276,12 @@
         (gate_hbm.at[:, theirs], pair_ref.at[:, pl.ds(0, units)]),
         (up_hbm.at[:, theirs], pair_ref.at[:, pl.ds(units, units)]),
         (w_hbm.at[:, cols], own_ref),
-        (down_hbm.at[theirs, :], down_pair_ref),
     )
     copies = [pltpu.make_async_copy(a, b, sems.at[i]) for i, (a, b) in enumerate(moves)]
     for copy in copies:
         copy.start()
     ends = (
-        (pair_ref, pair_hbm), (own_ref, own_hbm), (down_pair_ref, down_pair_hbm),
-        (kv_ref, kv_hbm), (pay_ref, pay_hbm),
+        (pair_ref, pair_hbm), (own_ref, own_hbm), (kv_ref, kv_hbm), (pay_ref, pay_hbm),
     )
     leave = [pltpu.make_async_copy(a, b, out_sems.at[i]) for i, (a, b) in enumerate(ends)]
     tok = k_ref.shape[0]
@@ -308,7 +306,7 @@
     kv_ref[:, kvs * lanes :] = v_ref[...]
     for copy in copies[11:]:
         copy.wait()
-    for copy in leave[:4]:
+    for copy in leave[:3]:
         copy.start()
     qn, kn = qn_ref[...].astype(f32), kn_ref[...].astype(f32)
     vn, gn = vn_ref[...].astype(f32), gn_ref[...].astype(f32)
@@ -372,7 +370,7 @@
             out = pay[4 * g : 4 * g + 4, :].astype(bf16)
             for peer in range(z * peers // slices, (z + 1) * peers // slices):
                 pay_ref[peer, g] = out
-    leave[4].start()
+    leave[3].start()
     for copy in leave:
         copy.wait()
 
@@ -394,14 +392,20 @@
         copy.wait()
 
 
-def columns_kernel(w_hbm, w_ref, sems):
+def columns_kernel(w_hbm, down_hbm, w_ref, down_ref, sems):
     width = w_ref.shape[1]
-    z = lax.div(lax.axis_index("req"), 2)
-    copy = pltpu.make_async_copy(
-        w_hbm.at[:, pl.ds(pl.multiple_of(z * width, lanes), width)], w_ref, sems.at[0]
-    )
-    copy.start()
-    copy.wait()
+    units = down_ref.shape[0]
+    req = lax.axis_index("req")
+    cols = pl.ds(pl.multiple_of(lax.div(req, 2) * width, lanes), width)
+    theirs = pl.ds(pl.multiple_of((1 - lax.rem(req, 2)) * units, lanes), units)
+    copies = (
+        pltpu.make_async_copy(w_hbm.at[:, cols], w_ref, sems.at[0]),
+        pltpu.make_async_copy(down_hbm.at[theirs, :], down_ref, sems.at[1]),
+    )
+    for copy in copies:
+        copy.start()
+    for copy in copies:
+        copy.wait()
 
 
 def ready_kernel(*refs):
@@ -474,7 +478,7 @@
     msg_ref[...] = out[...].astype(bf16)
 
 
-def down_kernel(m0_ref, m1_ref, m2_ref, m3_ref, hid_ref, down_ref, pair_ref, back_ref, part, pay, whole):
+def down_kernel(m0_ref, m1_ref, m2_ref, m3_ref, hid_ref, down_ref, pair_ref, back_ref, pay, whole):
     tp = lax.axis_index("tp")
     tps = lax.axis_size("tp")
     y = lax.rem(lax.axis_index("req"), 2)
@@ -499,8 +503,8 @@
         pieces.append((gate / (1.0 + jnp.exp(-gate)) * up).astype(bf16))
     hidden = jnp.concatenate(pieces, axis=1)
     own_rows = pl.ds(pl.multiple_of(y * units, lanes), units)
-    part[y] = dot(hidden, down_ref[own_rows, :])
-    part[1 - y] = dot(hidden, pair_ref[...])
+    mine, theirs = dot(hidden, down_ref[own_rows, :]), dot(hidden, pair_ref[...])
+    part = (jnp.where(y == 0, mine, theirs), jnp.where(y == 0, theirs, mine))
     chunks = width // lanes
     groups = pay.shape[0]
     rpg = toks // groups
@@ -656,16 +660,15 @@
 
     inputs = (
         lengths, k_pre, v_pre, q_new, k_new, v_new, gate_new, resid, qg, kg, freqs,
-        w_out, w_gate, w_up, w_down,
+        w_out, w_gate, w_up,
     )
     outputs = (
         jax.ShapeDtypeStruct((tok, 2 * k_pre.shape[1]), bf16),
         jax.ShapeDtypeStruct((peers, pay_rows // 4, 4, lanes), bf16),
         jax.ShapeDtypeStruct((w_out.shape[0], part), bf16),
         jax.ShapeDtypeStruct((w_gate.shape[0], 2 * units), bf16),
-        jax.ShapeDtypeStruct((units, w_down.shape[1]), bf16),
-    )
-    kv, pay, w_own, pair, down_pair = call(
+    )
+    kv, pay, w_own, pair = call(
         partial_kernel,
         outputs,
         inputs,
@@ -689,12 +692,15 @@
         hbm=True,
         scratch=[pltpu.SemaphoreType.DMA((3,))],
     )
-    w_here = call(
+    w_here, down_pair = call(
         columns_kernel,
-        jax.ShapeDtypeStruct(w_own.shape, bf16),
-        (w_out,),
+        (
+            jax.ShapeDtypeStruct(w_own.shape, bf16),
+            jax.ShapeDtypeStruct((units, w_down.shape[1]), bf16),
+        ),
+        (w_out, w_down),
         hbm=True,
-        scratch=[pltpu.SemaphoreType.DMA((1,))],
+        scratch=[pltpu.SemaphoreType.DMA((2,))],
     )
     late_far, _, _ = lax.optimization_barrier((w_far, mine, w_here))
     w_near, w_both = cross(w_own, 1), cross(late_far, 1)
@@ -737,7 +743,7 @@
         down_kernel,
         jax.ShapeDtypeStruct((peers, back_rows // 4, 4, lanes), bf16),
         (*msgs, hid, w_down, down_pair),
-        scratch=[(2, toks, part // 2), (reqs, back_rows, lanes), msg_shape],
+        scratch=[(reqs, back_rows, lanes), msg_shape],
         flops=3 * 10**9,
     )
     returned = lax.all_to_all(back, ("req", "tp"), 0, 0, tiled=True)

time: 42.3 us -> 42.2 us (level)
    unnamed x27 -> x23, local copies, waits for them, and re-layouts: 1.41 us -> 1.14 us
  transfers between devices with their start and end apart: 13 -> 13, of which waited for: 6 -> 6; matrix products, arithmetic and copies ran while one was open for 0% -> 0% of each run, Pallas kernels for 12% -> 13%
where the time goes in v7:
time: 42.2 us; the launch traced here: 41.9 us
  starting transfers between devices  20.4 us (48%)
  waiting for transfers between devices  10.7 us (25%)
  Pallas kernels  8.85 us (21%)
  local copies, waits for them, and re-layouts  1.14 us (3%)
  between operations  0.8 us (2%)
    pallas_call x7, Pallas kernels, call(): pl.pallas_call(body, out_shape=out_shape, in_specs=specs, out_specs=jax.t...  8.85 us
    ppermute x2, starting transfers between devices, swap(): return lax.ppermute(array, 'req', [(i, i ^ 1) for i in range(reqs)])  5.44 us
    ppermute x3, starting transfers between devices, along(): return lax.ppermute(array, 'req', [(i, i ^ 2 * by) for i in range(reqs)])  4.45 us
    all_to_all x1, starting transfers between devices, local(): got = lax.all_to_all(pay, ('req', 'tp'), 0, 0, tiled=True)  3.97 us
    all_to_all x1, waiting for transfers between devices, local(): returned = lax.all_to_all(back, ('req', 'tp'), 0, 0, tiled=True)  3.78 us
    ppermute x6, starting transfers between devices, cross(): return lax.ppermute(array, 'tp', [(i, i ^ by) for i in range(tps)])  3.61 us
    all_to_all x1, starting transfers between devices, local(): returned = lax.all_to_all(back, ('req', 'tp'), 0, 0, tiled=True)  2.9 us
    all_to_all x1, waiting for transfers between devices, local(): got = lax.all_to_all(pay, ('req', 'tp'), 0, 0, tiled=True)  2.75 us
  transfers between devices with their start and end apart: 13, of which 6 were waited for; matrix products, arithmetic and copies ran while one was open for 0% of the time, Pallas kernels for 13%

profile of v7, /device:TPU:0, one launch (start us, length us, event | category | flops | bytes accessed | tf_op | source)
XLA Modules:
  0.0 41.9 jit_solution(4620060098306036110)
XLA Ops:
  0.6 0.0 copy-start
  0.6 2.9 %shard_map.185 = (bf16[128,1024]{1,0:T(8,128)(2,1)}, bf16[32,7,4,128]{3,2,1,0:T(4,128)(2,1)}, bf16[256,512]{1,0:T(8,128)(2,1)}, bf16[256,768]{1,0:T(8,128)(2,1)}) custom-call(s32[1,3]{1,0:T(1,128)} %len_ref.1, bf16[128,512]{1,0:T(8,128)(2,1)} %k_hbm.1, bf16[128,512]{1,0:T(8,128)(2,1)} %v_hbm.1, bf16[3,1024]{1,0:T(4,128)(2,1)} %qn_hbm.1, ...), custom_call_target="tpu_custom_call" | custom-call | flops 10000000 | bytes 2123324 | tf_op jit(solution)/shard_map/pallas_call | solution.py:588
  3.6 0.0 copy-start.3
  3.6 3.0 %collective-permute-start.3 = (bf16[256,768]{1,0:T(8,128)(2,1)}, bf16[256,768]{1,0:T(8,128)(2,1)S(1)}, u32[]{:S(2)}, u32[]{:S(2)}) collective-permute-start(bf16[256,768]{1,0:T(8,128)(2,1)} %get-tuple-element.22), channel_id=1, source_target_pairs={{0,4},{4,0},{8,12},{12,8},{16,20},{20,16},{24,28},{28,24},{1,5},{5... | collective-permute-start | bytes 1179656 | tf_op jit(solution)/shard_map/ppermute | solution.py:656
  6.6 1.5 %collective-permute-start.1 = (bf16[256,512]{1,0:T(8,128)(2,1)}, bf16[256,512]{1,0:T(8,128)(2,1)S(1)}, u32[]{:S(2)}, u32[]{:S(2)}) collective-permute-start(bf16[256,512]{1,0:T(8,128)(2,1)} %get-tuple-element.19), channel_id=1, source_target_pairs={{0,2},{1,3},{2,0},{3,1},{4,6},{5,7},{6,4},{7,5},{8,10},{9,11},{10,... | collective-permute-start | bytes 786440 | tf_op jit(solution)/shard_map/ppermute | solution.py:653
  8.1 4.0 %all-to-all-start = ((bf16[32,7,4,128]{3,2,1,0:T(4,128)(2,1)}), bf16[32,7,4,128]{3,2,1,0:T(4,128)(2,1)S(1)}, u32[]{:S(2)}, u32[]{:S(2)}) async-start(bf16[32,7,4,128]{3,2,1,0:T(4,128)(2,1)} %get-tuple-element.17), calls=%async_computation | async-start | bytes 458752 | tf_op jit(solution)/shard_map/all_to_all | solution.py:712
  12.1 0.0 copy-start.1
  12.1 0.0 copy-start.2
  12.1 0.0 copy-start.4
  12.1 0.3 collective-permute-start
  12.4 0.0 copy-done
  12.4 0.3 shard_map.186
  12.7 0.3 copy-done.1
  13.1 0.1 copy-done.2
  13.2 0.1 shard_map.187
  13.3 1.3 %collective-permute-done.1.w2_ref = bf16[256,512]{1,0:T(8,128)(2,1)S(1)} collective-permute-done((bf16[256,512]{1,0:T(8,128)(2,1)}, bf16[256,512]{1,0:T(8,128)(2,1)S(1)}, u32[]{:S(2)}, u32[]{:S(2)}) %collective-permute-start.1) | collective-permute-done | bytes 262176 | tf_op jit(solution)/shard_map/ppermute | solution.py:653
  14.6 0.0 collective-permute-start.2
  14.6 1.8 %collective-permute-start.9 = (bf16[128,1024]{1,0:T(8,128)(2,1)S(1)}, bf16[128,1024]{1,0:T(8,128)(2,1)S(1)}, u32[]{:S(2)}, u32[]{:S(2)}) collective-permute-start(bf16[128,1024]{1,0:T(8,128)(2,1)S(1)} %copy-done.9), channel_id=1, source_target_pairs={{0,2},{1,3},{2,0},{3,1},{4,6},{5,7},{6,4},{7,5},{8,10},{9,11},{10,... | collective-permute-start | bytes 786440 | tf_op jit(solution)/shard_map/ppermute | solution.py:653
  16.4 0.3 collective-permute-done.3.refs_0_.pair_ref
  16.7 2.4 %collective-permute-start.7 = (bf16[384,256]{1,0:T(8,128)(2,1)S(1)}, bf16[384,256]{1,0:T(8,128)(2,1)S(1)}, u32[]{:S(2)}, u32[]{:S(2)}) collective-permute-start(bf16[384,256]{1,0:T(8,128)(2,1)S(1)} %get-tuple-element.27), channel_id=1, source_target_pairs={{0,4},{4,0},{8,12},{12,8},{16,20},{20,16},{24,28},{28,24},{1,5},{5... | collective-permute-start | bytes 589832 | tf_op jit(solution)/shard_map/ppermute | solution.py:656
  19.1 0.0 collective-permute-done.refs_1_.w1_ref
  19.1 0.0 collective-permute-done.2.refs_2_.w3_ref
  19.1 2.8 %all-to-all-done.pay_ref = bf16[32,7,4,128]{3,2,1,0:T(4,128)(2,1)S(1)} async-done(((bf16[32,7,4,128]{3,2,1,0:T(4,128)(2,1)}), bf16[32,7,4,128]{3,2,1,0:T(4,128)(2,1)S(1)}, u32[]{:S(2)}, u32[]{:S(2)}) %all-to-all-start) | async-done | bytes 229408 | tf_op jit(solution)/shard_map/all_to_all | solution.py:712
  21.9 0.7 %shard_map.190 = (f32[24,512]{1,0:T(8,128)S(1)}, bf16[152,128]{1,0:T(8,128)(2,1)S(1)}) custom-call(bf16[32,7,4,128]{3,2,1,0:T(4,128)(2,1)S(1)} %all-to-all-done.pay_ref, bf16[256,512]{1,0:T(8,128)(2,1)S(1)} %get-tuple-element.18.w0_ref, bf16[256,512]{1,0:T(8,128)(2,1)S(1)} %collective-permute-done.refs_1_.w1_ref, ...), custom_call_target="tpu_custom_call" | custom-call | flops 10000000 | bytes 2070528 | tf_op jit(solution)/shard_map/pallas_call | solution.py:588
  22.6 1.6 %collective-permute-start.4 = (bf16[152,128]{1,0:T(8,128)(2,1)S(1)}, bf16[152,128]{1,0:T(8,128)(2,1)S(1)}, u32[]{:S(2)}, u32[]{:S(2)}) collective-permute-start(bf16[152,128]{1,0:T(8,128)(2,1)S(1)} %get-tuple-element.24.m0_ref), channel_id=1, source_target_pairs={{0,24},{4,28},{8,16},{12,20},{16,8},{20,12},{24,0},{28,4},{1,25},{... | collective-permute-start | bytes 116744 | tf_op jit(solution)/shard_map/ppermute | solution.py:659
  24.2 0.9 %collective-permute-start.5 = (bf16[152,128]{1,0:T(8,128)(2,1)S(1)}, bf16[152,128]{1,0:T(8,128)(2,1)S(1)}, u32[]{:S(2)}, u32[]{:S(2)}) collective-permute-start(bf16[152,128]{1,0:T(8,128)(2,1)S(1)} %get-tuple-element.24.m0_ref), channel_id=1, source_target_pairs={{0,16},{4,20},{8,24},{12,28},{16,0},{20,4},{24,8},{28,12},{1,17},{... | collective-permute-start | bytes 116744 | tf_op jit(solution)/shard_map/ppermute | solution.py:659
  25.1 1.9 %collective-permute-start.6 = (bf16[152,128]{1,0:T(8,128)(2,1)S(1)}, bf16[152,128]{1,0:T(8,128)(2,1)S(1)}, u32[]{:S(2)}, u32[]{:S(2)}) collective-permute-start(bf16[152,128]{1,0:T(8,128)(2,1)S(1)} %get-tuple-element.24.m0_ref), channel_id=1, source_target_pairs={{0,8},{4,12},{8,0},{12,4},{16,24},{20,28},{24,16},{28,20},{1,9},{5... | collective-permute-start | bytes 116744 | tf_op jit(solution)/shard_map/ppermute | solution.py:659
  27.0 0.0 collective-permute-done.9.kv2_ref
  27.0 0.0 collective-permute-start.8
  27.0 1.8 %collective-permute-done.4.m1_ref = bf16[152,128]{1,0:T(8,128)(2,1)S(1)} collective-permute-done((bf16[152,128]{1,0:T(8,128)(2,1)S(1)}, bf16[152,128]{1,0:T(8,128)(2,1)S(1)}, u32[]{:S(2)}, u32[]{:S(2)}) %collective-permute-start.4) | collective-permute-done | bytes 38944 | tf_op jit(solution)/shard_map/ppermute | solution.py:659
  28.8 0.0 collective-permute-start.10
  28.8 0.8 %collective-permute-done.5.m2_ref = bf16[152,128]{1,0:T(8,128)(2,1)S(1)} collective-permute-done((bf16[152,128]{1,0:T(8,128)(2,1)S(1)}, bf16[152,128]{1,0:T(8,128)(2,1)S(1)}, u32[]{:S(2)}, u32[]{:S(2)}) %collective-permute-start.5) | collective-permute-done | bytes 38944 | tf_op jit(solution)/shard_map/ppermute | solution.py:659
  29.6 0.0 collective-permute-done.6.m3_ref
  29.6 0.0 collective-permute-done.7.pair_ref
  29.6 0.9 %shard_map.191 = bf16[32,3,4,128]{3,2,1,0:T(4,128)(2,1)} custom-call(bf16[152,128]{1,0:T(8,128)(2,1)S(1)} %get-tuple-element.24.m0_ref, bf16[152,128]{1,0:T(8,128)(2,1)S(1)} %collective-permute-done.4.m1_ref, bf16[152,128]{1,0:T(8,128)(2,1)S(1)} %collective-permute-done.5.m2_ref, bf16[152,128]{1,0:T(8,128)(2,1)S(1)} %collective-permute-done.6.m3_ref, ...), custom_call_target="tpu_custom_call" | custom-call | flops 3000000000 | bytes 794624 | tf_op jit(solution)/shard_map/pallas_call | solution.py:588
  30.5 2.9 %all-to-all-start.1 = ((bf16[32,3,4,128]{3,2,1,0:T(4,128)(2,1)}), bf16[32,3,4,128]{3,2,1,0:T(4,128)(2,1)S(1)}, u32[]{:S(2)}, u32[]{:S(2)}) async-start(bf16[32,3,4,128]{3,2,1,0:T(4,128)(2,1)} %shard_map.191), calls=%async_computation.1 | async-start | bytes 196608 | tf_op jit(solution)/shard_map/all_to_all | solution.py:749
  33.4 0.0 copy-start.5
  33.4 0.0 copy-start.6
  33.5 0.0 copy-start.7
  33.5 0.1 copy.20.g_ref
  33.6 0.0 collective-permute-done.8.kv1_ref
  33.6 0.0 collective-permute-done.10.kv3_ref
  33.6 0.5 %copy-done.5 = s32[1,3]{1,0:T(1,128)S(1)} copy-done((s32[1,3]{1,0:T(1,128)S(1)}, s32[1,3]{1,0:T(1,128)}, u32[]{:S(2)}) %copy-start.5) | copy-done | bytes 36
  34.1 0.0 copy-done.6
  34.1 0.0 copy-done.7
  34.1 3.3 %shard_map.192 = bf16[128,1024]{1,0:T(8,128)(2,1)} custom-call(s32[1,3]{1,0:T(1,128)S(1)} %copy-done.5, bf16[128,1024]{1,0:T(8,128)(2,1)S(1)} %copy-done.8, bf16[128,8]{1,0:T(8,128)(2,1)S(1)} %copy.20.g_ref, bf16[128,1024]{1,0:T(8,128)(2,1)S(1)} %copy-done.9, bf16[128,1024]{1,0:T(8,128)(2,1)S(1)} %collective-permute-done.8.kv1_ref, ...), custom_call_target="tpu_custom_call" | custom-call | flops 1000000000 | bytes 1313804 | tf_op jit(solution)/shard_map/pallas_call | solution.py:588
  37.5 3.8 %all-to-all-done.1.back_ref = bf16[32,3,4,128]{3,2,1,0:T(4,128)(2,1)S(1)} async-done(((bf16[32,3,4,128]{3,2,1,0:T(4,128)(2,1)}), bf16[32,3,4,128]{3,2,1,0:T(4,128)(2,1)S(1)}, u32[]{:S(2)}, u32[]{:S(2)}) %all-to-all-start.1) | async-done | bytes 98336 | tf_op jit(solution)/shard_map/all_to_all | solution.py:749
  41.2 0.7 %shard_map.193 = bf16[3,2048]{1,0:T(4,128)(2,1)} custom-call(bf16[32,3,4,128]{3,2,1,0:T(4,128)(2,1)S(1)} %all-to-all-done.1.back_ref), custom_call_target="tpu_custom_call" | custom-call | flops 1000000 | bytes 98304 | tf_op jit(solution)/shard_map/pallas_call | solution.py:588
  (10 shorter events, 0.0 us)
Async XLA Ops:
  0.6 11.8 %copy-start = (bf16[256,2048]{1,0:T(8,128)(2,1)S(1)}, bf16[256,2048]{1,0:T(8,128)(2,1)}, u32[]{:S(2)}) copy-start(bf16[256,2048]{1,0:T(8,128)(2,1)} %w_hbm.3) | copy-start | bytes 3145732
  3.6 8.9 %copy-start.3 = (bf16[768,256]{1,0:T(8,128)(2,1)S(1)}, bf16[768,256]{1,0:T(8,128)(2,1)}, u32[]{:S(2)}) copy-start(bf16[768,256]{1,0:T(8,128)(2,1)} %down_ref.1) | copy-start | bytes 1179652
  3.6 13.1 %collective-permute-start.3 = (bf16[256,768]{1,0:T(8,128)(2,1)}, bf16[256,768]{1,0:T(8,128)(2,1)S(1)}, u32[]{:S(2)}, u32[]{:S(2)}) collective-permute-start(bf16[256,768]{1,0:T(8,128)(2,1)} %get-tuple-element.22), channel_id=1, source_target_pairs={{0,4},{4,0},{8,12},{12,8},{16,20},{20,16},{24,28},{28,24},{1,5},{5... | collective-permute-start | bytes 1179656 | tf_op jit(solution)/shard_map/ppermute | solution.py:656
  6.6 8.0 %collective-permute-start.1 = (bf16[256,512]{1,0:T(8,128)(2,1)}, bf16[256,512]{1,0:T(8,128)(2,1)S(1)}, u32[]{:S(2)}, u32[]{:S(2)}) collective-permute-start(bf16[256,512]{1,0:T(8,128)(2,1)} %get-tuple-element.19), channel_id=1, source_target_pairs={{0,2},{1,3},{2,0},{3,1},{4,6},{5,7},{6,4},{7,5},{8,10},{9,11},{10,... | collective-permute-start | bytes 786440 | tf_op jit(solution)/shard_map/ppermute | solution.py:653
  8.1 13.8 %all-to-all-start = ((bf16[32,7,4,128]{3,2,1,0:T(4,128)(2,1)}), bf16[32,7,4,128]{3,2,1,0:T(4,128)(2,1)S(1)}, u32[]{:S(2)}, u32[]{:S(2)}) async-start(bf16[32,7,4,128]{3,2,1,0:T(4,128)(2,1)} %get-tuple-element.17), calls=%async_computation | async-start | bytes 458752 | tf_op jit(solution)/shard_map/all_to_all | solution.py:712
  12.1 1.0 %copy-start.1 = (bf16[256,768]{1,0:T(8,128)(2,1)S(1)}, bf16[256,768]{1,0:T(8,128)(2,1)}, u32[]{:S(2)}) copy-start(bf16[256,768]{1,0:T(8,128)(2,1)} %gate_hbm.3) | copy-start | bytes 1179652
  12.1 1.1 %copy-start.2 = (bf16[256,768]{1,0:T(8,128)(2,1)S(1)}, bf16[256,768]{1,0:T(8,128)(2,1)}, u32[]{:S(2)}) copy-start(bf16[256,768]{1,0:T(8,128)(2,1)} %up_hbm.3) | copy-start | bytes 1179652
  12.1 1.1 %copy-start.4 = (f32[2048]{0:T(1024)S(1)}, f32[2048]{0:T(1024)}, u32[]{:S(2)}) copy-start(f32[2048]{0:T(1024)} %param.31) | copy-start | bytes 24580
  12.1 7.0 %collective-permute-start = (bf16[256,512]{1,0:T(8,128)(2,1)}, bf16[256,512]{1,0:T(8,128)(2,1)S(1)}, u32[]{:S(2)}, u32[]{:S(2)}) collective-permute-start(bf16[256,512]{1,0:T(8,128)(2,1)} %get-tuple-element.19), channel_id=1, source_target_pairs={{0,1},{1,0},{2,3},{3,2},{4,5},{5,4},{6,7},{7,6},{8,9},{9,8},{10,11... | collective-permute-start | bytes 786440 | tf_op jit(solution)/shard_map/ppermute | solution.py:653
  13.2 1.4 %copy-start.9 = (bf16[128,1024]{1,0:T(8,128)(2,1)S(1)}, bf16[128,1024]{1,0:T(8,128)(2,1)}, u32[]{:S(2)}) copy-start(bf16[128,1024]{1,0:T(8,128)(2,1)} %get-tuple-element.29.kv0_ref) | copy-start | bytes 786436
  14.6 4.5 %collective-permute-start.2 = (bf16[256,512]{1,0:T(8,128)(2,1)S(1)}, bf16[256,512]{1,0:T(8,128)(2,1)S(1)}, u32[]{:S(2)}, u32[]{:S(2)}) collective-permute-start(bf16[256,512]{1,0:T(8,128)(2,1)S(1)} %collective-permute-done.1.w2_ref), channel_id=1, source_target_pairs={{0,1},{1,0},{2,3},{3,2},{4,5},{5,4},{6,7},{7,6},{8,9},{9,8},{10,11... | collective-permute-start | bytes 786440 | tf_op jit(solution)/shard_map/ppermute | solution.py:653
  14.6 12.4 %collective-permute-start.9 = (bf16[128,1024]{1,0:T(8,128)(2,1)S(1)}, bf16[128,1024]{1,0:T(8,128)(2,1)S(1)}, u32[]{:S(2)}, u32[]{:S(2)}) collective-permute-start(bf16[128,1024]{1,0:T(8,128)(2,1)S(1)} %copy-done.9), channel_id=1, source_target_pairs={{0,2},{1,3},{2,0},{3,1},{4,6},{5,7},{6,4},{7,5},{8,10},{9,11},{10,... | collective-permute-start | bytes 786440 | tf_op jit(solution)/shard_map/ppermute | solution.py:653
  16.7 12.9 %collective-permute-start.7 = (bf16[384,256]{1,0:T(8,128)(2,1)S(1)}, bf16[384,256]{1,0:T(8,128)(2,1)S(1)}, u32[]{:S(2)}, u32[]{:S(2)}) collective-permute-start(bf16[384,256]{1,0:T(8,128)(2,1)S(1)} %get-tuple-element.27), channel_id=1, source_target_pairs={{0,4},{4,0},{8,12},{12,8},{16,20},{20,16},{24,28},{28,24},{1,5},{5... | collective-permute-start | bytes 589832 | tf_op jit(solution)/shard_map/ppermute | solution.py:656
  22.6 6.2 %collective-permute-start.4 = (bf16[152,128]{1,0:T(8,128)(2,1)S(1)}, bf16[152,128]{1,0:T(8,128)(2,1)S(1)}, u32[]{:S(2)}, u32[]{:S(2)}) collective-permute-start(bf16[152,128]{1,0:T(8,128)(2,1)S(1)} %get-tuple-element.24.m0_ref), channel_id=1, source_target_pairs={{0,24},{4,28},{8,16},{12,20},{16,8},{20,12},{24,0},{28,4},{1,25},{... | collective-permute-start | bytes 116744 | tf_op jit(solution)/shard_map/ppermute | solution.py:659
  24.2 5.4 %collective-permute-start.5 = (bf16[152,128]{1,0:T(8,128)(2,1)S(1)}, bf16[152,128]{1,0:T(8,128)(2,1)S(1)}, u32[]{:S(2)}, u32[]{:S(2)}) collective-permute-start(bf16[152,128]{1,0:T(8,128)(2,1)S(1)} %get-tuple-element.24.m0_ref), channel_id=1, source_target_pairs={{0,16},{4,20},{8,24},{12,28},{16,0},{20,4},{24,8},{28,12},{1,17},{... | collective-permute-start | bytes 116744 | tf_op jit(solution)/shard_map/ppermute | solution.py:659
  25.1 4.5 %collective-permute-start.6 = (bf16[152,128]{1,0:T(8,128)(2,1)S(1)}, bf16[152,128]{1,0:T(8,128)(2,1)S(1)}, u32[]{:S(2)}, u32[]{:S(2)}) collective-permute-start(bf16[152,128]{1,0:T(8,128)(2,1)S(1)} %get-tuple-element.24.m0_ref), channel_id=1, source_target_pairs={{0,8},{4,12},{8,0},{12,4},{16,24},{20,28},{24,16},{28,20},{1,9},{5... | collective-permute-start | bytes 116744 | tf_op jit(solution)/shard_map/ppermute | solution.py:659
  27.0 6.6 %collective-permute-start.8 = (bf16[128,1024]{1,0:T(8,128)(2,1)S(1)}, bf16[128,1024]{1,0:T(8,128)(2,1)S(1)}, u32[]{:S(2)}, u32[]{:S(2)}) collective-permute-start(bf16[128,1024]{1,0:T(8,128)(2,1)S(1)} %copy-done.9), channel_id=1, source_target_pairs={{0,1},{1,0},{2,3},{3,2},{4,5},{5,4},{6,7},{7,6},{8,9},{9,8},{10,11... | collective-permute-start | bytes 786440 | tf_op jit(solution)/shard_map/ppermute | solution.py:653
  28.8 4.8 %collective-permute-start.10 = (bf16[128,1024]{1,0:T(8,128)(2,1)S(1)}, bf16[128,1024]{1,0:T(8,128)(2,1)S(1)}, u32[]{:S(2)}, u32[]{:S(2)}) collective-permute-start(bf16[128,1024]{1,0:T(8,128)(2,1)S(1)} %collective-permute-done.9.kv2_ref), channel_id=1, source_target_pairs={{0,1},{1,0},{2,3},{3,2},{4,5},{5,4},{6,7},{7,6},{8,9},{9,8},{10,11... | collective-permute-start | bytes 786440 | tf_op jit(solution)/shard_map/ppermute | solution.py:653
  29.6 4.0 %copy-start.8 = (bf16[128,1024]{1,0:T(8,128)(2,1)S(1)}, bf16[128,1024]{1,0:T(8,128)(2,1)}, u32[]{:S(2)}) copy-start(bf16[128,1024]{1,0:T(8,128)(2,1)} %q_ref.1) | copy-start | bytes 786436
  30.5 2.9 %copy-start.10 = (bf16[128,8]{0,1:T(8,128)(2,1)S(1)}, bf16[128,8]{0,1:T(8,128)(2,1)}, u32[]{:S(2)}) copy-start(bf16[128,8]{0,1:T(8,128)(2,1)} %param.19) | copy-start | bytes 6148
  30.5 10.7 %all-to-all-start.1 = ((bf16[32,3,4,128]{3,2,1,0:T(4,128)(2,1)}), bf16[32,3,4,128]{3,2,1,0:T(4,128)(2,1)S(1)}, u32[]{:S(2)}, u32[]{:S(2)}) async-start(bf16[32,3,4,128]{3,2,1,0:T(4,128)(2,1)} %shard_map.191), calls=%async_computation.1 | async-start | bytes 196608 | tf_op jit(solution)/shard_map/all_to_all | solution.py:749
  33.4 0.7 %copy-start.5 = (s32[1,3]{1,0:T(1,128)S(1)}, s32[1,3]{1,0:T(1,128)}, u32[]{:S(2)}) copy-start(s32[1,3]{1,0:T(1,128)} %len_ref.1) | copy-start | bytes 40
  33.4 0.7 %copy-start.6 = (f32[128]{0:T(128)S(1)}, f32[128]{0:T(128)}, u32[]{:S(2)}) copy-start(f32[128]{0:T(128)} %param.22) | copy-start | bytes 1540
  33.5 0.7 %copy-start.7 = (f32[1,128]{1,0:T(1,128)S(1)}, f32[1,128]{1,0:T(1,128)}, u32[]{:S(2)}) copy-start(f32[1,128]{1,0:T(1,128)} %constant.2.clone.freq_hbm.freq_ref) | copy-start | bytes 1540

commit v8 on v7

--- a/solution.py
+++ b/solution.py
@@ -333,8 +333,8 @@
         last = jnp.where(mine, end, last)
     new_factors = rope_factors(length.astype(f32) * freq)
     scale = lanes ** (-0.5)
-    new_q = norm_rope(row_q[...], qg, new_factors)
-    new_k = norm_rope(row_k[...], kg, new_factors)
+    new_q = norm_rope(row_q[0:rows, :], qg, new_factors)
+    new_k = norm_rope(row_k[0:rows, :], kg, new_factors)
     scores = jnp.zeros((rows, tok), f32)
     for k in range(kvs):
         mine = (head >= k * per) & (head < (k + 1) * per)
@@ -352,7 +352,7 @@
     self_score = jnp.sum(new_q.astype(f32) * new_k.astype(f32), axis=-1, keepdims=True)
     self_weight = jnp.where(tp == 0, jnp.exp(self_score * scale), 0.0)
     totals = totals + self_weight
-    mixed = (mixed + self_weight * row_v[...]) * jax.nn.sigmoid(row_g[...])
+    mixed = (mixed + self_weight * row_v[0:rows, :]) * jax.nn.sigmoid(row_g[0:rows, :])
     total_row = jnp.sum(jnp.where(row == col, totals, 0.0), axis=0, keepdims=True)
     high = total_row.astype(bf16).astype(f32)
     rest = pltpu.roll(jnp.broadcast_to(total_row - high, (8, lanes)), lanes // 2, 1)
@@ -420,7 +420,7 @@
     req = lax.axis_index("req")
     tps = lax.axis_size("tp")
     z, y = lax.div(req, 2), lax.rem(req, 2)
-    heads, toks, _ = att.shape
+    heads, toks = att.shape[0], hid_ref.shape[0]
     groups = pay_ref.shape[0] // tps
     rpg = toks // groups
     rows = heads * rpg
@@ -443,13 +443,13 @@
     for r in range(groups):
         for h in range(heads):
             att[h, r * rpg : (r + 1) * rpg, :] = acc[r, h * rpg : (h + 1) * rpg, :]
-    state = hid[...]
+    state = hid[0:toks, :]
     per = heads // tps
     for d, w_ref in enumerate((w0_ref, w1_ref, w2_ref, w3_ref)):
         source = tp ^ d
         for j in range(per):
             state = state + dot(
-                att[source * per + j].astype(bf16), w_ref[j * lanes : (j + 1) * lanes, :]
+                att[source * per + j, 0:toks, :].astype(bf16), w_ref[j * lanes : (j + 1) * lanes, :]
             )
     hid_ref[...] = state
     width = state.shape[1]
@@ -475,7 +475,7 @@
     out[base : base + 8, :] = jnp.where(
         first == 0, high, jnp.where(first == 1, sums_row - high, 0.0)
     )
-    msg_ref[...] = out[...].astype(bf16)
+    msg_ref[...] = out[0 : msg_ref.shape[0], :].astype(bf16)
 
 
 def down_kernel(m0_ref, m1_ref, m2_ref, m3_ref, hid_ref, down_ref, pair_ref, back_ref, pay, whole):
@@ -487,7 +487,7 @@
     total = m0_ref[...].astype(f32)
     for m_ref in (m1_ref, m2_ref, m3_ref):
         total = total + m_ref[...].astype(f32)
-    whole[...] = total
+    whole[0 : total.shape[0], :] = total
     blocks = units // lanes
     base = 2 * blocks * toks
     square = iota((toks, lanes), 0) == iota((toks, lanes), 1)
@@ -578,6 +578,10 @@
                 weights.astype(bf16), kv_ref[:, (kvs + k) * lanes : (kvs + k + 1) * lanes]
             )
         out_ref[:, at] = (mixed / totals * gates[:, h : h + 1]).astype(bf16)
+
+
+def room(rows):
+    return (rows + 15) // 8 * 8
 
 
 def call(body, out_shape, args, scratch=(), hbm=False, out_any=False, smem=0, flops=0, limit=12):
@@ -673,8 +677,8 @@
         outputs,
         inputs,
         scratch=[pltpu.VMEM(o.shape, o.dtype) for o in outputs]
-        + [(heads * rpg, lanes)] * 4
-        + [(pay_rows, lanes), pltpu.SMEM(lengths.shape, jnp.int32)]
+        + [(room(heads * rpg), lanes)] * 4
+        + [(room(pay_rows), lanes), pltpu.SMEM(lengths.shape, jnp.int32)]
         + [pltpu.VMEM(a.shape, a.dtype) for a in inputs[1:11]]
         + [pltpu.SemaphoreType.DMA((len(inputs),)), pltpu.SemaphoreType.DMA((len(outputs),))],
         hbm=True,
@@ -721,11 +725,11 @@
         ),
         (got, w_here, w_near, w_far, w_both, mine, pair, ng, token),
         scratch=[
-            (heads, toks, lanes),
-            (toks, part),
+            (heads, room(toks), lanes),
+            (room(toks), part),
             (2, toks, part // 2),
-            (reqs, pay_rows, lanes),
-            msg_shape,
+            (reqs, room(pay_rows), lanes),
+            (room(msg_shape[0]), lanes),
         ],
         flops=10**7,
     )
@@ -743,7 +747,7 @@
         down_kernel,
         jax.ShapeDtypeStruct((peers, back_rows // 4, 4, lanes), bf16),
         (*msgs, hid, w_down, down_pair),
-        scratch=[(reqs, back_rows, lanes), msg_shape],
+        scratch=[(reqs, room(back_rows), lanes), (room(msg_shape[0]), lanes)],
         flops=3 * 10**9,
     )
     returned = lax.all_to_all(back, ("req", "tp"), 0, 0, tiled=True)
@@ -752,7 +756,7 @@
         final_kernel,
         jax.ShapeDtypeStruct((rpg, width), bf16),
         (returned,),
-        scratch=[(slices, back_rows, lanes), (8, width)],
+        scratch=[(slices, room(back_rows), lanes), (room(rpg), width)],
         flops=10**6,
     )
     return (prefill_out, decode_out)

time: 42.2 us -> 42.2 us (level)
  no operation moved by 1% of the time
where the time goes in v8:
time: 42.2 us; the launch traced here: 41.9 us
  starting transfers between devices  20.4 us (48%)
  waiting for transfers between devices  10.7 us (25%)
  Pallas kernels  8.85 us (21%)
  local copies, waits for them, and re-layouts  1.14 us (3%)
  between operations  0.8 us (2%)
    pallas_call x7, Pallas kernels, call(): pl.pallas_call(body, out_shape=out_shape, in_specs=specs, out_specs=jax.t...  8.85 us
    ppermute x2, starting transfers between devices, swap(): return lax.ppermute(array, 'req', [(i, i ^ 1) for i in range(reqs)])  5.44 us
    ppermute x3, starting transfers between devices, along(): return lax.ppermute(array, 'req', [(i, i ^ 2 * by) for i in range(reqs)])  4.45 us
    all_to_all x1, starting transfers between devices, local(): got = lax.all_to_all(pay, ('req', 'tp'), 0, 0, tiled=True)  3.97 us
    all_to_all x1, waiting for transfers between devices, local(): returned = lax.all_to_all(back, ('req', 'tp'), 0, 0, tiled=True)  3.78 us
    ppermute x6, starting transfers between devices, cross(): return lax.ppermute(array, 'tp', [(i, i ^ by) for i in range(tps)])  3.61 us
    all_to_all x1, starting transfers between devices, local(): returned = lax.all_to_all(back, ('req', 'tp'), 0, 0, tiled=True)  2.89 us
    all_to_all x1, waiting for transfers between devices, local(): got = lax.all_to_all(pay, ('req', 'tp'), 0, 0, tiled=True)  2.75 us
  transfers between devices with their start and end apart: 13, of which 6 were waited for; matrix products, arithmetic and copies ran while one was open for 0% of the time, Pallas kernels for 13%

profile of v8, /device:TPU:0, one launch (start us, length us, event | category | flops | bytes accessed | tf_op | source)
XLA Modules:
  0.0 41.9 jit_solution(5581998468986288598)
XLA Ops:
  0.6 2.9 %shard_map.185 = (bf16[128,1024]{1,0:T(8,128)(2,1)}, bf16[32,7,4,128]{3,2,1,0:T(4,128)(2,1)}, bf16[256,512]{1,0:T(8,128)(2,1)}, bf16[256,768]{1,0:T(8,128)(2,1)}) custom-call(s32[1,3]{1,0:T(1,128)} %len_ref.1, bf16[128,512]{1,0:T(8,128)(2,1)} %k_hbm.1, bf16[128,512]{1,0:T(8,128)(2,1)} %v_hbm.1, bf16[3,1024]{1,0:T(4,128)(2,1)} %qn_hbm.1, ...), custom_call_target="tpu_custom_call" | custom-call | flops 10000000 | bytes 2123324 | tf_op jit(solution)/shard_map/pallas_call | solution.py:592
  3.6 0.0 copy-start.3
  3.6 3.0 %collective-permute-start.3 = (bf16[256,768]{1,0:T(8,128)(2,1)}, bf16[256,768]{1,0:T(8,128)(2,1)S(1)}, u32[]{:S(2)}, u32[]{:S(2)}) collective-permute-start(bf16[256,768]{1,0:T(8,128)(2,1)} %get-tuple-element.22), channel_id=1, source_target_pairs={{0,4},{4,0},{8,12},{12,8},{16,20},{20,16},{24,28},{28,24},{1,5},{5... | collective-permute-start | bytes 1179656 | tf_op jit(solution)/shard_map/ppermute | solution.py:660
  6.6 1.5 %collective-permute-start.1 = (bf16[256,512]{1,0:T(8,128)(2,1)}, bf16[256,512]{1,0:T(8,128)(2,1)S(1)}, u32[]{:S(2)}, u32[]{:S(2)}) collective-permute-start(bf16[256,512]{1,0:T(8,128)(2,1)} %get-tuple-element.19), channel_id=1, source_target_pairs={{0,2},{1,3},{2,0},{3,1},{4,6},{5,7},{6,4},{7,5},{8,10},{9,11},{10,... | collective-permute-start | bytes 786440 | tf_op jit(solution)/shard_map/ppermute | solution.py:657
  8.1 4.0 %all-to-all-start = ((bf16[32,7,4,128]{3,2,1,0:T(4,128)(2,1)}), bf16[32,7,4,128]{3,2,1,0:T(4,128)(2,1)S(1)}, u32[]{:S(2)}, u32[]{:S(2)}) async-start(bf16[32,7,4,128]{3,2,1,0:T(4,128)(2,1)} %get-tuple-element.17), calls=%async_computation | async-start | bytes 458752 | tf_op jit(solution)/shard_map/all_to_all | solution.py:716
  12.1 0.0 copy-start.1
  12.1 0.0 copy-start.2
  12.1 0.0 copy-start.4
  12.1 0.3 collective-permute-start
  12.4 0.0 copy-done
  12.4 0.3 shard_map.186
  12.7 0.3 copy-done.1
  13.1 0.1 copy-done.2
  13.2 0.0 copy-done.4
  13.2 0.1 shard_map.187
  13.3 1.3 %collective-permute-done.1.w2_ref = bf16[256,512]{1,0:T(8,128)(2,1)S(1)} collective-permute-done((bf16[256,512]{1,0:T(8,128)(2,1)}, bf16[256,512]{1,0:T(8,128)(2,1)S(1)}, u32[]{:S(2)}, u32[]{:S(2)}) %collective-permute-start.1) | collective-permute-done | bytes 262176 | tf_op jit(solution)/shard_map/ppermute | solution.py:657
  14.6 0.0 collective-permute-start.2
  14.6 1.8 %collective-permute-start.9 = (bf16[128,1024]{1,0:T(8,128)(2,1)S(1)}, bf16[128,1024]{1,0:T(8,128)(2,1)S(1)}, u32[]{:S(2)}, u32[]{:S(2)}) collective-permute-start(bf16[128,1024]{1,0:T(8,128)(2,1)S(1)} %copy-done.9), channel_id=1, source_target_pairs={{0,2},{1,3},{2,0},{3,1},{4,6},{5,7},{6,4},{7,5},{8,10},{9,11},{10,... | collective-permute-start | bytes 786440 | tf_op jit(solution)/shard_map/ppermute | solution.py:657
  16.4 0.3 collective-permute-done.3.refs_0_.pair_ref
  16.7 2.4 %collective-permute-start.7 = (bf16[384,256]{1,0:T(8,128)(2,1)S(1)}, bf16[384,256]{1,0:T(8,128)(2,1)S(1)}, u32[]{:S(2)}, u32[]{:S(2)}) collective-permute-start(bf16[384,256]{1,0:T(8,128)(2,1)S(1)} %get-tuple-element.27), channel_id=1, source_target_pairs={{0,4},{4,0},{8,12},{12,8},{16,20},{20,16},{24,28},{28,24},{1,5},{5... | collective-permute-start | bytes 589832 | tf_op jit(solution)/shard_map/ppermute | solution.py:660
  19.1 0.0 collective-permute-done.refs_1_.w1_ref
  19.1 0.0 collective-permute-done.2.refs_2_.w3_ref
  19.1 2.8 %all-to-all-done.pay_ref = bf16[32,7,4,128]{3,2,1,0:T(4,128)(2,1)S(1)} async-done(((bf16[32,7,4,128]{3,2,1,0:T(4,128)(2,1)}), bf16[32,7,4,128]{3,2,1,0:T(4,128)(2,1)S(1)}, u32[]{:S(2)}, u32[]{:S(2)}) %all-to-all-start) | async-done | bytes 229408 | tf_op jit(solution)/shard_map/all_to_all | solution.py:716
  21.9 0.7 %shard_map.190 = (f32[24,512]{1,0:T(8,128)S(1)}, bf16[152,128]{1,0:T(8,128)(2,1)S(1)}) custom-call(bf16[32,7,4,128]{3,2,1,0:T(4,128)(2,1)S(1)} %all-to-all-done.pay_ref, bf16[256,512]{1,0:T(8,128)(2,1)S(1)} %get-tuple-element.18.w0_ref, bf16[256,512]{1,0:T(8,128)(2,1)S(1)} %collective-permute-done.refs_1_.w1_ref, ...), custom_call_target="tpu_custom_call" | custom-call | flops 10000000 | bytes 2070528 | tf_op jit(solution)/shard_map/pallas_call | solution.py:592
  22.6 1.6 %collective-permute-start.4 = (bf16[152,128]{1,0:T(8,128)(2,1)S(1)}, bf16[152,128]{1,0:T(8,128)(2,1)S(1)}, u32[]{:S(2)}, u32[]{:S(2)}) collective-permute-start(bf16[152,128]{1,0:T(8,128)(2,1)S(1)} %get-tuple-element.24.m0_ref), channel_id=1, source_target_pairs={{0,24},{4,28},{8,16},{12,20},{16,8},{20,12},{24,0},{28,4},{1,25},{... | collective-permute-start | bytes 116744 | tf_op jit(solution)/shard_map/ppermute | solution.py:663
  24.2 0.9 %collective-permute-start.5 = (bf16[152,128]{1,0:T(8,128)(2,1)S(1)}, bf16[152,128]{1,0:T(8,128)(2,1)S(1)}, u32[]{:S(2)}, u32[]{:S(2)}) collective-permute-start(bf16[152,128]{1,0:T(8,128)(2,1)S(1)} %get-tuple-element.24.m0_ref), channel_id=1, source_target_pairs={{0,16},{4,20},{8,24},{12,28},{16,0},{20,4},{24,8},{28,12},{1,17},{... | collective-permute-start | bytes 116744 | tf_op jit(solution)/shard_map/ppermute | solution.py:663
  25.1 1.9 %collective-permute-start.6 = (bf16[152,128]{1,0:T(8,128)(2,1)S(1)}, bf16[152,128]{1,0:T(8,128)(2,1)S(1)}, u32[]{:S(2)}, u32[]{:S(2)}) collective-permute-start(bf16[152,128]{1,0:T(8,128)(2,1)S(1)} %get-tuple-element.24.m0_ref), channel_id=1, source_target_pairs={{0,8},{4,12},{8,0},{12,4},{16,24},{20,28},{24,16},{28,20},{1,9},{5... | collective-permute-start | bytes 116744 | tf_op jit(solution)/shard_map/ppermute | solution.py:663
  27.0 0.0 collective-permute-done.9.kv2_ref
  27.0 0.0 collective-permute-start.8
  27.0 1.8 %collective-permute-done.4.m1_ref = bf16[152,128]{1,0:T(8,128)(2,1)S(1)} collective-permute-done((bf16[152,128]{1,0:T(8,128)(2,1)S(1)}, bf16[152,128]{1,0:T(8,128)(2,1)S(1)}, u32[]{:S(2)}, u32[]{:S(2)}) %collective-permute-start.4) | collective-permute-done | bytes 38944 | tf_op jit(solution)/shard_map/ppermute | solution.py:663
  28.8 0.0 collective-permute-start.10
  28.8 0.8 %collective-permute-done.5.m2_ref = bf16[152,128]{1,0:T(8,128)(2,1)S(1)} collective-permute-done((bf16[152,128]{1,0:T(8,128)(2,1)S(1)}, bf16[152,128]{1,0:T(8,128)(2,1)S(1)}, u32[]{:S(2)}, u32[]{:S(2)}) %collective-permute-start.5) | collective-permute-done | bytes 38944 | tf_op jit(solution)/shard_map/ppermute | solution.py:663
  29.6 0.0 collective-permute-done.6.m3_ref
  29.6 0.0 collective-permute-done.7.pair_ref
  29.6 0.9 %shard_map.191 = bf16[32,3,4,128]{3,2,1,0:T(4,128)(2,1)} custom-call(bf16[152,128]{1,0:T(8,128)(2,1)S(1)} %get-tuple-element.24.m0_ref, bf16[152,128]{1,0:T(8,128)(2,1)S(1)} %collective-permute-done.4.m1_ref, bf16[152,128]{1,0:T(8,128)(2,1)S(1)} %collective-permute-done.5.m2_ref, bf16[152,128]{1,0:T(8,128)(2,1)S(1)} %collective-permute-done.6.m3_ref, ...), custom_call_target="tpu_custom_call" | custom-call | flops 3000000000 | bytes 794624 | tf_op jit(solution)/shard_map/pallas_call | solution.py:592
  30.5 2.9 %all-to-all-start.1 = ((bf16[32,3,4,128]{3,2,1,0:T(4,128)(2,1)}), bf16[32,3,4,128]{3,2,1,0:T(4,128)(2,1)S(1)}, u32[]{:S(2)}, u32[]{:S(2)}) async-start(bf16[32,3,4,128]{3,2,1,0:T(4,128)(2,1)} %shard_map.191), calls=%async_computation.1 | async-start | bytes 196608 | tf_op jit(solution)/shard_map/all_to_all | solution.py:753
  33.4 0.0 copy-start.5
  33.4 0.0 copy-start.6
  33.5 0.0 copy-start.7
  33.5 0.1 copy.20.g_ref
  33.6 0.0 collective-permute-done.8.kv1_ref
  33.6 0.0 collective-permute-done.10.kv3_ref
  33.6 0.5 %copy-done.5 = s32[1,3]{1,0:T(1,128)S(1)} copy-done((s32[1,3]{1,0:T(1,128)S(1)}, s32[1,3]{1,0:T(1,128)}, u32[]{:S(2)}) %copy-start.5) | copy-done | bytes 36
  34.1 0.0 copy-done.6
  34.1 0.0 copy-done.7
  34.1 3.3 %shard_map.192 = bf16[128,1024]{1,0:T(8,128)(2,1)} custom-call(s32[1,3]{1,0:T(1,128)S(1)} %copy-done.5, bf16[128,1024]{1,0:T(8,128)(2,1)S(1)} %copy-done.8, bf16[128,8]{1,0:T(8,128)(2,1)S(1)} %copy.20.g_ref, bf16[128,1024]{1,0:T(8,128)(2,1)S(1)} %copy-done.9, bf16[128,1024]{1,0:T(8,128)(2,1)S(1)} %collective-permute-done.8.kv1_ref, ...), custom_call_target="tpu_custom_call" | custom-call | flops 1000000000 | bytes 1313804 | tf_op jit(solution)/shard_map/pallas_call | solution.py:592
  37.5 3.8 %all-to-all-done.1.back_ref = bf16[32,3,4,128]{3,2,1,0:T(4,128)(2,1)S(1)} async-done(((bf16[32,3,4,128]{3,2,1,0:T(4,128)(2,1)}), bf16[32,3,4,128]{3,2,1,0:T(4,128)(2,1)S(1)}, u32[]{:S(2)}, u32[]{:S(2)}) %all-to-all-start.1) | async-done | bytes 98336 | tf_op jit(solution)/shard_map/all_to_all | solution.py:753
  41.2 0.7 %shard_map.193 = bf16[3,2048]{1,0:T(4,128)(2,1)} custom-call(bf16[32,3,4,128]{3,2,1,0:T(4,128)(2,1)S(1)} %all-to-all-done.1.back_ref), custom_call_target="tpu_custom_call" | custom-call | flops 1000000 | bytes 98304 | tf_op jit(solution)/shard_map/pallas_call | solution.py:592
  (10 shorter events, 0.0 us)
Async XLA Ops:
  0.6 11.8 %copy-start = (bf16[256,2048]{1,0:T(8,128)(2,1)S(1)}, bf16[256,2048]{1,0:T(8,128)(2,1)}, u32[]{:S(2)}) copy-start(bf16[256,2048]{1,0:T(8,128)(2,1)} %w_hbm.3) | copy-start | bytes 3145732
  3.6 8.9 %copy-start.3 = (bf16[768,256]{1,0:T(8,128)(2,1)S(1)}, bf16[768,256]{1,0:T(8,128)(2,1)}, u32[]{:S(2)}) copy-start(bf16[768,256]{1,0:T(8,128)(2,1)} %down_ref.1) | copy-start | bytes 1179652
  3.6 13.1 %collective-permute-start.3 = (bf16[256,768]{1,0:T(8,128)(2,1)}, bf16[256,768]{1,0:T(8,128)(2,1)S(1)}, u32[]{:S(2)}, u32[]{:S(2)}) collective-permute-start(bf16[256,768]{1,0:T(8,128)(2,1)} %get-tuple-element.22), channel_id=1, source_target_pairs={{0,4},{4,0},{8,12},{12,8},{16,20},{20,16},{24,28},{28,24},{1,5},{5... | collective-permute-start | bytes 1179656 | tf_op jit(solution)/shard_map/ppermute | solution.py:660
  6.6 8.0 %collective-permute-start.1 = (bf16[256,512]{1,0:T(8,128)(2,1)}, bf16[256,512]{1,0:T(8,128)(2,1)S(1)}, u32[]{:S(2)}, u32[]{:S(2)}) collective-permute-start(bf16[256,512]{1,0:T(8,128)(2,1)} %get-tuple-element.19), channel_id=1, source_target_pairs={{0,2},{1,3},{2,0},{3,1},{4,6},{5,7},{6,4},{7,5},{8,10},{9,11},{10,... | collective-permute-start | bytes 786440 | tf_op jit(solution)/shard_map/ppermute | solution.py:657
  8.1 13.8 %all-to-all-start = ((bf16[32,7,4,128]{3,2,1,0:T(4,128)(2,1)}), bf16[32,7,4,128]{3,2,1,0:T(4,128)(2,1)S(1)}, u32[]{:S(2)}, u32[]{:S(2)}) async-start(bf16[32,7,4,128]{3,2,1,0:T(4,128)(2,1)} %get-tuple-element.17), calls=%async_computation | async-start | bytes 458752 | tf_op jit(solution)/shard_map/all_to_all | solution.py:716
  12.1 1.0 %copy-start.1 = (bf16[256,768]{1,0:T(8,128)(2,1)S(1)}, bf16[256,768]{1,0:T(8,128)(2,1)}, u32[]{:S(2)}) copy-start(bf16[256,768]{1,0:T(8,128)(2,1)} %gate_hbm.3) | copy-start | bytes 1179652
  12.1 1.1 %copy-start.2 = (bf16[256,768]{1,0:T(8,128)(2,1)S(1)}, bf16[256,768]{1,0:T(8,128)(2,1)}, u32[]{:S(2)}) copy-start(bf16[256,768]{1,0:T(8,128)(2,1)} %up_hbm.3) | copy-start | bytes 1179652
  12.1 1.1 %copy-start.4 = (f32[2048]{0:T(1024)S(1)}, f32[2048]{0:T(1024)}, u32[]{:S(2)}) copy-start(f32[2048]{0:T(1024)} %param.31) | copy-start | bytes 24580
  12.1 7.0 %collective-permute-start = (bf16[256,512]{1,0:T(8,128)(2,1)}, bf16[256,512]{1,0:T(8,128)(2,1)S(1)}, u32[]{:S(2)}, u32[]{:S(2)}) collective-permute-start(bf16[256,512]{1,0:T(8,128)(2,1)} %get-tuple-element.19), channel_id=1, source_target_pairs={{0,1},{1,0},{2,3},{3,2},{4,5},{5,4},{6,7},{7,6},{8,9},{9,8},{10,11... | collective-permute-start | bytes 786440 | tf_op jit(solution)/shard_map/ppermute | solution.py:657
  13.2 1.4 %copy-start.9 = (bf16[128,1024]{1,0:T(8,128)(2,1)S(1)}, bf16[128,1024]{1,0:T(8,128)(2,1)}, u32[]{:S(2)}) copy-start(bf16[128,1024]{1,0:T(8,128)(2,1)} %get-tuple-element.29.kv0_ref) | copy-start | bytes 786436
  14.6 4.5 %collective-permute-start.2 = (bf16[256,512]{1,0:T(8,128)(2,1)S(1)}, bf16[256,512]{1,0:T(8,128)(2,1)S(1)}, u32[]{:S(2)}, u32[]{:S(2)}) collective-permute-start(bf16[256,512]{1,0:T(8,128)(2,1)S(1)} %collective-permute-done.1.w2_ref), channel_id=1, source_target_pairs={{0,1},{1,0},{2,3},{3,2},{4,5},{5,4},{6,7},{7,6},{8,9},{9,8},{10,11... | collective-permute-start | bytes 786440 | tf_op jit(solution)/shard_map/ppermute | solution.py:657
  14.6 12.4 %collective-permute-start.9 = (bf16[128,1024]{1,0:T(8,128)(2,1)S(1)}, bf16[128,1024]{1,0:T(8,128)(2,1)S(1)}, u32[]{:S(2)}, u32[]{:S(2)}) collective-permute-start(bf16[128,1024]{1,0:T(8,128)(2,1)S(1)} %copy-done.9), channel_id=1, source_target_pairs={{0,2},{1,3},{2,0},{3,1},{4,6},{5,7},{6,4},{7,5},{8,10},{9,11},{10,... | collective-permute-start | bytes 786440 | tf_op jit(solution)/shard_map/ppermute | solution.py:657
  16.7 12.9 %collective-permute-start.7 = (bf16[384,256]{1,0:T(8,128)(2,1)S(1)}, bf16[384,256]{1,0:T(8,128)(2,1)S(1)}, u32[]{:S(2)}, u32[]{:S(2)}) collective-permute-start(bf16[384,256]{1,0:T(8,128)(2,1)S(1)} %get-tuple-element.27), channel_id=1, source_target_pairs={{0,4},{4,0},{8,12},{12,8},{16,20},{20,16},{24,28},{28,24},{1,5},{5... | collective-permute-start | bytes 589832 | tf_op jit(solution)/shard_map/ppermute | solution.py:660
  22.6 6.2 %collective-permute-start.4 = (bf16[152,128]{1,0:T(8,128)(2,1)S(1)}, bf16[152,128]{1,0:T(8,128)(2,1)S(1)}, u32[]{:S(2)}, u32[]{:S(2)}) collective-permute-start(bf16[152,128]{1,0:T(8,128)(2,1)S(1)} %get-tuple-element.24.m0_ref), channel_id=1, source_target_pairs={{0,24},{4,28},{8,16},{12,20},{16,8},{20,12},{24,0},{28,4},{1,25},{... | collective-permute-start | bytes 116744 | tf_op jit(solution)/shard_map/ppermute | solution.py:663
  24.2 5.4 %collective-permute-start.5 = (bf16[152,128]{1,0:T(8,128)(2,1)S(1)}, bf16[152,128]{1,0:T(8,128)(2,1)S(1)}, u32[]{:S(2)}, u32[]{:S(2)}) collective-permute-start(bf16[152,128]{1,0:T(8,128)(2,1)S(1)} %get-tuple-element.24.m0_ref), channel_id=1, source_target_pairs={{0,16},{4,20},{8,24},{12,28},{16,0},{20,4},{24,8},{28,12},{1,17},{... | collective-permute-start | bytes 116744 | tf_op jit(solution)/shard_map/ppermute | solution.py:663
  25.1 4.5 %collective-permute-start.6 = (bf16[152,128]{1,0:T(8,128)(2,1)S(1)}, bf16[152,128]{1,0:T(8,128)(2,1)S(1)}, u32[]{:S(2)}, u32[]{:S(2)}) collective-permute-start(bf16[152,128]{1,0:T(8,128)(2,1)S(1)} %get-tuple-element.24.m0_ref), channel_id=1, source_target_pairs={{0,8},{4,12},{8,0},{12,4},{16,24},{20,28},{24,16},{28,20},{1,9},{5... | collective-permute-start | bytes 116744 | tf_op jit(solution)/shard_map/ppermute | solution.py:663
  27.0 6.6 %collective-permute-start.8 = (bf16[128,1024]{1,0:T(8,128)(2,1)S(1)}, bf16[128,1024]{1,0:T(8,128)(2,1)S(1)}, u32[]{:S(2)}, u32[]{:S(2)}) collective-permute-start(bf16[128,1024]{1,0:T(8,128)(2,1)S(1)} %copy-done.9), channel_id=1, source_target_pairs={{0,1},{1,0},{2,3},{3,2},{4,5},{5,4},{6,7},{7,6},{8,9},{9,8},{10,11... | collective-permute-start | bytes 786440 | tf_op jit(solution)/shard_map/ppermute | solution.py:657
  28.8 4.8 %collective-permute-start.10 = (bf16[128,1024]{1,0:T(8,128)(2,1)S(1)}, bf16[128,1024]{1,0:T(8,128)(2,1)S(1)}, u32[]{:S(2)}, u32[]{:S(2)}) collective-permute-start(bf16[128,1024]{1,0:T(8,128)(2,1)S(1)} %collective-permute-done.9.kv2_ref), channel_id=1, source_target_pairs={{0,1},{1,0},{2,3},{3,2},{4,5},{5,4},{6,7},{7,6},{8,9},{9,8},{10,11... | collective-permute-start | bytes 786440 | tf_op jit(solution)/shard_map/ppermute | solution.py:657
  29.6 4.0 %copy-start.8 = (bf16[128,1024]{1,0:T(8,128)(2,1)S(1)}, bf16[128,1024]{1,0:T(8,128)(2,1)}, u32[]{:S(2)}) copy-start(bf16[128,1024]{1,0:T(8,128)(2,1)} %q_ref.1) | copy-start | bytes 786436
  30.5 2.9 %copy-start.10 = (bf16[128,8]{0,1:T(8,128)(2,1)S(1)}, bf16[128,8]{0,1:T(8,128)(2,1)}, u32[]{:S(2)}) copy-start(bf16[128,8]{0,1:T(8,128)(2,1)} %param.19) | copy-start | bytes 6148
  30.5 10.7 %all-to-all-start.1 = ((bf16[32,3,4,128]{3,2,1,0:T(4,128)(2,1)}), bf16[32,3,4,128]{3,2,1,0:T(4,128)(2,1)S(1)}, u32[]{:S(2)}, u32[]{:S(2)}) async-start(bf16[32,3,4,128]{3,2,1,0:T(4,128)(2,1)} %shard_map.191), calls=%async_computation.1 | async-start | bytes 196608 | tf_op jit(solution)/shard_map/all_to_all | solution.py:753
  33.4 0.7 %copy-start.5 = (s32[1,3]{1,0:T(1,128)S(1)}, s32[1,3]{1,0:T(1,128)}, u32[]{:S(2)}) copy-start(s32[1,3]{1,0:T(1,128)} %len_ref.1) | copy-start | bytes 40
  33.4 0.7 %copy-start.6 = (f32[128]{0:T(128)S(1)}, f32[128]{0:T(128)}, u32[]{:S(2)}) copy-start(f32[128]{0:T(128)} %param.22) | copy-start | bytes 1540
  33.5 0.7 %copy-start.7 = (f32[1,128]{1,0:T(1,128)S(1)}, f32[1,128]{1,0:T(1,128)}, u32[]{:S(2)}) copy-start(f32[1,128]{1,0:T(1,128)} %constant.2.clone.freq_hbm.freq_ref) | copy-start | bytes 1540

commit v9 on v8

--- a/solution.py
+++ b/solution.py
@@ -542,42 +542,59 @@
     out_ref[...] = rows_out[0:rpg, :].astype(bf16)
 
 
-def prefill_kernel(
-    len_ref, q_ref, g_ref, kv0_ref, kv1_ref, kv2_ref, kv3_ref, qg_ref, freq_ref, out_ref, mid_ref
-):
+def query_kernel(len_ref, q_ref, g_ref, qg_ref, freq_ref, query_ref, side_ref):
     tp = lax.axis_index("tp")
     tok = q_ref.shape[0]
     heads = q_ref.shape[1] // lanes
+    tok_index = tp * tok + iota((tok, lanes), 0)
+    begin = begin_of(tok_index, len_ref)
+    factors = rope_factors((tok_index - begin).astype(f32) * freq_ref[...])
+    gates = jax.nn.sigmoid(g_ref[...].astype(f32))
+    lane = iota((tok, lanes), 1)
+    side = jnp.where(lane == heads, begin.astype(f32), 0.0)
+    for h in range(heads):
+        at = slice(h * lanes, (h + 1) * lanes)
+        query_ref[:, at] = norm_rope(q_ref[:, at].astype(f32), qg_ref[...], factors)
+        side = jnp.where(lane == h, gates[:, h : h + 1], side)
+    side_ref[...] = side
+
+
+def prefill_kernel(query_ref, side_ref, kv0_ref, kv1_ref, kv2_ref, kv3_ref, out_ref, mid_ref):
+    tp = lax.axis_index("tp")
+    tok = query_ref.shape[0]
+    heads = query_ref.shape[1] // lanes
     kvs = kv0_ref.shape[1] // (2 * lanes)
     per = heads // kvs
     third = tp == 2
     mid_ref[...] = jnp.where(third, kv3_ref[...], kv1_ref[...])
     blocks = ((tp, kv0_ref), (jnp.where(third, tp ^ 3, tp ^ 1), mid_ref), (tp ^ 2, kv2_ref))
-    tok_index = tp * tok + iota((tok, lanes), 0)
-    begin = begin_of(tok_index, len_ref)
-    factors = rope_factors((tok_index - begin).astype(f32) * freq_ref[...])
+    tok_index = tp * tok + iota((tok, tok), 0)
+    begin = side_ref[:, heads : heads + 1].astype(jnp.int32)
     col = iota((tok, tok), 1)
     allowed = []
     for block, _ in blocks:
         key_index = block * tok + col
-        allowed.append((key_index >= begin) & (key_index <= tok_index))
-    gates = jax.nn.sigmoid(g_ref[...].astype(f32))
-    qg = qg_ref[...]
+        mask = ((key_index >= begin) & (key_index <= tok_index)).astype(f32)
+        allowed.append(jnp.concatenate([mask] * per, axis=0) > 0.5)
+    ones = jnp.ones((tok, lanes), bf16)
     scale = lanes ** (-0.5)
-    for h in range(heads):
-        k = h // per
-        at = slice(h * lanes, (h + 1) * lanes)
-        query = norm_rope(q_ref[:, at].astype(f32), qg, factors)
-        totals = jnp.zeros((tok, 1), f32)
-        mixed = jnp.zeros((tok, lanes), f32)
+    for k in range(kvs):
+        query = jnp.concatenate(
+            [query_ref[:, h * lanes : (h + 1) * lanes] for h in range(k * per, (k + 1) * per)],
+            axis=0,
+        )
+        sums = jnp.zeros((per * tok, 2 * lanes), f32)
         for b, (_, kv_ref) in enumerate(blocks):
             scores = dot_nt(query, kv_ref[:, k * lanes : (k + 1) * lanes])
-            weights = jnp.where(allowed[b], jnp.exp(scores * scale), 0.0)
-            totals = totals + jnp.sum(weights, axis=-1, keepdims=True)
-            mixed = mixed + dot(
-                weights.astype(bf16), kv_ref[:, (kvs + k) * lanes : (kvs + k + 1) * lanes]
-            )
-        out_ref[:, at] = (mixed / totals * gates[:, h : h + 1]).astype(bf16)
+            weights = jnp.where(allowed[b], jnp.exp(scores * scale), 0.0).astype(bf16)
+            values = kv_ref[:, (kvs + k) * lanes : (kvs + k + 1) * lanes]
+            sums = sums + dot(weights, jnp.concatenate([values, ones], axis=1))
+        for i in range(per):
+            h = k * per + i
+            rows = slice(i * tok, (i + 1) * tok)
+            out_ref[:, h * lanes : (h + 1) * lanes] = (
+                sums[rows, :lanes] / sums[rows, lanes:] * side_ref[:, h : h + 1]
+            ).astype(bf16)
 
 
 def room(rows):
@@ -706,7 +723,14 @@
         hbm=True,
         scratch=[pltpu.SemaphoreType.DMA((2,))],
     )
-    late_far, _, _ = lax.optimization_barrier((w_far, mine, w_here))
+    query, side = call(
+        query_kernel,
+        (jax.ShapeDtypeStruct(q_pre.shape, bf16), jax.ShapeDtypeStruct((tok, lanes), f32)),
+        (lengths, q_pre, gate_pre, qg, freqs),
+        smem=1,
+        flops=10**6,
+    )
+    late_far, _, _, _ = lax.optimization_barrier((w_far, mine, w_here, side))
     w_near, w_both = cross(w_own, 1), cross(late_far, 1)
     kv_near = cross(kv, 1)
     late_kv, _ = lax.optimization_barrier((kv, w_far))
@@ -738,9 +762,8 @@
     prefill_out = call(
         prefill_kernel,
         jax.ShapeDtypeStruct(q_pre.shape, bf16),
-        (lengths, q_pre, gate_pre, kv, kv_near, kv_far, kv_both, qg, freqs),
+        (query, side, kv, kv_near, kv_far, kv_both),
         scratch=[pltpu.VMEM(kv.shape, bf16)],
-        smem=1,
         flops=10**9,
     )
     back = call(

time: 42.2 us -> 43.2 us (1.024)
  Pallas kernels: 8.85 us -> 10.9 us
  starting transfers between devices: 20.4 us -> 19.7 us
    all_to_all x1, waiting for transfers between devices: 3.78 us -> 5.91 us  [local(): returned = lax.all_to_all(back, ('req', 'tp'), 0, 0, tiled=True)]
    pallas_call x7 -> x8, Pallas kernels: 8.85 us -> 10.9 us  [call(): pl.pallas_call(body, out_shape=out_shape, in_specs=specs, out_specs=jax.t...]
    ppermute x6, waiting for transfers between devices: 1.32 us -> 0.02 us  [cross(): return lax.ppermute(array, 'tp', [(i, i ^ by) for i in range(tps)])]
    ppermute x2, starting transfers between devices: 5.44 us -> 4.5 us  [swap(): return lax.ppermute(array, 'req', [(i, i ^ 1) for i in range(reqs)])]
    all_to_all x1, waiting for transfers between devices: 2.75 us -> 1.9 us  [local(): got = lax.all_to_all(pay, ('req', 'tp'), 0, 0, tiled=True)]
  transfers between devices with their start and end apart: 13 -> 13, of which waited for: 6 -> 4; matrix products, arithmetic and copies ran while one was open for 0% -> 0% of each run, Pallas kernels for 13% -> 17%
where the time goes in v9:
time: 43.2 us; the launch traced here: 42.8 us
  starting transfers between devices  19.7 us (46%)
  Pallas kernels  10.9 us (25%)
  waiting for transfers between devices  10.4 us (24%)
  local copies, waits for them, and re-layouts  1.06 us (2%)
  between operations  0.81 us (2%)
    pallas_call x8, Pallas kernels, call(): pl.pallas_call(body, out_shape=out_shape, in_specs=specs, out_specs=jax.t...  10.9 us
    all_to_all x1, waiting for transfers between devices, local(): returned = lax.all_to_all(back, ('req', 'tp'), 0, 0, tiled=True)  5.91 us
    ppermute x2, starting transfers between devices, swap(): return lax.ppermute(array, 'req', [(i, i ^ 1) for i in range(reqs)])  4.5 us
    ppermute x3, starting transfers between devices, along(): return lax.ppermute(array, 'req', [(i, i ^ 2 * by) for i in range(reqs)])  4.45 us
    all_to_all x1, starting transfers between devices, local(): got = lax.all_to_all(pay, ('req', 'tp'), 0, 0, tiled=True)  3.97 us
    ppermute x6, starting transfers between devices, cross(): return lax.ppermute(array, 'tp', [(i, i ^ by) for i in range(tps)])  3.9 us
    all_to_all x1, starting transfers between devices, local(): returned = lax.all_to_all(back, ('req', 'tp'), 0, 0, tiled=True)  2.89 us
    ppermute x3, waiting for transfers between devices, along(): return lax.ppermute(array, 'req', [(i, i ^ 2 * by) for i in range(reqs)])  2.55 us
  transfers between devices with their start and end apart: 13, of which 4 were waited for; matrix products, arithmetic and copies ran while one was open for 0% of the time, Pallas kernels for 17%

profile of v9, /device:TPU:0, one launch (start us, length us, event | category | flops | bytes accessed | tf_op | source)
XLA Modules:
  0.0 42.8 jit_solution(10996167251724499056)
XLA Ops:
  0.6 0.0 copy-start
  0.6 2.9 %shard_map.185 = (bf16[128,1024]{1,0:T(8,128)(2,1)}, bf16[32,7,4,128]{3,2,1,0:T(4,128)(2,1)}, bf16[256,512]{1,0:T(8,128)(2,1)}, bf16[256,768]{1,0:T(8,128)(2,1)}) custom-call(s32[1,3]{1,0:T(1,128)} %len_ref.1, bf16[128,512]{1,0:T(8,128)(2,1)} %k_hbm.1, bf16[128,512]{1,0:T(8,128)(2,1)} %v_hbm.1, bf16[3,1024]{1,0:T(4,128)(2,1)} %qn_hbm.1, ...), custom_call_target="tpu_custom_call" | custom-call | flops 10000000 | bytes 2123324 | tf_op jit(solution)/shard_map/pallas_call | solution.py:609
  3.6 0.0 copy-start.3
  3.6 3.0 %collective-permute-start.3 = (bf16[256,768]{1,0:T(8,128)(2,1)}, bf16[256,768]{1,0:T(8,128)(2,1)S(1)}, u32[]{:S(2)}, u32[]{:S(2)}) collective-permute-start(bf16[256,768]{1,0:T(8,128)(2,1)} %get-tuple-element.25), channel_id=1, source_target_pairs={{0,4},{4,0},{8,12},{12,8},{16,20},{20,16},{24,28},{28,24},{1,5},{5... | collective-permute-start | bytes 1179656 | tf_op jit(solution)/shard_map/ppermute | solution.py:677
  6.6 1.5 %collective-permute-start.1 = (bf16[256,512]{1,0:T(8,128)(2,1)}, bf16[256,512]{1,0:T(8,128)(2,1)S(1)}, u32[]{:S(2)}, u32[]{:S(2)}) collective-permute-start(bf16[256,512]{1,0:T(8,128)(2,1)} %get-tuple-element.21), channel_id=1, source_target_pairs={{0,2},{1,3},{2,0},{3,1},{4,6},{5,7},{6,4},{7,5},{8,10},{9,11},{10,... | collective-permute-start | bytes 786440 | tf_op jit(solution)/shard_map/ppermute | solution.py:674
  8.1 4.0 %all-to-all-start = ((bf16[32,7,4,128]{3,2,1,0:T(4,128)(2,1)}), bf16[32,7,4,128]{3,2,1,0:T(4,128)(2,1)S(1)}, u32[]{:S(2)}, u32[]{:S(2)}) async-start(bf16[32,7,4,128]{3,2,1,0:T(4,128)(2,1)} %get-tuple-element.19), calls=%async_computation | async-start | bytes 458752 | tf_op jit(solution)/shard_map/all_to_all | solution.py:740
  12.1 0.3 collective-permute-start
  12.4 0.0 copy-done.10
  12.4 0.1 copy.20.g_ref
  12.5 0.0 copy-done
  12.5 0.0 copy-done.3
  12.5 0.0 copy-start.1
  12.5 0.0 copy-start.2
  12.6 0.0 copy-start.5
  12.6 1.0 %shard_map.186 = (bf16[256,512]{1,0:T(8,128)(2,1)S(1)}, bf16[384,256]{1,0:T(8,128)(2,1)}) custom-call(bf16[256,2048]{1,0:T(8,128)(2,1)S(1)} %copy-done, bf16[768,256]{1,0:T(8,128)(2,1)S(1)} %copy-done.3), custom_call_target="tpu_custom_call" | custom-call | bytes 1441792 | tf_op jit(solution)/shard_map/pallas_call | solution.py:609
  13.6 0.0 copy-done.1
  13.6 0.1 copy-done.2
  13.7 0.0 copy-start.8
  13.7 0.1 shard_map.187
  13.8 0.8 %copy-done.4 = bf16[128,1024]{1,0:T(8,128)(2,1)S(1)} copy-done((bf16[128,1024]{1,0:T(8,128)(2,1)S(1)}, bf16[128,1024]{1,0:T(8,128)(2,1)}, u32[]{:S(2)}) %copy-start.4) | copy-done | bytes 262168
  14.6 0.0 copy-done.8
  14.6 1.8 %shard_map.188 = (bf16[128,1024]{1,0:T(8,128)(2,1)S(1)}, f32[128,128]{1,0:T(8,128)S(1)}) custom-call(s32[1,3]{1,0:T(1,128)S(1)} %copy-done.6, bf16[128,1024]{1,0:T(8,128)(2,1)S(1)} %copy-done.4, bf16[128,8]{1,0:T(8,128)(2,1)S(1)} %copy.20.g_ref, f32[1,128]{1,0:T(1,128)S(1)} %bitcast.5, f32[1,128]{1,0:T(1,128)S(1)} %copy-done.8), custom_call_target="tpu_custom_call" | custom-call | flops 1000000 | bytes 265228 | tf_op jit(solution)/shard_map/pallas_call | solution.py:609
  16.4 0.0 collective-permute-done.1.w2_ref
  16.4 0.3 collective-permute-start.2
  16.7 1.8 %collective-permute-start.9 = (bf16[128,1024]{1,0:T(8,128)(2,1)S(1)}, bf16[128,1024]{1,0:T(8,128)(2,1)S(1)}, u32[]{:S(2)}, u32[]{:S(2)}) collective-permute-start(bf16[128,1024]{1,0:T(8,128)(2,1)S(1)} %copy-done.9), channel_id=1, source_target_pairs={{0,2},{1,3},{2,0},{3,1},{4,6},{5,7},{6,4},{7,5},{8,10},{9,11},{10,... | collective-permute-start | bytes 786440 | tf_op jit(solution)/shard_map/ppermute | solution.py:674
  18.5 0.0 collective-permute-done.3.refs_0_.pair_ref
  18.5 1.5 %collective-permute-start.7 = (bf16[384,256]{1,0:T(8,128)(2,1)}, bf16[384,256]{1,0:T(8,128)(2,1)}, u32[]{:S(2)}, u32[]{:S(2)}) collective-permute-start(bf16[384,256]{1,0:T(8,128)(2,1)} %get-tuple-element.30), channel_id=1, source_target_pairs={{0,4},{4,0},{8,12},{12,8},{16,20},{20,16},{24,28},{28,24},{1,5},{5... | collective-permute-start | bytes 589832 | tf_op jit(solution)/shard_map/ppermute | solution.py:677
  20.0 0.0 collective-permute-done.refs_1_.w1_ref
  20.0 0.0 collective-permute-done.2.refs_2_.w3_ref
  20.0 1.9 %all-to-all-done.pay_ref = bf16[32,7,4,128]{3,2,1,0:T(4,128)(2,1)S(1)} async-done(((bf16[32,7,4,128]{3,2,1,0:T(4,128)(2,1)}), bf16[32,7,4,128]{3,2,1,0:T(4,128)(2,1)S(1)}, u32[]{:S(2)}, u32[]{:S(2)}) %all-to-all-start) | async-done | bytes 229408 | tf_op jit(solution)/shard_map/all_to_all | solution.py:740
  21.9 0.7 %shard_map.191 = (f32[24,512]{1,0:T(8,128)S(1)}, bf16[152,128]{1,0:T(8,128)(2,1)S(1)}) custom-call(bf16[32,7,4,128]{3,2,1,0:T(4,128)(2,1)S(1)} %all-to-all-done.pay_ref, bf16[256,512]{1,0:T(8,128)(2,1)S(1)} %get-tuple-element.20.w0_ref, bf16[256,512]{1,0:T(8,128)(2,1)S(1)} %collective-permute-done.refs_1_.w1_ref, ...), custom_call_target="tpu_custom_call" | custom-call | flops 10000000 | bytes 2070528 | tf_op jit(solution)/shard_map/pallas_call | solution.py:609
  22.6 1.6 %collective-permute-start.4 = (bf16[152,128]{1,0:T(8,128)(2,1)S(1)}, bf16[152,128]{1,0:T(8,128)(2,1)S(1)}, u32[]{:S(2)}, u32[]{:S(2)}) collective-permute-start(bf16[152,128]{1,0:T(8,128)(2,1)S(1)} %get-tuple-element.27.m0_ref), channel_id=1, source_target_pairs={{0,24},{4,28},{8,16},{12,20},{16,8},{20,12},{24,0},{28,4},{1,25},{... | collective-permute-start | bytes 116744 | tf_op jit(solution)/shard_map/ppermute | solution.py:680
  24.1 1.0 %collective-permute-start.5 = (bf16[152,128]{1,0:T(8,128)(2,1)S(1)}, bf16[152,128]{1,0:T(8,128)(2,1)S(1)}, u32[]{:S(2)}, u32[]{:S(2)}) collective-permute-start(bf16[152,128]{1,0:T(8,128)(2,1)S(1)} %get-tuple-element.27.m0_ref), channel_id=1, source_target_pairs={{0,16},{4,20},{8,24},{12,28},{16,0},{20,4},{24,8},{28,12},{1,17},{... | collective-permute-start | bytes 116744 | tf_op jit(solution)/shard_map/ppermute | solution.py:680
  25.1 1.9 %collective-permute-start.6 = (bf16[152,128]{1,0:T(8,128)(2,1)S(1)}, bf16[152,128]{1,0:T(8,128)(2,1)S(1)}, u32[]{:S(2)}, u32[]{:S(2)}) collective-permute-start(bf16[152,128]{1,0:T(8,128)(2,1)S(1)} %get-tuple-element.27.m0_ref), channel_id=1, source_target_pairs={{0,8},{4,12},{8,0},{12,4},{16,24},{20,28},{24,16},{28,20},{1,9},{5... | collective-permute-start | bytes 116744 | tf_op jit(solution)/shard_map/ppermute | solution.py:680
  27.0 0.0 collective-permute-done.9.kv2_ref
  27.0 0.0 collective-permute-start.8
  27.0 1.8 %collective-permute-done.4.m1_ref = bf16[152,128]{1,0:T(8,128)(2,1)S(1)} collective-permute-done((bf16[152,128]{1,0:T(8,128)(2,1)S(1)}, bf16[152,128]{1,0:T(8,128)(2,1)S(1)}, u32[]{:S(2)}, u32[]{:S(2)}) %collective-permute-start.4) | collective-permute-done | bytes 38944 | tf_op jit(solution)/shard_map/ppermute | solution.py:680
  28.8 0.0 collective-permute-start.10
  28.8 0.8 %collective-permute-done.5.m2_ref = bf16[152,128]{1,0:T(8,128)(2,1)S(1)} collective-permute-done((bf16[152,128]{1,0:T(8,128)(2,1)S(1)}, bf16[152,128]{1,0:T(8,128)(2,1)S(1)}, u32[]{:S(2)}, u32[]{:S(2)}) %collective-permute-start.5) | collective-permute-done | bytes 38944 | tf_op jit(solution)/shard_map/ppermute | solution.py:680
  29.6 0.0 collective-permute-done.6.m3_ref
  29.6 0.0 collective-permute-done.7.pair_ref
  29.6 1.9 %shard_map.192 = bf16[32,3,4,128]{3,2,1,0:T(4,128)(2,1)} custom-call(bf16[152,128]{1,0:T(8,128)(2,1)S(1)} %get-tuple-element.27.m0_ref, bf16[152,128]{1,0:T(8,128)(2,1)S(1)} %collective-permute-done.4.m1_ref, bf16[152,128]{1,0:T(8,128)(2,1)S(1)} %collective-permute-done.5.m2_ref, bf16[152,128]{1,0:T(8,128)(2,1)S(1)} %collective-permute-done.6.m3_ref, ...), custom_call_target="tpu_custom_call" | custom-call | flops 3000000000 | bytes 794624 | tf_op jit(solution)/shard_map/pallas_call | solution.py:609
  31.5 2.9 %all-to-all-start.1 = ((bf16[32,3,4,128]{3,2,1,0:T(4,128)(2,1)}), bf16[32,3,4,128]{3,2,1,0:T(4,128)(2,1)S(1)}, u32[]{:S(2)}, u32[]{:S(2)}) async-start(bf16[32,3,4,128]{3,2,1,0:T(4,128)(2,1)} %shard_map.192), calls=%async_computation.1 | async-start | bytes 196608 | tf_op jit(solution)/shard_map/all_to_all | solution.py:776
  34.4 0.0 collective-permute-done.8.kv1_ref
  34.4 0.0 collective-permute-done.10.kv3_ref
  34.4 1.9 %shard_map.193 = bf16[128,1024]{1,0:T(8,128)(2,1)} custom-call(bf16[128,1024]{1,0:T(8,128)(2,1)S(1)} %get-tuple-element.31.query_ref, f32[128,128]{1,0:T(8,128)S(1)} %get-tuple-element.23.side_ref, bf16[128,1024]{1,0:T(8,128)(2,1)S(1)} %copy-done.9, bf16[128,1024]{1,0:T(8,128)(2,1)S(1)} %collective-permute-done.8.kv1_ref, ...), custom_call_target="tpu_custom_call" | custom-call | flops 1000000000 | bytes 1376256 | tf_op jit(solution)/shard_map/pallas_call | solution.py:609
  36.3 5.9 %all-to-all-done.1.back_ref = bf16[32,3,4,128]{3,2,1,0:T(4,128)(2,1)S(1)} async-done(((bf16[32,3,4,128]{3,2,1,0:T(4,128)(2,1)}), bf16[32,3,4,128]{3,2,1,0:T(4,128)(2,1)S(1)}, u32[]{:S(2)}, u32[]{:S(2)}) %all-to-all-start.1) | async-done | bytes 98336 | tf_op jit(solution)/shard_map/all_to_all | solution.py:776
  42.2 0.7 %shard_map.194 = bf16[3,2048]{1,0:T(4,128)(2,1)} custom-call(bf16[32,3,4,128]{3,2,1,0:T(4,128)(2,1)S(1)} %all-to-all-done.1.back_ref), custom_call_target="tpu_custom_call" | custom-call | flops 1000000 | bytes 98304 | tf_op jit(solution)/shard_map/pallas_call | solution.py:609
  (11 shorter events, 0.0 us)
Async XLA Ops:
  0.6 11.9 %copy-start = (bf16[256,2048]{1,0:T(8,128)(2,1)S(1)}, bf16[256,2048]{1,0:T(8,128)(2,1)}, u32[]{:S(2)}) copy-start(bf16[256,2048]{1,0:T(8,128)(2,1)} %w_hbm.3) | copy-start | bytes 3145732
  3.6 9.0 %copy-start.3 = (bf16[768,256]{1,0:T(8,128)(2,1)S(1)}, bf16[768,256]{1,0:T(8,128)(2,1)}, u32[]{:S(2)}) copy-start(bf16[768,256]{1,0:T(8,128)(2,1)} %down_ref.1) | copy-start | bytes 1179652
  3.6 14.9 %collective-permute-start.3 = (bf16[256,768]{1,0:T(8,128)(2,1)}, bf16[256,768]{1,0:T(8,128)(2,1)S(1)}, u32[]{:S(2)}, u32[]{:S(2)}) collective-permute-start(bf16[256,768]{1,0:T(8,128)(2,1)} %get-tuple-element.25), channel_id=1, source_target_pairs={{0,4},{4,0},{8,12},{12,8},{16,20},{20,16},{24,28},{28,24},{1,5},{5... | collective-permute-start | bytes 1179656 | tf_op jit(solution)/shard_map/ppermute | solution.py:677
  6.6 9.8 %collective-permute-start.1 = (bf16[256,512]{1,0:T(8,128)(2,1)}, bf16[256,512]{1,0:T(8,128)(2,1)S(1)}, u32[]{:S(2)}, u32[]{:S(2)}) collective-permute-start(bf16[256,512]{1,0:T(8,128)(2,1)} %get-tuple-element.21), channel_id=1, source_target_pairs={{0,2},{1,3},{2,0},{3,1},{4,6},{5,7},{6,4},{7,5},{8,10},{9,11},{10,... | collective-permute-start | bytes 786440 | tf_op jit(solution)/shard_map/ppermute | solution.py:674
  8.1 4.3 %copy-start.10 = (bf16[128,8]{0,1:T(8,128)(2,1)S(1)}, bf16[128,8]{0,1:T(8,128)(2,1)}, u32[]{:S(2)}) copy-start(bf16[128,8]{0,1:T(8,128)(2,1)} %param.19) | copy-start | bytes 6148
  8.1 13.8 %all-to-all-start = ((bf16[32,7,4,128]{3,2,1,0:T(4,128)(2,1)}), bf16[32,7,4,128]{3,2,1,0:T(4,128)(2,1)S(1)}, u32[]{:S(2)}, u32[]{:S(2)}) async-start(bf16[32,7,4,128]{3,2,1,0:T(4,128)(2,1)} %get-tuple-element.19), calls=%async_computation | async-start | bytes 458752 | tf_op jit(solution)/shard_map/all_to_all | solution.py:740
  12.1 7.9 %collective-permute-start = (bf16[256,512]{1,0:T(8,128)(2,1)}, bf16[256,512]{1,0:T(8,128)(2,1)S(1)}, u32[]{:S(2)}, u32[]{:S(2)}) collective-permute-start(bf16[256,512]{1,0:T(8,128)(2,1)} %get-tuple-element.21), channel_id=1, source_target_pairs={{0,1},{1,0},{2,3},{3,2},{4,5},{5,4},{6,7},{7,6},{8,9},{9,8},{10,11... | collective-permute-start | bytes 786440 | tf_op jit(solution)/shard_map/ppermute | solution.py:674
  12.5 1.1 %copy-start.1 = (bf16[256,768]{1,0:T(8,128)(2,1)S(1)}, bf16[256,768]{1,0:T(8,128)(2,1)}, u32[]{:S(2)}) copy-start(bf16[256,768]{1,0:T(8,128)(2,1)} %gate_hbm.3) | copy-start | bytes 1179652
  12.5 1.1 %copy-start.2 = (bf16[256,768]{1,0:T(8,128)(2,1)S(1)}, bf16[256,768]{1,0:T(8,128)(2,1)}, u32[]{:S(2)}) copy-start(bf16[256,768]{1,0:T(8,128)(2,1)} %up_hbm.3) | copy-start | bytes 1179652
  12.6 1.1 %copy-start.5 = (f32[2048]{0:T(1024)S(1)}, f32[2048]{0:T(1024)}, u32[]{:S(2)}) copy-start(f32[2048]{0:T(1024)} %param.31) | copy-start | bytes 24580
  13.7 1.0 %copy-start.4 = (bf16[128,1024]{1,0:T(8,128)(2,1)S(1)}, bf16[128,1024]{1,0:T(8,128)(2,1)}, u32[]{:S(2)}) copy-start(bf16[128,1024]{1,0:T(8,128)(2,1)} %q_ref.1) | copy-start | bytes 786436
  13.7 1.0 %copy-start.6 = (s32[1,3]{1,0:T(1,128)S(1)}, s32[1,3]{1,0:T(1,128)}, u32[]{:S(2)}) copy-start(s32[1,3]{1,0:T(1,128)} %len_ref.1) | copy-start | bytes 40
  13.7 1.0 %copy-start.7 = (f32[128]{0:T(128)S(1)}, f32[128]{0:T(128)}, u32[]{:S(2)}) copy-start(f32[128]{0:T(128)} %param.22) | copy-start | bytes 1540
  13.7 0.9 %copy-start.8 = (f32[1,128]{1,0:T(1,128)S(1)}, f32[1,128]{1,0:T(1,128)}, u32[]{:S(2)}) copy-start(f32[1,128]{1,0:T(1,128)} %constant.2.clone.freq_hbm.freq_ref) | copy-start | bytes 1540
  14.6 2.1 %copy-start.9 = (bf16[128,1024]{1,0:T(8,128)(2,1)S(1)}, bf16[128,1024]{1,0:T(8,128)(2,1)}, u32[]{:S(2)}) copy-start(bf16[128,1024]{1,0:T(8,128)(2,1)} %get-tuple-element.33.kv0_ref) | copy-start | bytes 786436
  16.4 3.6 %collective-permute-start.2 = (bf16[256,512]{1,0:T(8,128)(2,1)S(1)}, bf16[256,512]{1,0:T(8,128)(2,1)S(1)}, u32[]{:S(2)}, u32[]{:S(2)}) collective-permute-start(bf16[256,512]{1,0:T(8,128)(2,1)S(1)} %collective-permute-done.1.w2_ref), channel_id=1, source_target_pairs={{0,1},{1,0},{2,3},{3,2},{4,5},{5,4},{6,7},{7,6},{8,9},{9,8},{10,11... | collective-permute-start | bytes 786440 | tf_op jit(solution)/shard_map/ppermute | solution.py:674
  16.7 10.3 %collective-permute-start.9 = (bf16[128,1024]{1,0:T(8,128)(2,1)S(1)}, bf16[128,1024]{1,0:T(8,128)(2,1)S(1)}, u32[]{:S(2)}, u32[]{:S(2)}) collective-permute-start(bf16[128,1024]{1,0:T(8,128)(2,1)S(1)} %copy-done.9), channel_id=1, source_target_pairs={{0,2},{1,3},{2,0},{3,1},{4,6},{5,7},{6,4},{7,5},{8,10},{9,11},{10,... | collective-permute-start | bytes 786440 | tf_op jit(solution)/shard_map/ppermute | solution.py:674
  18.5 11.1 %collective-permute-start.7 = (bf16[384,256]{1,0:T(8,128)(2,1)}, bf16[384,256]{1,0:T(8,128)(2,1)}, u32[]{:S(2)}, u32[]{:S(2)}) collective-permute-start(bf16[384,256]{1,0:T(8,128)(2,1)} %get-tuple-element.30), channel_id=1, source_target_pairs={{0,4},{4,0},{8,12},{12,8},{16,20},{20,16},{24,28},{28,24},{1,5},{5... | collective-permute-start | bytes 589832 | tf_op jit(solution)/shard_map/ppermute | solution.py:677
  22.6 6.2 %collective-permute-start.4 = (bf16[152,128]{1,0:T(8,128)(2,1)S(1)}, bf16[152,128]{1,0:T(8,128)(2,1)S(1)}, u32[]{:S(2)}, u32[]{:S(2)}) collective-permute-start(bf16[152,128]{1,0:T(8,128)(2,1)S(1)} %get-tuple-element.27.m0_ref), channel_id=1, source_target_pairs={{0,24},{4,28},{8,16},{12,20},{16,8},{20,12},{24,0},{28,4},{1,25},{... | collective-permute-start | bytes 116744 | tf_op jit(solution)/shard_map/ppermute | solution.py:680
  24.1 5.4 %collective-permute-start.5 = (bf16[152,128]{1,0:T(8,128)(2,1)S(1)}, bf16[152,128]{1,0:T(8,128)(2,1)S(1)}, u32[]{:S(2)}, u32[]{:S(2)}) collective-permute-start(bf16[152,128]{1,0:T(8,128)(2,1)S(1)} %get-tuple-element.27.m0_ref), channel_id=1, source_target_pairs={{0,16},{4,20},{8,24},{12,28},{16,0},{20,4},{24,8},{28,12},{1,17},{... | collective-permute-start | bytes 116744 | tf_op jit(solution)/shard_map/ppermute | solution.py:680
  25.1 4.5 %collective-permute-start.6 = (bf16[152,128]{1,0:T(8,128)(2,1)S(1)}, bf16[152,128]{1,0:T(8,128)(2,1)S(1)}, u32[]{:S(2)}, u32[]{:S(2)}) collective-permute-start(bf16[152,128]{1,0:T(8,128)(2,1)S(1)} %get-tuple-element.27.m0_ref), channel_id=1, source_target_pairs={{0,8},{4,12},{8,0},{12,4},{16,24},{20,28},{24,16},{28,20},{1,9},{5... | collective-permute-start | bytes 116744 | tf_op jit(solution)/shard_map/ppermute | solution.py:680
  27.0 7.3 %collective-permute-start.8 = (bf16[128,1024]{1,0:T(8,128)(2,1)S(1)}, bf16[128,1024]{1,0:T(8,128)(2,1)S(1)}, u32[]{:S(2)}, u32[]{:S(2)}) collective-permute-start(bf16[128,1024]{1,0:T(8,128)(2,1)S(1)} %copy-done.9), channel_id=1, source_target_pairs={{0,1},{1,0},{2,3},{3,2},{4,5},{5,4},{6,7},{7,6},{8,9},{9,8},{10,11... | collective-permute-start | bytes 786440 | tf_op jit(solution)/shard_map/ppermute | solution.py:674
  28.8 5.6 %collective-permute-start.10 = (bf16[128,1024]{1,0:T(8,128)(2,1)S(1)}, bf16[128,1024]{1,0:T(8,128)(2,1)S(1)}, u32[]{:S(2)}, u32[]{:S(2)}) collective-permute-start(bf16[128,1024]{1,0:T(8,128)(2,1)S(1)} %collective-permute-done.9.kv2_ref), channel_id=1, source_target_pairs={{0,1},{1,0},{2,3},{3,2},{4,5},{5,4},{6,7},{7,6},{8,9},{9,8},{10,11... | collective-permute-start | bytes 786440 | tf_op jit(solution)/shard_map/ppermute | solution.py:674
  31.5 10.7 %all-to-all-start.1 = ((bf16[32,3,4,128]{3,2,1,0:T(4,128)(2,1)}), bf16[32,3,4,128]{3,2,1,0:T(4,128)(2,1)S(1)}, u32[]{:S(2)}, u32[]{:S(2)}) async-start(bf16[32,3,4,128]{3,2,1,0:T(4,128)(2,1)} %shard_map.192), calls=%async_computation.1 | async-start | bytes 196608 | tf_op jit(solution)/shard_map/all_to_all | solution.py:776

commit v10 on v8

--- a/solution.py
+++ b/solution.py
@@ -295,14 +295,17 @@
     freq = freq_ref[...]
     tok_index = tp * tok + iota((tok, lanes), 0)
     factors = rope_factors((tok_index - begin_of(tok_index, len_ref)).astype(f32) * freq)
-    for copy in copies[2:11]:
+    for copy in copies[2:4]:
         copy.wait()
-    qg, kg = qg_ref[...], kg_ref[...]
+    kg = kg_ref[...]
     keys = []
     for k in range(kvs):
         at = slice(k * lanes, (k + 1) * lanes)
         keys.append(norm_rope(k_ref[:, at].astype(f32), kg, factors))
         kv_ref[:, at] = keys[-1]
+    for copy in copies[4:11]:
+        copy.wait()
+    qg = qg_ref[...]
     kv_ref[:, kvs * lanes :] = v_ref[...]
     for copy in copies[11:]:
         copy.wait()

time: 42.2 us -> 42.2 us (level)
  no operation moved by 1% of the time
where the time goes in v10:
time: 42.2 us; the launch traced here: 41.8 us
  starting transfers between devices  20.4 us (48%)
  waiting for transfers between devices  10.7 us (25%)
  Pallas kernels  8.81 us (21%)
  local copies, waits for them, and re-layouts  1.14 us (3%)
  between operations  0.8 us (2%)
    pallas_call x7, Pallas kernels, call(): pl.pallas_call(body, out_shape=out_shape, in_specs=specs, out_specs=jax.t...  8.8 us
    ppermute x2, starting transfers between devices, swap(): return lax.ppermute(array, 'req', [(i, i ^ 1) for i in range(reqs)])  5.44 us
    ppermute x3, starting transfers between devices, along(): return lax.ppermute(array, 'req', [(i, i ^ 2 * by) for i in range(reqs)])  4.45 us
    all_to_all x1, starting transfers between devices, local(): got = lax.all_to_all(pay, ('req', 'tp'), 0, 0, tiled=True)  3.97 us
    all_to_all x1, waiting for transfers between devices, local(): returned = lax.all_to_all(back, ('req', 'tp'), 0, 0, tiled=True)  3.78 us
    ppermute x6, starting transfers between devices, cross(): return lax.ppermute(array, 'tp', [(i, i ^ by) for i in range(tps)])  3.61 us
    all_to_all x1, starting transfers between devices, local(): returned = lax.all_to_all(back, ('req', 'tp'), 0, 0, tiled=True)  2.9 us
    all_to_all x1, waiting for transfers between devices, local(): got = lax.all_to_all(pay, ('req', 'tp'), 0, 0, tiled=True)  2.75 us
  transfers between devices with their start and end apart: 13, of which 6 were waited for; matrix products, arithmetic and copies ran while one was open for 0% of the time, Pallas kernels for 13%

profile of v10, /device:TPU:0, one launch (start us, length us, event | category | flops | bytes accessed | tf_op | source)
XLA Modules:
  0.0 41.8 jit_solution(196151000850230172)
XLA Ops:
  0.6 0.0 copy-start
  0.6 2.9 %shard_map.185 = (bf16[128,1024]{1,0:T(8,128)(2,1)}, bf16[32,7,4,128]{3,2,1,0:T(4,128)(2,1)}, bf16[256,512]{1,0:T(8,128)(2,1)}, bf16[256,768]{1,0:T(8,128)(2,1)}) custom-call(s32[1,3]{1,0:T(1,128)} %len_ref.1, bf16[128,512]{1,0:T(8,128)(2,1)} %k_hbm.1, bf16[128,512]{1,0:T(8,128)(2,1)} %v_hbm.1, bf16[3,1024]{1,0:T(4,128)(2,1)} %qn_hbm.1, ...), custom_call_target="tpu_custom_call" | custom-call | flops 10000000 | bytes 2123324 | tf_op jit(solution)/shard_map/pallas_call | solution.py:595
  3.5 0.0 copy-start.3
  3.5 3.0 %collective-permute-start.3 = (bf16[256,768]{1,0:T(8,128)(2,1)}, bf16[256,768]{1,0:T(8,128)(2,1)S(1)}, u32[]{:S(2)}, u32[]{:S(2)}) collective-permute-start(bf16[256,768]{1,0:T(8,128)(2,1)} %get-tuple-element.22), channel_id=1, source_target_pairs={{0,4},{4,0},{8,12},{12,8},{16,20},{20,16},{24,28},{28,24},{1,5},{5... | collective-permute-start | bytes 1179656 | tf_op jit(solution)/shard_map/ppermute | solution.py:663
  6.6 1.5 %collective-permute-start.1 = (bf16[256,512]{1,0:T(8,128)(2,1)}, bf16[256,512]{1,0:T(8,128)(2,1)S(1)}, u32[]{:S(2)}, u32[]{:S(2)}) collective-permute-start(bf16[256,512]{1,0:T(8,128)(2,1)} %get-tuple-element.19), channel_id=1, source_target_pairs={{0,2},{1,3},{2,0},{3,1},{4,6},{5,7},{6,4},{7,5},{8,10},{9,11},{10,... | collective-permute-start | bytes 786440 | tf_op jit(solution)/shard_map/ppermute | solution.py:660
  8.0 4.0 %all-to-all-start = ((bf16[32,7,4,128]{3,2,1,0:T(4,128)(2,1)}), bf16[32,7,4,128]{3,2,1,0:T(4,128)(2,1)S(1)}, u32[]{:S(2)}, u32[]{:S(2)}) async-start(bf16[32,7,4,128]{3,2,1,0:T(4,128)(2,1)} %get-tuple-element.17), calls=%async_computation | async-start | bytes 458752 | tf_op jit(solution)/shard_map/all_to_all | solution.py:719
  12.0 0.0 copy-start.1
  12.0 0.0 copy-start.2
  12.0 0.0 copy-start.4
  12.1 0.3 collective-permute-start
  12.4 0.3 shard_map.186
  12.7 0.3 copy-done.1
  13.0 0.1 copy-done.2
  13.1 0.0 copy-done.4
  13.1 0.1 shard_map.187
  13.2 1.3 %collective-permute-done.1.w2_ref = bf16[256,512]{1,0:T(8,128)(2,1)S(1)} collective-permute-done((bf16[256,512]{1,0:T(8,128)(2,1)}, bf16[256,512]{1,0:T(8,128)(2,1)S(1)}, u32[]{:S(2)}, u32[]{:S(2)}) %collective-permute-start.1) | collective-permute-done | bytes 262176 | tf_op jit(solution)/shard_map/ppermute | solution.py:660
  14.5 0.0 collective-permute-start.2
  14.5 1.8 %collective-permute-start.9 = (bf16[128,1024]{1,0:T(8,128)(2,1)S(1)}, bf16[128,1024]{1,0:T(8,128)(2,1)S(1)}, u32[]{:S(2)}, u32[]{:S(2)}) collective-permute-start(bf16[128,1024]{1,0:T(8,128)(2,1)S(1)} %copy-done.9), channel_id=1, source_target_pairs={{0,2},{1,3},{2,0},{3,1},{4,6},{5,7},{6,4},{7,5},{8,10},{9,11},{10,... | collective-permute-start | bytes 786440 | tf_op jit(solution)/shard_map/ppermute | solution.py:660
  16.3 0.3 collective-permute-done.3.refs_0_.pair_ref
  16.7 2.4 %collective-permute-start.7 = (bf16[384,256]{1,0:T(8,128)(2,1)S(1)}, bf16[384,256]{1,0:T(8,128)(2,1)S(1)}, u32[]{:S(2)}, u32[]{:S(2)}) collective-permute-start(bf16[384,256]{1,0:T(8,128)(2,1)S(1)} %get-tuple-element.27), channel_id=1, source_target_pairs={{0,4},{4,0},{8,12},{12,8},{16,20},{20,16},{24,28},{28,24},{1,5},{5... | collective-permute-start | bytes 589832 | tf_op jit(solution)/shard_map/ppermute | solution.py:663
  19.1 0.0 collective-permute-done.refs_1_.w1_ref
  19.1 0.0 collective-permute-done.2.refs_2_.w3_ref
  19.1 2.8 %all-to-all-done.pay_ref = bf16[32,7,4,128]{3,2,1,0:T(4,128)(2,1)S(1)} async-done(((bf16[32,7,4,128]{3,2,1,0:T(4,128)(2,1)}), bf16[32,7,4,128]{3,2,1,0:T(4,128)(2,1)S(1)}, u32[]{:S(2)}, u32[]{:S(2)}) %all-to-all-start) | async-done | bytes 229408 | tf_op jit(solution)/shard_map/all_to_all | solution.py:719
  21.8 0.7 %shard_map.190 = (f32[24,512]{1,0:T(8,128)S(1)}, bf16[152,128]{1,0:T(8,128)(2,1)S(1)}) custom-call(bf16[32,7,4,128]{3,2,1,0:T(4,128)(2,1)S(1)} %all-to-all-done.pay_ref, bf16[256,512]{1,0:T(8,128)(2,1)S(1)} %get-tuple-element.18.w0_ref, bf16[256,512]{1,0:T(8,128)(2,1)S(1)} %collective-permute-done.refs_1_.w1_ref, ...), custom_call_target="tpu_custom_call" | custom-call | flops 10000000 | bytes 2070528 | tf_op jit(solution)/shard_map/pallas_call | solution.py:595
  22.5 1.6 %collective-permute-start.4 = (bf16[152,128]{1,0:T(8,128)(2,1)S(1)}, bf16[152,128]{1,0:T(8,128)(2,1)S(1)}, u32[]{:S(2)}, u32[]{:S(2)}) collective-permute-start(bf16[152,128]{1,0:T(8,128)(2,1)S(1)} %get-tuple-element.24.m0_ref), channel_id=1, source_target_pairs={{0,24},{4,28},{8,16},{12,20},{16,8},{20,12},{24,0},{28,4},{1,25},{... | collective-permute-start | bytes 116744 | tf_op jit(solution)/shard_map/ppermute | solution.py:666
  24.1 0.9 %collective-permute-start.5 = (bf16[152,128]{1,0:T(8,128)(2,1)S(1)}, bf16[152,128]{1,0:T(8,128)(2,1)S(1)}, u32[]{:S(2)}, u32[]{:S(2)}) collective-permute-start(bf16[152,128]{1,0:T(8,128)(2,1)S(1)} %get-tuple-element.24.m0_ref), channel_id=1, source_target_pairs={{0,16},{4,20},{8,24},{12,28},{16,0},{20,4},{24,8},{28,12},{1,17},{... | collective-permute-start | bytes 116744 | tf_op jit(solution)/shard_map/ppermute | solution.py:666
  25.1 1.9 %collective-permute-start.6 = (bf16[152,128]{1,0:T(8,128)(2,1)S(1)}, bf16[152,128]{1,0:T(8,128)(2,1)S(1)}, u32[]{:S(2)}, u32[]{:S(2)}) collective-permute-start(bf16[152,128]{1,0:T(8,128)(2,1)S(1)} %get-tuple-element.24.m0_ref), channel_id=1, source_target_pairs={{0,8},{4,12},{8,0},{12,4},{16,24},{20,28},{24,16},{28,20},{1,9},{5... | collective-permute-start | bytes 116744 | tf_op jit(solution)/shard_map/ppermute | solution.py:666
  27.0 0.0 collective-permute-done.9.kv2_ref
  27.0 0.0 collective-permute-start.8
  27.0 1.8 %collective-permute-done.4.m1_ref = bf16[152,128]{1,0:T(8,128)(2,1)S(1)} collective-permute-done((bf16[152,128]{1,0:T(8,128)(2,1)S(1)}, bf16[152,128]{1,0:T(8,128)(2,1)S(1)}, u32[]{:S(2)}, u32[]{:S(2)}) %collective-permute-start.4) | collective-permute-done | bytes 38944 | tf_op jit(solution)/shard_map/ppermute | solution.py:666
  28.7 0.0 collective-permute-start.10
  28.7 0.8 %collective-permute-done.5.m2_ref = bf16[152,128]{1,0:T(8,128)(2,1)S(1)} collective-permute-done((bf16[152,128]{1,0:T(8,128)(2,1)S(1)}, bf16[152,128]{1,0:T(8,128)(2,1)S(1)}, u32[]{:S(2)}, u32[]{:S(2)}) %collective-permute-start.5) | collective-permute-done | bytes 38944 | tf_op jit(solution)/shard_map/ppermute | solution.py:666
  29.5 0.0 collective-permute-done.6.m3_ref
  29.5 0.0 collective-permute-done.7.pair_ref
  29.5 0.9 %shard_map.191 = bf16[32,3,4,128]{3,2,1,0:T(4,128)(2,1)} custom-call(bf16[152,128]{1,0:T(8,128)(2,1)S(1)} %get-tuple-element.24.m0_ref, bf16[152,128]{1,0:T(8,128)(2,1)S(1)} %collective-permute-done.4.m1_ref, bf16[152,128]{1,0:T(8,128)(2,1)S(1)} %collective-permute-done.5.m2_ref, bf16[152,128]{1,0:T(8,128)(2,1)S(1)} %collective-permute-done.6.m3_ref, ...), custom_call_target="tpu_custom_call" | custom-call | flops 3000000000 | bytes 794624 | tf_op jit(solution)/shard_map/pallas_call | solution.py:595
  30.5 2.9 %all-to-all-start.1 = ((bf16[32,3,4,128]{3,2,1,0:T(4,128)(2,1)}), bf16[32,3,4,128]{3,2,1,0:T(4,128)(2,1)S(1)}, u32[]{:S(2)}, u32[]{:S(2)}) async-start(bf16[32,3,4,128]{3,2,1,0:T(4,128)(2,1)} %shard_map.191), calls=%async_computation.1 | async-start | bytes 196608 | tf_op jit(solution)/shard_map/all_to_all | solution.py:756
  33.4 0.0 copy-start.5
  33.4 0.0 copy-start.6
  33.4 0.0 copy-start.7
  33.4 0.1 copy.20.g_ref
  33.5 0.0 collective-permute-done.8.kv1_ref
  33.6 0.0 collective-permute-done.10.kv3_ref
  33.6 0.5 %copy-done.5 = s32[1,3]{1,0:T(1,128)S(1)} copy-done((s32[1,3]{1,0:T(1,128)S(1)}, s32[1,3]{1,0:T(1,128)}, u32[]{:S(2)}) %copy-start.5) | copy-done | bytes 36
  34.0 0.0 copy-done.6
  34.1 0.0 copy-done.7
  34.1 3.3 %shard_map.192 = bf16[128,1024]{1,0:T(8,128)(2,1)} custom-call(s32[1,3]{1,0:T(1,128)S(1)} %copy-done.5, bf16[128,1024]{1,0:T(8,128)(2,1)S(1)} %copy-done.8, bf16[128,8]{1,0:T(8,128)(2,1)S(1)} %copy.20.g_ref, bf16[128,1024]{1,0:T(8,128)(2,1)S(1)} %copy-done.9, bf16[128,1024]{1,0:T(8,128)(2,1)S(1)} %collective-permute-done.8.kv1_ref, ...), custom_call_target="tpu_custom_call" | custom-call | flops 1000000000 | bytes 1313804 | tf_op jit(solution)/shard_map/pallas_call | solution.py:595
  37.4 3.8 %all-to-all-done.1.back_ref = bf16[32,3,4,128]{3,2,1,0:T(4,128)(2,1)S(1)} async-done(((bf16[32,3,4,128]{3,2,1,0:T(4,128)(2,1)}), bf16[32,3,4,128]{3,2,1,0:T(4,128)(2,1)S(1)}, u32[]{:S(2)}, u32[]{:S(2)}) %all-to-all-start.1) | async-done | bytes 98336 | tf_op jit(solution)/shard_map/all_to_all | solution.py:756
  41.2 0.7 %shard_map.193 = bf16[3,2048]{1,0:T(4,128)(2,1)} custom-call(bf16[32,3,4,128]{3,2,1,0:T(4,128)(2,1)S(1)} %all-to-all-done.1.back_ref), custom_call_target="tpu_custom_call" | custom-call | flops 1000000 | bytes 98304 | tf_op jit(solution)/shard_map/pallas_call | solution.py:595
  (10 shorter events, 0.0 us)
Async XLA Ops:
  0.6 11.7 %copy-start = (bf16[256,2048]{1,0:T(8,128)(2,1)S(1)}, bf16[256,2048]{1,0:T(8,128)(2,1)}, u32[]{:S(2)}) copy-start(bf16[256,2048]{1,0:T(8,128)(2,1)} %w_hbm.3) | copy-start | bytes 3145732
  3.5 8.9 %copy-start.3 = (bf16[768,256]{1,0:T(8,128)(2,1)S(1)}, bf16[768,256]{1,0:T(8,128)(2,1)}, u32[]{:S(2)}) copy-start(bf16[768,256]{1,0:T(8,128)(2,1)} %down_ref.1) | copy-start | bytes 1179652
  3.5 13.1 %collective-permute-start.3 = (bf16[256,768]{1,0:T(8,128)(2,1)}, bf16[256,768]{1,0:T(8,128)(2,1)S(1)}, u32[]{:S(2)}, u32[]{:S(2)}) collective-permute-start(bf16[256,768]{1,0:T(8,128)(2,1)} %get-tuple-element.22), channel_id=1, source_target_pairs={{0,4},{4,0},{8,12},{12,8},{16,20},{20,16},{24,28},{28,24},{1,5},{5... | collective-permute-start | bytes 1179656 | tf_op jit(solution)/shard_map/ppermute | solution.py:663
  6.6 8.0 %collective-permute-start.1 = (bf16[256,512]{1,0:T(8,128)(2,1)}, bf16[256,512]{1,0:T(8,128)(2,1)S(1)}, u32[]{:S(2)}, u32[]{:S(2)}) collective-permute-start(bf16[256,512]{1,0:T(8,128)(2,1)} %get-tuple-element.19), channel_id=1, source_target_pairs={{0,2},{1,3},{2,0},{3,1},{4,6},{5,7},{6,4},{7,5},{8,10},{9,11},{10,... | collective-permute-start | bytes 786440 | tf_op jit(solution)/shard_map/ppermute | solution.py:660
  8.0 13.8 %all-to-all-start = ((bf16[32,7,4,128]{3,2,1,0:T(4,128)(2,1)}), bf16[32,7,4,128]{3,2,1,0:T(4,128)(2,1)S(1)}, u32[]{:S(2)}, u32[]{:S(2)}) async-start(bf16[32,7,4,128]{3,2,1,0:T(4,128)(2,1)} %get-tuple-element.17), calls=%async_computation | async-start | bytes 458752 | tf_op jit(solution)/shard_map/all_to_all | solution.py:719
  12.0 1.0 %copy-start.1 = (bf16[256,768]{1,0:T(8,128)(2,1)S(1)}, bf16[256,768]{1,0:T(8,128)(2,1)}, u32[]{:S(2)}) copy-start(bf16[256,768]{1,0:T(8,128)(2,1)} %gate_hbm.3) | copy-start | bytes 1179652
  12.0 1.1 %copy-start.2 = (bf16[256,768]{1,0:T(8,128)(2,1)S(1)}, bf16[256,768]{1,0:T(8,128)(2,1)}, u32[]{:S(2)}) copy-start(bf16[256,768]{1,0:T(8,128)(2,1)} %up_hbm.3) | copy-start | bytes 1179652
  12.0 1.1 %copy-start.4 = (f32[2048]{0:T(1024)S(1)}, f32[2048]{0:T(1024)}, u32[]{:S(2)}) copy-start(f32[2048]{0:T(1024)} %param.31) | copy-start | bytes 24580
  12.1 7.0 %collective-permute-start = (bf16[256,512]{1,0:T(8,128)(2,1)}, bf16[256,512]{1,0:T(8,128)(2,1)S(1)}, u32[]{:S(2)}, u32[]{:S(2)}) collective-permute-start(bf16[256,512]{1,0:T(8,128)(2,1)} %get-tuple-element.19), channel_id=1, source_target_pairs={{0,1},{1,0},{2,3},{3,2},{4,5},{5,4},{6,7},{7,6},{8,9},{9,8},{10,11... | collective-permute-start | bytes 786440 | tf_op jit(solution)/shard_map/ppermute | solution.py:660
  13.1 1.4 %copy-start.9 = (bf16[128,1024]{1,0:T(8,128)(2,1)S(1)}, bf16[128,1024]{1,0:T(8,128)(2,1)}, u32[]{:S(2)}) copy-start(bf16[128,1024]{1,0:T(8,128)(2,1)} %get-tuple-element.29.kv0_ref) | copy-start | bytes 786436
  14.5 4.5 %collective-permute-start.2 = (bf16[256,512]{1,0:T(8,128)(2,1)S(1)}, bf16[256,512]{1,0:T(8,128)(2,1)S(1)}, u32[]{:S(2)}, u32[]{:S(2)}) collective-permute-start(bf16[256,512]{1,0:T(8,128)(2,1)S(1)} %collective-permute-done.1.w2_ref), channel_id=1, source_target_pairs={{0,1},{1,0},{2,3},{3,2},{4,5},{5,4},{6,7},{7,6},{8,9},{9,8},{10,11... | collective-permute-start | bytes 786440 | tf_op jit(solution)/shard_map/ppermute | solution.py:660
  14.5 12.4 %collective-permute-start.9 = (bf16[128,1024]{1,0:T(8,128)(2,1)S(1)}, bf16[128,1024]{1,0:T(8,128)(2,1)S(1)}, u32[]{:S(2)}, u32[]{:S(2)}) collective-permute-start(bf16[128,1024]{1,0:T(8,128)(2,1)S(1)} %copy-done.9), channel_id=1, source_target_pairs={{0,2},{1,3},{2,0},{3,1},{4,6},{5,7},{6,4},{7,5},{8,10},{9,11},{10,... | collective-permute-start | bytes 786440 | tf_op jit(solution)/shard_map/ppermute | solution.py:660
  16.7 12.9 %collective-permute-start.7 = (bf16[384,256]{1,0:T(8,128)(2,1)S(1)}, bf16[384,256]{1,0:T(8,128)(2,1)S(1)}, u32[]{:S(2)}, u32[]{:S(2)}) collective-permute-start(bf16[384,256]{1,0:T(8,128)(2,1)S(1)} %get-tuple-element.27), channel_id=1, source_target_pairs={{0,4},{4,0},{8,12},{12,8},{16,20},{20,16},{24,28},{28,24},{1,5},{5... | collective-permute-start | bytes 589832 | tf_op jit(solution)/shard_map/ppermute | solution.py:663
  22.5 6.2 %collective-permute-start.4 = (bf16[152,128]{1,0:T(8,128)(2,1)S(1)}, bf16[152,128]{1,0:T(8,128)(2,1)S(1)}, u32[]{:S(2)}, u32[]{:S(2)}) collective-permute-start(bf16[152,128]{1,0:T(8,128)(2,1)S(1)} %get-tuple-element.24.m0_ref), channel_id=1, source_target_pairs={{0,24},{4,28},{8,16},{12,20},{16,8},{20,12},{24,0},{28,4},{1,25},{... | collective-permute-start | bytes 116744 | tf_op jit(solution)/shard_map/ppermute | solution.py:666
  24.1 5.4 %collective-permute-start.5 = (bf16[152,128]{1,0:T(8,128)(2,1)S(1)}, bf16[152,128]{1,0:T(8,128)(2,1)S(1)}, u32[]{:S(2)}, u32[]{:S(2)}) collective-permute-start(bf16[152,128]{1,0:T(8,128)(2,1)S(1)} %get-tuple-element.24.m0_ref), channel_id=1, source_target_pairs={{0,16},{4,20},{8,24},{12,28},{16,0},{20,4},{24,8},{28,12},{1,17},{... | collective-permute-start | bytes 116744 | tf_op jit(solution)/shard_map/ppermute | solution.py:666
  25.1 4.5 %collective-permute-start.6 = (bf16[152,128]{1,0:T(8,128)(2,1)S(1)}, bf16[152,128]{1,0:T(8,128)(2,1)S(1)}, u32[]{:S(2)}, u32[]{:S(2)}) collective-permute-start(bf16[152,128]{1,0:T(8,128)(2,1)S(1)} %get-tuple-element.24.m0_ref), channel_id=1, source_target_pairs={{0,8},{4,12},{8,0},{12,4},{16,24},{20,28},{24,16},{28,20},{1,9},{5... | collective-permute-start | bytes 116744 | tf_op jit(solution)/shard_map/ppermute | solution.py:666
  27.0 6.6 %collective-permute-start.8 = (bf16[128,1024]{1,0:T(8,128)(2,1)S(1)}, bf16[128,1024]{1,0:T(8,128)(2,1)S(1)}, u32[]{:S(2)}, u32[]{:S(2)}) collective-permute-start(bf16[128,1024]{1,0:T(8,128)(2,1)S(1)} %copy-done.9), channel_id=1, source_target_pairs={{0,1},{1,0},{2,3},{3,2},{4,5},{5,4},{6,7},{7,6},{8,9},{9,8},{10,11... | collective-permute-start | bytes 786440 | tf_op jit(solution)/shard_map/ppermute | solution.py:660
  28.7 4.8 %collective-permute-start.10 = (bf16[128,1024]{1,0:T(8,128)(2,1)S(1)}, bf16[128,1024]{1,0:T(8,128)(2,1)S(1)}, u32[]{:S(2)}, u32[]{:S(2)}) collective-permute-start(bf16[128,1024]{1,0:T(8,128)(2,1)S(1)} %collective-permute-done.9.kv2_ref), channel_id=1, source_target_pairs={{0,1},{1,0},{2,3},{3,2},{4,5},{5,4},{6,7},{7,6},{8,9},{9,8},{10,11... | collective-permute-start | bytes 786440 | tf_op jit(solution)/shard_map/ppermute | solution.py:660
  29.5 4.0 %copy-start.8 = (bf16[128,1024]{1,0:T(8,128)(2,1)S(1)}, bf16[128,1024]{1,0:T(8,128)(2,1)}, u32[]{:S(2)}) copy-start(bf16[128,1024]{1,0:T(8,128)(2,1)} %q_ref.1) | copy-start | bytes 786436
  30.5 2.9 %copy-start.10 = (bf16[128,8]{0,1:T(8,128)(2,1)S(1)}, bf16[128,8]{0,1:T(8,128)(2,1)}, u32[]{:S(2)}) copy-start(bf16[128,8]{0,1:T(8,128)(2,1)} %param.19) | copy-start | bytes 6148
  30.5 10.7 %all-to-all-start.1 = ((bf16[32,3,4,128]{3,2,1,0:T(4,128)(2,1)}), bf16[32,3,4,128]{3,2,1,0:T(4,128)(2,1)S(1)}, u32[]{:S(2)}, u32[]{:S(2)}) async-start(bf16[32,3,4,128]{3,2,1,0:T(4,128)(2,1)} %shard_map.191), calls=%async_computation.1 | async-start | bytes 196608 | tf_op jit(solution)/shard_map/all_to_all | solution.py:756
  33.4 0.7 %copy-start.5 = (s32[1,3]{1,0:T(1,128)S(1)}, s32[1,3]{1,0:T(1,128)}, u32[]{:S(2)}) copy-start(s32[1,3]{1,0:T(1,128)} %len_ref.1) | copy-start | bytes 40
  33.4 0.7 %copy-start.6 = (f32[128]{0:T(128)S(1)}, f32[128]{0:T(128)}, u32[]{:S(2)}) copy-start(f32[128]{0:T(128)} %param.22) | copy-start | bytes 1540
  33.4 0.7 %copy-start.7 = (f32[1,128]{1,0:T(1,128)S(1)}, f32[1,128]{1,0:T(1,128)}, u32[]{:S(2)}) copy-start(f32[1,128]{1,0:T(1,128)} %constant.2.clone.freq_hbm.freq_ref) | copy-start | bytes 1540
